TPU v7x, 128 devices: a whole 4x4x4 slice. The times are simulated.
128 devices in a mesh: expert: 16 (over y_hi, x, core), dp: 8 (over y_lo, z).
Axes of the slice: x: 4, y: 4 (y_hi: 2, y_lo: 2; y = y_hi * 2 + y_lo), z: 4, core: 2. Of those that a mesh axis runs over, the one named last changes fastest.
Arguments:
- tokens: bfloat16 [128, 256, 1280], P(('expert', 'dp')), may hold values from -64 to 64
- slot_params: bfloat16 [128, 1280], replicated, may hold values from -1 to 1
- expert_in: bfloat16 [64, 4608, 1280], P('expert', 'dp'), may hold values from -0.15625 to 0.15625
- expert_out: bfloat16 [64, 4608, 1280], P('expert', 'dp'), may hold values from -0.09375 to 0.09375
- grad_out: bfloat16 [128, 256, 1280], P(('expert', 'dp')), may hold values from -6 to 6
Outputs:
- grad_tokens: bfloat16 [128, 256, 1280], P(('expert', 'dp'))
- grad_params: float32 [128, 1280], replicated
- grad_w_in: bfloat16 [64, 4608, 1280], P('expert', 'dp')
- grad_w_out: bfloat16 [64, 4608, 1280], P('expert', 'dp')
All inputs are finite; a program needn't handle non-finite values.
Results may differ from a plain program's by a relative error of at most 0.009.
Values may be sent and summed in bfloat16 or wider, within the bound.
No kernel may reach another device: no remote copies, remote signals or barrier semaphores. Data moves between devices by JAX's collectives and lax.ppermute only.
A program may use at most 128 MiB of HBM per device.

v0:
```python
import math

import jax
import jax.numpy as jnp
from jax import lax
from jax.sharding import PartitionSpec as P

SLOTS = 2


inv_root_two = 1.0 / math.sqrt(2.0)
inv_root_tau = 1.0 / math.sqrt(2.0 * math.pi)


def gelu_value(values):
    return 0.5 * values * (1.0 + lax.erf(values * inv_root_two))


def gelu_slope(values):
    return (
        0.5 * (1.0 + lax.erf(values * inv_root_two))
        + values * jnp.exp(-0.5 * values * values) * inv_root_tau
    )


def to_experts(blocks):
    n_group = lax.axis_size("dp")
    resident, n_expert, row_block, feature = blocks.shape
    copies = jnp.broadcast_to(blocks[:, :, None], (resident, n_expert, n_group, row_block, feature))
    copies = copies.reshape(resident, n_expert * n_group * row_block, feature)
    return lax.all_to_all(copies, ("expert", "dp"), split_axis=1, concat_axis=1, tiled=True)


def from_experts(partial_value, n_expert):
    n_group = lax.axis_size("dp")
    resident, total_rows, feature = partial_value.shape
    row_block = total_rows // (n_expert * n_group)
    returned = lax.all_to_all(
        partial_value, ("expert", "dp"), split_axis=1, concat_axis=1, tiled=True
    )
    returned = returned.reshape(resident, n_expert, n_group, row_block, feature)
    return jnp.sum(returned, axis=2).astype(jnp.bfloat16)


def per_device(tokens, slot_params, expert_in, expert_out, grad_out):
    n_expert = lax.axis_size("expert")
    images, length, feature = tokens.shape
    resident = expert_in.shape[0]
    logits = jnp.einsum("sd,nmd->nsm", slot_params, tokens, preferred_element_type=jnp.float32)
    p_dispatch = jax.nn.softmax(logits, axis=2)
    p_combine = jax.nn.softmax(logits, axis=1)
    dispatch = p_dispatch.astype(jnp.bfloat16)
    combine = p_combine.astype(jnp.bfloat16)
    slot_in = jnp.einsum(
        "nsm,nmd->snd", dispatch, tokens, preferred_element_type=jnp.float32
    ).astype(jnp.bfloat16)
    blocks = slot_in.reshape(n_expert, resident, SLOTS * images, feature).transpose(1, 0, 2, 3)
    expert_rows = to_experts(blocks)
    hidden = jnp.einsum("ehd,erd->ehr", expert_in, expert_rows, preferred_element_type=jnp.float32)
    active = gelu_value(hidden).astype(jnp.bfloat16)
    partial_value = jnp.einsum(
        "ehr,ehd->erd", active, expert_out, preferred_element_type=jnp.float32
    )
    slot_out = (
        from_experts(partial_value, n_expert).transpose(1, 0, 2, 3).reshape(-1, images, feature)
    )
    d_combine = jnp.einsum("nmd,snd->nsm", grad_out, slot_out, preferred_element_type=jnp.float32)
    d_slot_out = jnp.einsum(
        "nsm,nmd->snd", combine, grad_out, preferred_element_type=jnp.float32
    ).astype(jnp.bfloat16)
    d_blocks = d_slot_out.reshape(n_expert, resident, SLOTS * images, feature).transpose(1, 0, 2, 3)
    d_rows = to_experts(d_blocks)
    d_active = jnp.einsum("ehd,erd->ehr", expert_out, d_rows, preferred_element_type=jnp.float32)
    grad_w_out = jnp.einsum(
        "ehr,erd->ehd", active, d_rows, preferred_element_type=jnp.float32
    ).astype(jnp.bfloat16)
    d_hidden = (d_active * gelu_slope(hidden)).astype(jnp.bfloat16)
    grad_w_in = jnp.einsum(
        "ehr,erd->ehd", d_hidden, expert_rows, preferred_element_type=jnp.float32
    ).astype(jnp.bfloat16)
    d_partial = jnp.einsum("ehr,ehd->erd", d_hidden, expert_in, preferred_element_type=jnp.float32)
    d_slot_in = from_experts(d_partial, n_expert).transpose(1, 0, 2, 3).reshape(-1, images, feature)
    d_dispatch = jnp.einsum("snd,nmd->nsm", d_slot_in, tokens, preferred_element_type=jnp.float32)
    d_logits = (
        p_dispatch * (d_dispatch - jnp.sum(p_dispatch * d_dispatch, axis=2, keepdims=True))
        + p_combine * (d_combine - jnp.sum(p_combine * d_combine, axis=1, keepdims=True))
    ).astype(jnp.bfloat16)
    grad_tokens = (
        jnp.einsum("nsm,snd->nmd", dispatch, d_slot_in, preferred_element_type=jnp.float32)
        + jnp.einsum("nsm,sd->nmd", d_logits, slot_params, preferred_element_type=jnp.float32)
    ).astype(jnp.bfloat16)
    local_params = jnp.einsum("nsm,nmd->sd", d_logits, tokens, preferred_element_type=jnp.float32)
    grad_params = lax.psum(local_params, ("expert", "dp"))
    return (grad_tokens, grad_params, grad_w_in, grad_w_out)


def solution(mesh):
    placed = (
        P(("expert", "dp"), None, None),
        P(),
        P("expert", "dp", None),
        P("expert", "dp", None),
        P(("expert", "dp"), None, None),
    )
    return jax.shard_map(
        per_device,
        mesh=mesh,
        in_specs=placed,
        out_specs=(
            P(("expert", "dp"), None, None),
            P(),
            P("expert", "dp", None),
            P("expert", "dp", None),
        ),
        check_vma=False,
    )
```

profile of v0, /device:TPU:1, one launch (start us, length us, event | category | flops | bytes accessed | tf_op | source)
XLA Modules:
  0.0 424.8 jit_solution(13775161743135687858)
XLA Ops:
  7.2 0.0 copy-start
  7.2 1.1 copy-done
  8.3 1.4 fusion.53
  9.6 0.2 fusion.39
  9.8 0.3 fusion.13
  10.1 0.1 reshape.110
  10.3 0.1 copy.23
  10.4 2.2 broadcast_in_dim.5
  12.6 11.5 %all-to-all-start.1 = ((bf16[4,256,1280]{2,0,1:T(4,128)(2,1)}), bf16[4,256,1280]{2,0,1:T(4,128)(2,1)S(1)}, u32[]{:S(2)}, u32[]{:S(2)}) async-start(bf16[4,256,1280]{2,0,1:T(4,128)(2,1)} %bitcast.171), calls=%async_computation.1 | async-start | bytes 5242880 | tf_op jit(solution)/shard_map/all_to_all | solution.py:31
  24.1 2.2 fusion.12
  26.3 1.8 reshape.108
  28.1 1.8 copy.21
  29.9 29.9 %all-to-all-done.1 = bf16[4,256,1280]{2,0,1:T(4,128)(2,1)S(1)} async-done(((bf16[4,256,1280]{2,0,1:T(4,128)(2,1)}), bf16[4,256,1280]{2,0,1:T(4,128)(2,1)S(1)}, u32[]{:S(2)}, u32[]{:S(2)}) %all-to-all-start.1) | async-done | bytes 2621472 | tf_op jit(solution)/shard_map/all_to_all | solution.py:31
  59.8 3.1 broadcast_in_dim.4
  63.0 5.6 %all-to-all-start = ((bf16[4,256,1280]{2,0,1:T(4,128)(2,1)}), bf16[4,256,1280]{2,0,1:T(4,128)(2,1)}, u32[]{:S(2)}, u32[]{:S(2)}) async-start(bf16[4,256,1280]{2,0,1:T(4,128)(2,1)} %bitcast.172), calls=%async_computation | async-start | bytes 5242880 | tf_op jit(solution)/shard_map/all_to_all | solution.py:31
  68.6 5.8 %fusion.15 = f32[4,256,576]{1,2,0:T(8,128)} fusion(bf16[4,576,1280]{2,1,0:T(8,128)(2,1)} %param.7, bf16[4,256,1280]{2,0,1:T(4,128)(2,1)S(1)} %all-to-all-done.1), kind=kOutput, calls=%fused_computation.23 | convolution fusion | flops 1509949440 | bytes 10878976 | tf_op jit(solution)/shard_map/ehd,erd->ehr/dot_general | solution.py:59
  74.4 29.8 %all-to-all-done = bf16[4,256,1280]{2,0,1:T(4,128)(2,1)} async-done(((bf16[4,256,1280]{2,0,1:T(4,128)(2,1)}), bf16[4,256,1280]{2,0,1:T(4,128)(2,1)}, u32[]{:S(2)}, u32[]{:S(2)}) %all-to-all-start) | async-done | bytes 2621472 | tf_op jit(solution)/shard_map/all_to_all | solution.py:31
  104.1 6.4 %fusion.7 = bf16[4,576,256]{2,1,0:T(8,128)(2,1)S(1)} fusion(f32[4,256,576]{1,2,0:T(8,128)} %fusion.15, bf16[4,576,1280]{2,1,0:T(8,128)(2,1)} %param.8, bf16[4,256,1280]{2,0,1:T(4,128)(2,1)} %all-to-all-done), kind=kOutput, calls=%fused_computation.13 | convolution fusion | flops 1515847680 | bytes 12058624 | tf_op jit(solution)/shard_map/ehd,erd->ehr/dot_general | solution.py:73
  110.5 0.0 copy-start.2
  110.5 1.0 copy-done.2
  111.6 4.9 %fusion.56 = f32[4,256,1280]{2,1,0:T(8,128)S(1)} fusion(bf16[4,576,256]{2,1,0:T(8,128)(2,1)S(1)} %fusion.7, bf16[4,576,1280]{2,1,0:T(8,128)(2,1)} %param.7), kind=kOutput, calls=%fused_computation.64 | convolution fusion | flops 1509949440 | bytes 12320768 | tf_op jit(solution)/shard_map/ehr,ehd->erd/dot_general | solution.py:81
  116.5 5.7 %copy.25 = f32[4,256,1280]{2,0,1:T(4,128)} copy(f32[4,256,1280]{2,1,0:T(8,128)S(1)} %fusion.56) | data formatting | bytes 10485760 | tf_op jit(solution)/shard_map/ehr,ehd->erd/dot_general | solution.py:81
  122.3 5.7 %all-to-all-start.2 = ((f32[4,256,1280]{2,0,1:T(4,128)}), f32[4,256,1280]{2,0,1:T(4,128)}, u32[]{:S(2)}, u32[]{:S(2)}) async-start(f32[4,256,1280]{2,0,1:T(4,128)} %copy.25), calls=%async_computation.2 | async-start | bytes 10485760 | tf_op jit(solution)/shard_map/all_to_all | solution.py:38
  127.9 5.7 %fusion.51 = f32[4,256,1280]{2,1,0:T(8,128)S(1)} fusion(bf16[4,576,1280]{2,1,0:T(8,128)(2,1)} %param.8, f32[4,256,576]{1,2,0:T(8,128)} %fusion.15), kind=kOutput, calls=%fused_computation.62 | convolution fusion | flops 1512898560 | bytes 13500416 | tf_op jit(solution)/shard_map/ehr,ehd->erd/dot_general | solution.py:61
  133.6 5.7 %copy.30 = f32[4,256,1280]{2,0,1:T(4,128)} copy(f32[4,256,1280]{2,1,0:T(8,128)S(1)} %fusion.51) | data formatting | bytes 10485760 | tf_op jit(solution)/shard_map/ehr,ehd->erd/dot_general | solution.py:61
  139.4 53.1 %all-to-all-done.2 = f32[4,256,1280]{2,0,1:T(4,128)} async-done(((f32[4,256,1280]{2,0,1:T(4,128)}), f32[4,256,1280]{2,0,1:T(4,128)}, u32[]{:S(2)}, u32[]{:S(2)}) %all-to-all-start.2) | async-done | bytes 5242912 | tf_op jit(solution)/shard_map/all_to_all | solution.py:38
  192.4 7.9 %all-to-all-start.3 = ((f32[4,256,1280]{2,0,1:T(4,128)}), f32[4,256,1280]{2,0,1:T(4,128)}, u32[]{:S(2)}, u32[]{:S(2)}) async-start(f32[4,256,1280]{2,0,1:T(4,128)} %copy.30), calls=%async_computation.3 | async-start | bytes 10485760 | tf_op jit(solution)/shard_map/all_to_all | solution.py:38
  200.3 0.3 all-reduce.2.cloned.1.call-start
  200.6 0.0 copy-start.1
  200.6 5.7 %convolution_convert_fusion.1 = bf16[4,576,1280]{2,1,0:T(8,128)(2,1)} fusion(bf16[4,576,256]{2,1,0:T(8,128)(2,1)} %copy-done.2, bf16[4,256,1280]{2,0,1:T(4,128)(2,1)S(1)} %all-to-all-done.1), kind=kOutput, calls=%fused_computation.1 | convolution fusion | flops 1512898560 | bytes 9699328 | tf_op jit(solution)/shard_map/ehr,erd->ehd/dot_general | solution.py:78
  206.3 5.3 %convolution_convert_fusion = bf16[4,576,1280]{2,1,0:T(8,128)(2,1)} fusion(bf16[4,256,1280]{2,0,1:T(4,128)(2,1)} %all-to-all-done, f32[4,256,576]{1,2,0:T(8,128)S(1)} %copy-done.1), kind=kOutput, calls=%fused_computation | convolution fusion | flops 1515847680 | bytes 10878976 | tf_op jit(solution)/shard_map/ehr,erd->ehd/dot_general | solution.py:74
  211.7 3.6 reduce_sum.56
  215.3 0.3 copy.56
  215.5 0.2 copy.27
  215.8 0.1 reshape.113
  215.9 48.8 %all-to-all-done.3 = f32[4,256,1280]{2,0,1:T(4,128)} async-done(((f32[4,256,1280]{2,0,1:T(4,128)}), f32[4,256,1280]{2,0,1:T(4,128)}, u32[]{:S(2)}, u32[]{:S(2)}) %all-to-all-start.3) | async-done | bytes 5242912 | tf_op jit(solution)/shard_map/all_to_all | solution.py:38
  264.7 3.6 reduce_sum.58
  268.3 0.3 copy.55
  268.6 0.2 copy.32
  268.8 0.1 reshape.115
  269.0 0.3 fusion.22
  269.3 0.4 fusion.35
  269.7 1.3 fusion.25
  270.9 0.0 all-reduce.2.cloned.1.call-update
  271.0 0.3 fusion.47
  271.3 1.3 fusion.1
  272.6 143.4 %all-reduce.2.cloned.1.call-done = f32[128,1280]{1,0:T(8,128)} async-done(((f32[128,1280]{1,0:T(8,128)}), f32[128,1280]{1,0:T(8,128)}) %all-reduce.2.cloned.1.call-update) | async-done | bytes 655376 | tf_op jit(solution)/shard_map/psum | solution.py:93
  416.0 2.0 copy.58
  (5 shorter events, 0.0 us)
Async XLA Ops:
  7.2 1.1 copy-start
  12.6 47.2 %all-to-all-start.1 = ((bf16[4,256,1280]{2,0,1:T(4,128)(2,1)}), bf16[4,256,1280]{2,0,1:T(4,128)(2,1)S(1)}, u32[]{:S(2)}, u32[]{:S(2)}) async-start(bf16[4,256,1280]{2,0,1:T(4,128)(2,1)} %bitcast.171), calls=%async_computation.1 | async-start | bytes 5242880 | tf_op jit(solution)/shard_map/all_to_all | solution.py:31
  63.0 41.2 %all-to-all-start = ((bf16[4,256,1280]{2,0,1:T(4,128)(2,1)}), bf16[4,256,1280]{2,0,1:T(4,128)(2,1)}, u32[]{:S(2)}, u32[]{:S(2)}) async-start(bf16[4,256,1280]{2,0,1:T(4,128)(2,1)} %bitcast.172), calls=%async_computation | async-start | bytes 5242880 | tf_op jit(solution)/shard_map/all_to_all | solution.py:31
  110.5 1.0 copy-start.2
  122.3 70.2 %all-to-all-start.2 = ((f32[4,256,1280]{2,0,1:T(4,128)}), f32[4,256,1280]{2,0,1:T(4,128)}, u32[]{:S(2)}, u32[]{:S(2)}) async-start(f32[4,256,1280]{2,0,1:T(4,128)} %copy.25), calls=%async_computation.2 | async-start | bytes 10485760 | tf_op jit(solution)/shard_map/all_to_all | solution.py:38
  192.4 72.3 %all-to-all-start.3 = ((f32[4,256,1280]{2,0,1:T(4,128)}), f32[4,256,1280]{2,0,1:T(4,128)}, u32[]{:S(2)}, u32[]{:S(2)}) async-start(f32[4,256,1280]{2,0,1:T(4,128)} %copy.30), calls=%async_computation.3 | async-start | bytes 10485760 | tf_op jit(solution)/shard_map/all_to_all | solution.py:38
  200.3 215.7 %all-reduce.2.cloned.1.call-start = ((), (), s32[]{:S(2)}) async-start(), calls=%async_computation.4 | async-start | bytes 1310720 | tf_op jit(solution)/shard_map/psum | solution.py:93
  200.6 5.7 %copy-start.1 = (f32[4,256,576]{1,2,0:T(8,128)S(1)}, f32[4,256,576]{1,2,0:T(8,128)}, u32[]{:S(2)}) copy-start(f32[4,256,576]{1,2,0:T(8,128)} %fusion.15) | copy-start | bytes 7077892
  264.7 4.3 %copy-start.3 = (bf16[1,256,1280]{2,1,0:T(8,128)(2,1)S(1)}, bf16[1,256,1280]{2,1,0:T(8,128)(2,1)}, u32[]{:S(2)}) copy-start(bf16[1,256,1280]{2,1,0:T(8,128)(2,1)} %param.9) | copy-start | bytes 1966084
  269.6 1.6 copy-start.4
Sparse Core Ops, SparseCore 0:
  271.1 144.8 all-reduce.1
where the time goes:
time: 426 us; the launch traced here: 425 us
  waiting for transfers between devices  305 us (72%)
  matrix products  41.3 us (10%)
  starting transfers between devices  30.9 us (7%)
  local copies, waits for them, and re-layouts  26 us (6%)
  between operations  14.2 us (3%)
  other arithmetic  7.38 us (2%)
    psum x1, waiting for transfers between devices, per_device(): grad_params = lax.psum(local_params, ('expert', 'dp'))  143 us
    all_to_all x2, waiting for transfers between devices, from_experts(): lax.all_to_all(partial_value, ('expert', 'dp'), split_axis=1, concat_axis...  102 us
    all_to_all x2, waiting for transfers between devices, to_experts(): lax.all_to_all(copies, ('expert', 'dp'), split_axis=1, concat_axis=1, til...  59.6 us
    all_to_all x2, starting transfers between devices, to_experts(): lax.all_to_all(copies, ('expert', 'dp'), split_axis=1, concat_axis=1, til...  17.1 us
    all_to_all x2, starting transfers between devices, from_experts(): lax.all_to_all(partial_value, ('expert', 'dp'), split_axis=1, concat_axis...  13.5 us
  transfers between devices with their start and end apart: 5, of which 5 were waited for; matrix products, arithmetic and copies ran while one was open for 9% of the time, Pallas kernels for 0%

commit v1 on v0

--- a/solution.py
+++ b/solution.py
@@ -39,7 +39,17 @@
         partial_value, ("expert", "dp"), split_axis=1, concat_axis=1, tiled=True
     )
     returned = returned.reshape(resident, n_expert, n_group, row_block, feature)
-    return jnp.sum(returned, axis=2).astype(jnp.bfloat16)
+    return jnp.sum(returned, axis=2, dtype=jnp.float32).astype(jnp.bfloat16)
+
+
+def sum_over_all(value):
+    axes = ("expert", "dp")
+    n = lax.axis_size(axes)
+    rows, feature = value.shape
+    terms = lax.all_to_all(value, axes, split_axis=0, concat_axis=0, tiled=True)
+    mine = jnp.sum(terms.reshape(n, rows // n, feature), axis=0)
+    copies = jnp.broadcast_to(mine[None], (n, rows // n, feature)).reshape(rows, feature)
+    return lax.all_to_all(copies, axes, split_axis=0, concat_axis=0, tiled=True)
 
 
 def per_device(tokens, slot_params, expert_in, expert_out, grad_out):
@@ -60,7 +70,7 @@
     active = gelu_value(hidden).astype(jnp.bfloat16)
     partial_value = jnp.einsum(
         "ehr,ehd->erd", active, expert_out, preferred_element_type=jnp.float32
-    )
+    ).astype(jnp.bfloat16)
     slot_out = (
         from_experts(partial_value, n_expert).transpose(1, 0, 2, 3).reshape(-1, images, feature)
     )
@@ -78,7 +88,9 @@
     grad_w_in = jnp.einsum(
         "ehr,erd->ehd", d_hidden, expert_rows, preferred_element_type=jnp.float32
     ).astype(jnp.bfloat16)
-    d_partial = jnp.einsum("ehr,ehd->erd", d_hidden, expert_in, preferred_element_type=jnp.float32)
+    d_partial = jnp.einsum(
+        "ehr,ehd->erd", d_hidden, expert_in, preferred_element_type=jnp.float32
+    ).astype(jnp.bfloat16)
     d_slot_in = from_experts(d_partial, n_expert).transpose(1, 0, 2, 3).reshape(-1, images, feature)
     d_dispatch = jnp.einsum("snd,nmd->nsm", d_slot_in, tokens, preferred_element_type=jnp.float32)
     d_logits = (
@@ -90,7 +102,7 @@
         + jnp.einsum("nsm,sd->nmd", d_logits, slot_params, preferred_element_type=jnp.float32)
     ).astype(jnp.bfloat16)
     local_params = jnp.einsum("nsm,nmd->sd", d_logits, tokens, preferred_element_type=jnp.float32)
-    grad_params = lax.psum(local_params, ("expert", "dp"))
+    grad_params = sum_over_all(local_params)
     return (grad_tokens, grad_params, grad_w_in, grad_w_out)
 
 

time: 426 us -> 255 us (0.60)
  waiting for transfers between devices: 305 us -> 129 us
  between operations: 14.2 us -> 0.94 us
  starting transfers between devices: 30.9 us -> 39.6 us
    psum x1 -> x0, waiting for transfers between devices: 143 us -> none  [per_device(): grad_params = lax.psum(local_params, ('expert', 'dp'))]
    all_to_all x2, waiting for transfers between devices: 102 us -> 54.4 us  [from_experts(): lax.all_to_all(partial_value, ('expert', 'dp'), split_axis=1, concat_axis...]
    all_to_all x0 -> x2, waiting for transfers between devices: none -> 15.5 us  [the longest x1 8.03 us: sum_over_all(): terms = lax.all_to_all(value, axes, split_axis=0, concat_axis=0, tiled=True)]
    dot_general x2 -> x0, local copies, waits for them, and re-layouts: 11.5 us -> none  [the longest x1 5.74 us: per_device(): jnp.einsum('ehr,ehd->erd', active, expert_out, preferred_element_type=jnp...]
    all_to_all x0 -> x2, starting transfers between devices: none -> 11.1 us  [the longest x1 5.57 us: sum_over_all(): return lax.all_to_all(copies, axes, split_axis=0, concat_axis=0, tiled=True)]
    convert_element_type x2, local copies, waits for them, and re-layouts: 0.45 us -> 7.03 us  [the longest x1 3.52 us: per_device(): d_partial = jnp.einsum('ehr,ehd->erd', d_hidden, expert_in, preferred_ele...]
    reduce_sum x2 -> x3, other arithmetic: 7.19 us -> 9.11 us  [the longest x2 7.61 us: from_experts(): return jnp.sum(returned, axis=2, dtype=jnp.float32).astype(jnp.bfloat16)]
  transfers between devices with their start and end apart: 5 -> 6, of which waited for: 5 -> 6; matrix products, arithmetic and copies ran while one was open for 9% -> 17% of each run, Pallas kernels for 0% -> 0%
where the time goes in v1:
time: 255 us; the launch traced here: 254 us
  waiting for transfers between devices  129 us (51%)
  matrix products  44.5 us (17%)
  starting transfers between devices  39.6 us (16%)
  local copies, waits for them, and re-layouts  30.2 us (12%)
  other arithmetic  9.31 us (4%)
    all_to_all x2, waiting for transfers between devices, to_experts(): lax.all_to_all(copies, ('expert', 'dp'), split_axis=1, concat_axis=1, til...  59.6 us
    all_to_all x2, waiting for transfers between devices, from_experts(): lax.all_to_all(partial_value, ('expert', 'dp'), split_axis=1, concat_axis...  54.4 us
    all_to_all x2, starting transfers between devices, to_experts(): lax.all_to_all(copies, ('expert', 'dp'), split_axis=1, concat_axis=1, til...  17.1 us
    all_to_all x2, starting transfers between devices, from_experts(): lax.all_to_all(partial_value, ('expert', 'dp'), split_axis=1, concat_axis...  11.4 us
    all_to_all x1, waiting for transfers between devices, sum_over_all(): terms = lax.all_to_all(value, axes, split_axis=0, concat_axis=0, tiled=True)  8.03 us
    reduce_sum x2, other arithmetic, from_experts(): return jnp.sum(returned, axis=2, dtype=jnp.float32).astype(jnp.bfloat16)  7.61 us
    all_to_all x1, waiting for transfers between devices, sum_over_all(): return lax.all_to_all(copies, axes, split_axis=0, concat_axis=0, tiled=True)  7.44 us
    dot_general x1, matrix products, per_device(): jnp.einsum('ehr,erd->ehd', active, d_rows, preferred_element_type=jnp.flo...  6.76 us
  transfers between devices with their start and end apart: 6, of which 6 were waited for; matrix products, arithmetic and copies ran while one was open for 17% of the time, Pallas kernels for 0%

profile of v1, /device:TPU:1, one launch (start us, length us, event | category | flops | bytes accessed | tf_op | source)
XLA Modules:
  0.0 253.8 jit_solution(9399114975168335287)
XLA Ops:
  0.6 0.0 copy-start
  0.6 1.1 copy-done
  1.7 1.4 fusion.51
  3.1 0.2 fusion.38
  3.3 0.3 fusion.13
  3.6 0.1 reshape.126
  3.7 0.1 copy.23
  3.9 2.2 broadcast_in_dim.5
  6.0 11.5 %all-to-all-start.1 = ((bf16[4,256,1280]{2,0,1:T(4,128)(2,1)}), bf16[4,256,1280]{2,0,1:T(4,128)(2,1)S(1)}, u32[]{:S(2)}, u32[]{:S(2)}) async-start(bf16[4,256,1280]{2,0,1:T(4,128)(2,1)} %bitcast.178), calls=%async_computation.1 | async-start | bytes 5242880 | tf_op jit(solution)/shard_map/all_to_all | solution.py:31
  17.6 2.2 fusion.12
  19.8 1.8 reshape.124
  21.6 1.8 copy.21
  23.4 29.9 %all-to-all-done.1 = bf16[4,256,1280]{2,0,1:T(4,128)(2,1)S(1)} async-done(((bf16[4,256,1280]{2,0,1:T(4,128)(2,1)}), bf16[4,256,1280]{2,0,1:T(4,128)(2,1)S(1)}, u32[]{:S(2)}, u32[]{:S(2)}) %all-to-all-start.1) | async-done | bytes 2621472 | tf_op jit(solution)/shard_map/all_to_all | solution.py:31
  53.3 3.1 %broadcast_in_dim.4 = bf16[4,16,8,2,1280]{4,0,3,2,1:T(4,128)(2,1)} broadcast(bf16[4,16,2,1280]{3,0,2,1:T(4,128)(2,1)} %copy.21), dimensions={0,1,3,4} | broadcast | bytes 2949120 | tf_op jit(solution)/shard_map/broadcast_in_dim | solution.py:29
  56.4 5.6 %all-to-all-start = ((bf16[4,256,1280]{2,0,1:T(4,128)(2,1)}), bf16[4,256,1280]{2,0,1:T(4,128)(2,1)}, u32[]{:S(2)}, u32[]{:S(2)}) async-start(bf16[4,256,1280]{2,0,1:T(4,128)(2,1)} %bitcast.179), calls=%async_computation | async-start | bytes 5242880 | tf_op jit(solution)/shard_map/all_to_all | solution.py:31
  62.0 5.9 %fusion.15 = f32[4,256,576]{1,2,0:T(8,128)} fusion(bf16[4,576,1280]{2,1,0:T(8,128)(2,1)} %param.7, bf16[4,256,1280]{2,0,1:T(4,128)(2,1)S(1)} %all-to-all-done.1), kind=kOutput, calls=%fused_computation.26 | convolution fusion | flops 1509949440 | bytes 10878976 | tf_op jit(solution)/shard_map/ehd,erd->ehr/dot_general | solution.py:69
  67.9 29.7 %all-to-all-done = bf16[4,256,1280]{2,0,1:T(4,128)(2,1)} async-done(((bf16[4,256,1280]{2,0,1:T(4,128)(2,1)}), bf16[4,256,1280]{2,0,1:T(4,128)(2,1)}, u32[]{:S(2)}, u32[]{:S(2)}) %all-to-all-start) | async-done | bytes 2621472 | tf_op jit(solution)/shard_map/all_to_all | solution.py:31
  97.6 6.4 %fusion.7 = bf16[4,576,256]{2,1,0:T(8,128)(2,1)S(1)} fusion(f32[4,256,576]{1,2,0:T(8,128)} %fusion.15, bf16[4,576,1280]{2,1,0:T(8,128)(2,1)} %param.8, bf16[4,256,1280]{2,0,1:T(4,128)(2,1)} %all-to-all-done), kind=kOutput, calls=%fused_computation.16 | convolution fusion | flops 1515847680 | bytes 12058624 | tf_op jit(solution)/shard_map/ehd,erd->ehr/dot_general | solution.py:83
  104.0 5.4 %convolution_convert_fusion.3 = bf16[4,256,1280]{2,1,0:T(8,128)(2,1)S(1)} fusion(bf16[4,576,256]{2,1,0:T(8,128)(2,1)S(1)} %fusion.7, bf16[4,576,1280]{2,1,0:T(8,128)(2,1)} %param.7), kind=kOutput, calls=%fused_computation.3 | convolution fusion | flops 1511260160 | bytes 9699328 | tf_op jit(solution)/shard_map/ehr,ehd->erd/dot_general | solution.py:91
  109.4 3.5 %copy.25 = bf16[4,256,1280]{2,0,1:T(4,128)(2,1)} copy(bf16[4,256,1280]{2,1,0:T(8,128)(2,1)S(1)} %convolution_convert_fusion.3) | data formatting | bytes 5242880 | tf_op jit(solution)/shard_map/convert_element_type | solution.py:93
  112.9 5.8 %all-to-all-start.2 = ((bf16[4,256,1280]{2,0,1:T(4,128)(2,1)}), bf16[4,256,1280]{2,0,1:T(4,128)(2,1)}, u32[]{:S(2)}, u32[]{:S(2)}) async-start(bf16[4,256,1280]{2,0,1:T(4,128)(2,1)} %copy.25), calls=%async_computation.2 | async-start | bytes 5242880 | tf_op jit(solution)/shard_map/all_to_all | solution.py:38
  118.7 5.7 %convolution_convert_fusion.2 = bf16[4,256,1280]{2,1,0:T(8,128)(2,1)S(1)} fusion(bf16[4,576,1280]{2,1,0:T(8,128)(2,1)} %param.8, f32[4,256,576]{1,2,0:T(8,128)} %fusion.15), kind=kOutput, calls=%fused_computation.2 | convolution fusion | flops 1514209280 | bytes 10878976 | tf_op jit(solution)/shard_map/ehr,ehd->erd/dot_general | solution.py:71
  124.4 3.5 %copy.30 = bf16[4,256,1280]{2,0,1:T(4,128)(2,1)} copy(bf16[4,256,1280]{2,1,0:T(8,128)(2,1)S(1)} %convolution_convert_fusion.2) | data formatting | bytes 5242880 | tf_op jit(solution)/shard_map/convert_element_type | solution.py:73
  127.9 26.4 %all-to-all-done.2 = bf16[4,256,1280]{2,0,1:T(4,128)(2,1)} async-done(((bf16[4,256,1280]{2,0,1:T(4,128)(2,1)}), bf16[4,256,1280]{2,0,1:T(4,128)(2,1)}, u32[]{:S(2)}, u32[]{:S(2)}) %all-to-all-start.2) | async-done | bytes 2621472 | tf_op jit(solution)/shard_map/all_to_all | solution.py:38
  154.3 5.6 %all-to-all-start.3 = ((bf16[4,256,1280]{2,0,1:T(4,128)(2,1)}), bf16[4,256,1280]{2,0,1:T(4,128)(2,1)}, u32[]{:S(2)}, u32[]{:S(2)}) async-start(bf16[4,256,1280]{2,0,1:T(4,128)(2,1)} %copy.30), calls=%async_computation.3 | async-start | bytes 5242880 | tf_op jit(solution)/shard_map/all_to_all | solution.py:38
  159.9 3.8 %reduce_sum.71 = bf16[4,16,2,1280]{3,0,2,1:T(4,128)(2,1)} reduce(bf16[4,16,8,2,1280]{4,0,3,2,1:T(4,128)(2,1)} %bitcast.19, bf16[]{:T(256)} %constant.18.clone.1), dimensions={2}, to_apply=%region_4.0 | reduce | flops 1146880 | bytes 2949122 | tf_op jit(solution)/shard_map/reduce_sum | solution.py:42
  163.7 1.9 copy.60
  165.6 1.8 reshape.129
  167.5 28.0 %all-to-all-done.3 = bf16[4,256,1280]{2,0,1:T(4,128)(2,1)} async-done(((bf16[4,256,1280]{2,0,1:T(4,128)(2,1)}), bf16[4,256,1280]{2,0,1:T(4,128)(2,1)}, u32[]{:S(2)}, u32[]{:S(2)}) %all-to-all-start.3) | async-done | bytes 2621472 | tf_op jit(solution)/shard_map/all_to_all | solution.py:38
  195.5 3.8 %reduce_sum.73 = bf16[4,16,2,1280]{3,0,2,1:T(4,128)(2,1)} reduce(bf16[4,16,8,2,1280]{4,0,3,2,1:T(4,128)(2,1)} %bitcast.23, bf16[]{:T(256)} %constant.18.clone.1), dimensions={2}, to_apply=%region_6.0 | reduce | flops 1146880 | bytes 2949122 | tf_op jit(solution)/shard_map/reduce_sum | solution.py:42
  199.3 1.9 copy.59
  201.2 1.8 reshape.131
  203.0 1.5 fusion.22
  204.5 1.3 fusion.34
  205.9 0.6 copy-done.4
  206.5 0.4 convolution_bitcast_fusion
  207.0 1.5 copy.35
  208.5 5.5 %all-to-all-start.4 = ((f32[128,1,1280]{2,1,0:T(1,128)}), f32[128,1,1280]{2,1,0:T(1,128)}, u32[]{:S(2)}, u32[]{:S(2)}) async-start(f32[128,1,1280]{2,1,0:T(1,128)} %copy.35), calls=%async_computation.4 | async-start | bytes 1310720 | tf_op jit(solution)/shard_map/all_to_all | solution.py:49
  214.0 6.8 %convolution_convert_fusion = bf16[4,576,1280]{2,1,0:T(8,128)(2,1)} fusion(bf16[4,256,1280]{2,0,1:T(4,128)(2,1)} %all-to-all-done, f32[4,256,576]{1,2,0:T(8,128)} %fusion.15), kind=kOutput, calls=%fused_computation | convolution fusion | flops 1515847680 | bytes 10878976 | tf_op jit(solution)/shard_map/ehr,erd->ehd/dot_general | solution.py:84
  220.8 8.0 %all-to-all-done.4 = f32[128,1,1280]{2,1,0:T(1,128)} async-done(((f32[128,1,1280]{2,1,0:T(1,128)}), f32[128,1,1280]{2,1,0:T(1,128)}, u32[]{:S(2)}, u32[]{:S(2)}) %all-to-all-start.4) | async-done | bytes 655392 | tf_op jit(solution)/shard_map/all_to_all | solution.py:49
  228.8 1.5 reduce_sum.75
  230.3 1.2 reshape.133
  231.5 5.6 %all-to-all-start.5 = ((f32[128,1,1280]{2,1,0:T(1,128)}), f32[128,1,1280]{2,1,0:T(1,128)}, u32[]{:S(2)}, u32[]{:S(2)}) async-start(f32[128,1,1280]{2,1,0:T(1,128)} %reshape.133), calls=%async_computation.5 | async-start | bytes 1310720 | tf_op jit(solution)/shard_map/all_to_all | solution.py:52
  237.2 5.6 %convolution_convert_fusion.1 = bf16[4,576,1280]{2,1,0:T(8,128)(2,1)} fusion(bf16[4,576,256]{2,1,0:T(8,128)(2,1)} %copy-done.1, bf16[4,256,1280]{2,0,1:T(4,128)(2,1)S(1)} %all-to-all-done.1), kind=kOutput, calls=%fused_computation.1 | convolution fusion | flops 1512898560 | bytes 9699328 | tf_op jit(solution)/shard_map/ehr,erd->ehd/dot_general | solution.py:88
  242.8 0.3 fusion.46
  243.2 1.3 fusion.1
  244.4 7.4 %all-to-all-done.5 = f32[128,1,1280]{2,1,0:T(1,128)} async-done(((f32[128,1,1280]{2,1,0:T(1,128)}), f32[128,1,1280]{2,1,0:T(1,128)}, u32[]{:S(2)}, u32[]{:S(2)}) %all-to-all-start.5) | async-done | bytes 655392 | tf_op jit(solution)/shard_map/all_to_all | solution.py:52
  251.9 2.0 copy.58
  (25 shorter events, 0.1 us)
Async XLA Ops:
  0.6 1.1 copy-start
  3.3 202.6 %copy-start.6 = (f32[256]{0:T(256)}, f32[256]{0:T(256)S(1)}, u32[]{:S(2)}) copy-start(f32[256]{0:T(256)S(1)} %get-tuple-element.6) | copy-start | bytes 3076
  3.3 202.6 %copy-start.8 = (f32[128]{0:T(128)}, f32[128]{0:T(128)S(1)}, u32[]{:S(2)}) copy-start(f32[128]{0:T(128)S(1)} %get-tuple-element.7) | copy-start | bytes 1540
  6.0 47.2 %all-to-all-start.1 = ((bf16[4,256,1280]{2,0,1:T(4,128)(2,1)}), bf16[4,256,1280]{2,0,1:T(4,128)(2,1)S(1)}, u32[]{:S(2)}, u32[]{:S(2)}) async-start(bf16[4,256,1280]{2,0,1:T(4,128)(2,1)} %bitcast.178), calls=%async_computation.1 | async-start | bytes 5242880 | tf_op jit(solution)/shard_map/all_to_all | solution.py:31
  56.4 41.2 %all-to-all-start = ((bf16[4,256,1280]{2,0,1:T(4,128)(2,1)}), bf16[4,256,1280]{2,0,1:T(4,128)(2,1)}, u32[]{:S(2)}, u32[]{:S(2)}) async-start(bf16[4,256,1280]{2,0,1:T(4,128)(2,1)} %bitcast.179), calls=%async_computation | async-start | bytes 5242880 | tf_op jit(solution)/shard_map/all_to_all | solution.py:31
  104.0 5.4 %copy-start.1 = (bf16[4,576,256]{2,1,0:T(8,128)(2,1)}, bf16[4,576,256]{2,1,0:T(8,128)(2,1)S(1)}, u32[]{:S(2)}) copy-start(bf16[4,576,256]{2,1,0:T(8,128)(2,1)S(1)} %fusion.7) | copy-start | bytes 3538948
  112.9 41.4 %all-to-all-start.2 = ((bf16[4,256,1280]{2,0,1:T(4,128)(2,1)}), bf16[4,256,1280]{2,0,1:T(4,128)(2,1)}, u32[]{:S(2)}, u32[]{:S(2)}) async-start(bf16[4,256,1280]{2,0,1:T(4,128)(2,1)} %copy.25), calls=%async_computation.2 | async-start | bytes 5242880 | tf_op jit(solution)/shard_map/all_to_all | solution.py:38
  154.3 41.2 %all-to-all-start.3 = ((bf16[4,256,1280]{2,0,1:T(4,128)(2,1)}), bf16[4,256,1280]{2,0,1:T(4,128)(2,1)}, u32[]{:S(2)}, u32[]{:S(2)}) async-start(bf16[4,256,1280]{2,0,1:T(4,128)(2,1)} %copy.30), calls=%async_computation.3 | async-start | bytes 5242880 | tf_op jit(solution)/shard_map/all_to_all | solution.py:38
  205.9 0.7 copy-start.4
  205.9 0.7 copy-start.10
  205.9 0.6 copy-start.12
  208.5 20.3 %all-to-all-start.4 = ((f32[128,1,1280]{2,1,0:T(1,128)}), f32[128,1,1280]{2,1,0:T(1,128)}, u32[]{:S(2)}, u32[]{:S(2)}) async-start(f32[128,1,1280]{2,1,0:T(1,128)} %copy.35), calls=%async_computation.4 | async-start | bytes 1310720 | tf_op jit(solution)/shard_map/all_to_all | solution.py:49
  231.5 20.4 %all-to-all-start.5 = ((f32[128,1,1280]{2,1,0:T(1,128)}), f32[128,1,1280]{2,1,0:T(1,128)}, u32[]{:S(2)}, u32[]{:S(2)}) async-start(f32[128,1,1280]{2,1,0:T(1,128)} %reshape.133), calls=%async_computation.5 | async-start | bytes 1310720 | tf_op jit(solution)/shard_map/all_to_all | solution.py:52
  237.1 5.7 %copy-start.3 = (bf16[128,1280]{1,0:T(8,128)(2,1)S(1)}, bf16[128,1280]{1,0:T(8,128)(2,1)}, u32[]{:S(2)}) copy-start(bf16[128,1280]{1,0:T(8,128)(2,1)} %reshape.129) | copy-start | bytes 983044
  237.1 5.7 %copy-start.9 = (f32[128]{0:T(128)S(1)}, f32[128]{0:T(128)}, u32[]{:S(2)}) copy-start(f32[128]{0:T(128)} %copy-done.8) | copy-start | bytes 1540
  237.1 6.0 %copy-start.2 = (bf16[128,1280]{1,0:T(8,128)(2,1)S(1)}, bf16[128,1280]{1,0:T(8,128)(2,1)}, u32[]{:S(2)}) copy-start(bf16[128,1280]{1,0:T(8,128)(2,1)} %param.6) | copy-start | bytes 983044
  237.1 6.0 %copy-start.5 = (f32[128,256]{0,1:T(8,128)S(1)}, f32[128,256]{0,1:T(8,128)}, u32[]{:S(2)}) copy-start(f32[128,256]{0,1:T(8,128)} %copy-done.4) | copy-start | bytes 393220
  237.1 6.0 %copy-start.7 = (f32[256]{0:T(256)S(1)}, f32[256]{0:T(256)}, u32[]{:S(2)}) copy-start(f32[256]{0:T(256)} %copy-done.6) | copy-start | bytes 3076
  237.1 6.0 %copy-start.11 = (f32[256]{0:T(256)S(1)}, f32[256]{0:T(256)}, u32[]{:S(2)}) copy-start(f32[256]{0:T(256)} %copy-done.10) | copy-start | bytes 3076
  237.1 6.0 %copy-start.13 = (f32[128]{0:T(128)S(1)}, f32[128]{0:T(128)}, u32[]{:S(2)}) copy-start(f32[128]{0:T(128)} %copy-done.12) | copy-start | bytes 1540

commit v2 on v1

v2 whole, which is shorter than its diff:
```python
import functools
import math

import jax
import jax.numpy as jnp
from jax import lax
from jax.experimental import pallas as pl
from jax.experimental.pallas import tpu as pltpu
from jax.sharding import Mesh, PartitionSpec as P

SLOTS = 2
NAMES = ("yh", "x", "c", "yl", "z")
EXPERT = ("yh", "x", "c")
GROUP = ("yl", "z")
SWAP = [(0, 1), (1, 0)]
BF = jnp.bfloat16
F32 = jnp.float32

inv_root_two = 1.0 / math.sqrt(2.0)
inv_root_tau = 1.0 / math.sqrt(2.0 * math.pi)


def dot(a, b, ca, cb):
    return lax.dot_general(a, b, (((ca,), (cb,)), ((), ())), preferred_element_type=F32)


def params(limit=24):
    return pltpu.CompilerParams(vmem_limit_bytes=limit * 2**20)


def up(value):
    return lax.ppermute(value, "z", [(i, (i + 1) % 4) for i in range(4)])


def down(value):
    return lax.ppermute(value, "z", [(i, (i + 3) % 4) for i in range(4)])


def across(value):
    return lax.ppermute(value, "yl", SWAP)


def one_hot_rows(rows, n_expert, resident):
    r = lax.broadcasted_iota(jnp.int32, (rows, rows), 0)
    k = lax.broadcasted_iota(jnp.int32, (rows, rows), 1)
    per = n_expert * SLOTS
    e, kind, source, s = r // (2 * per), r // per % 2, r % per // SLOTS, r % SLOTS
    wanted = ((source * 2 + kind) * resident + e) * SLOTS + s
    return (k == wanted).astype(F32).astype(BF)


def route_kernel(n_expert, tokens, slot_params, grad_out, rows, p_dispatch, p_combine):
    t = tokens[0]
    slots, feature = slot_params.shape
    logits = dot(slot_params[...], t, 1, 1)
    wide = jnp.exp(logits - jnp.max(logits, axis=1, keepdims=True))
    pd = wide / jnp.sum(wide, axis=1, keepdims=True)
    p_dispatch[...] = pd
    tall = jnp.exp(logits - jnp.max(logits, axis=0, keepdims=True))
    pc = tall / jnp.sum(tall, axis=0, keepdims=True)
    p_combine[...] = pc
    shape = (n_expert, slots // n_expert, feature)
    slot_in = dot(pd.astype(BF), t, 1, 0).reshape(shape)
    d_slot_out = dot(pc.astype(BF), grad_out[0], 1, 0).reshape(shape)
    both = jnp.concatenate([slot_in, d_slot_out], axis=1).astype(BF)
    rows[...] = both.reshape(rows.shape)


def route(tokens, slot_params, grad_out, n_expert):
    _, length, feature = tokens.shape
    slots = slot_params.shape[0]
    rows = jax.ShapeDtypeStruct((2 * slots, feature), BF)
    probs = jax.ShapeDtypeStruct((slots, length), F32)
    return pl.pallas_call(
        functools.partial(route_kernel, n_expert),
        out_shape=(rows, probs, probs),
        compiler_params=params(),
        name="route",
    )(tokens, slot_params, grad_out)


def sort_kernel(n_expert, resident, rows, whole, first, second):
    n = rows.shape[0]
    out = dot(one_hot_rows(n, n_expert, resident), rows[...], 1, 0).astype(BF)
    whole[...] = out.reshape(whole.shape)
    half = out.reshape(2, *first.shape)
    first[...] = half[0]
    second[...] = half[1]


def sort_rows(rows, n_expert, resident):
    n, feature = rows.shape
    block = n // resident
    return pl.pallas_call(
        functools.partial(sort_kernel, n_expert, resident),
        out_shape=(
            jax.ShapeDtypeStruct((resident, block, feature), BF),
            jax.ShapeDtypeStruct((resident // 2, block, feature), BF),
            jax.ShapeDtypeStruct((resident // 2, block, feature), BF),
        ),
        compiler_params=params(),
        name="sort_rows",
    )(rows)


def after(values, others):
    return lax.optimization_barrier((tuple(values), tuple(others)))[0]


def gather(whole, first, second):
    low_first, high_second = up(first), down(second)
    low_second, high_first = up(second), down(first)
    y = across(whole)
    (y,) = after((y,), (low_second, high_first))
    far_first, far_second = up(low_first), down(high_second)
    y_low, y_high = up(y), down(y)
    y_far_first, y_far_second = across(far_first), across(far_second)
    return (
        first, second, low_first, low_second, far_first, far_second, high_first, high_second,
        y, y_low, y_far_first, y_far_second, y_high,
    )


def piece_specs(block, feature, resident):
    half = resident // 2
    whole = pl.BlockSpec((1, block, feature), lambda e: (e, 0, 0))
    first = pl.BlockSpec((1, block, feature), lambda e: (jnp.minimum(e, half - 1), 0, 0))
    second = pl.BlockSpec((1, block, feature), lambda e: (jnp.maximum(e - half, 0), 0, 0))
    return whole, first, second


def assemble(refs, into, resident):
    e = pl.program_id(0)
    part = refs[0].shape[1] // 2
    halves = {0: (0, 1), 1: (2, 3), 2: (4, 5), 3: (6, 7), 6: (10, 11)}
    wholes = {4: 8, 5: 9, 7: 12}

    def copy(place, ref):
        for kind in range(2):
            into[kind, place * part : (place + 1) * part] = ref[0, kind * part : (kind + 1) * part]

    for place, at in wholes.items():
        copy(place, refs[at])

    @pl.when(e < resident // 2)
    def _():
        for place, (one, _) in halves.items():
            copy(place, refs[one])

    @pl.when(e >= resident // 2)
    def _():
        for place, (_, two) in halves.items():
            copy(place, refs[two])


def scatter_out(kind, total, refs, resident):
    e = pl.program_id(0)
    part = refs[0].shape[1] // 2
    own, y_own, low1, low2, far1, far2, high1, high2, yfar1, yfar2, ylow, yhigh = refs

    def put(ref, place):
        ref[0, kind * part : (kind + 1) * part] = total[place * part : (place + 1) * part]

    put(own, 0)
    put(y_own, 4)
    put(ylow, 5)
    put(yhigh, 7)

    @pl.when(e < resident // 2)
    def _():
        for ref, place in ((low1, 1), (far1, 2), (high1, 3), (yfar1, 6)):
            put(ref, place)

    @pl.when(e >= resident // 2)
    def _():
        for ref, place in ((low2, 1), (far2, 2), (high2, 3), (yfar2, 6)):
            put(ref, place)


def expert_kernel(resident, *refs):
    pieces, (w_in, w_out), (active, d_hidden) = refs[:13], refs[13:15], refs[15:17]
    partial, rows = refs[17:29], refs[29]
    assemble(pieces, rows, resident)
    hidden = dot(w_in[0], rows[0], 1, 1)
    d_active = dot(w_out[0], rows[1], 1, 1)
    bell = 0.5 * (1.0 + lax.erf(hidden * inv_root_two))
    act = (hidden * bell).astype(BF)
    active[0] = act
    slope = bell + hidden * jnp.exp(-0.5 * hidden * hidden) * inv_root_tau
    dh = (d_active * slope).astype(BF)
    d_hidden[0] = dh
    scatter_out(0, dot(act, w_out[0], 0, 0).astype(BF), partial, resident)
    scatter_out(1, dot(dh, w_in[0], 0, 0).astype(BF), partial, resident)


def per_expert(*shape):
    return pl.BlockSpec((1, *shape), lambda e: (e, 0, 0))


def expert_call(pieces, w_in, w_out):
    resident, hid, feature = w_in.shape
    block = pieces[8].shape[1]
    total = 4 * block
    whole, first, second = piece_specs(block, feature, resident)
    halves = [first, second]
    in_specs = halves * 4 + [whole, whole] + halves + [whole]
    in_specs += [per_expert(hid, feature)] * 2
    wide = jax.ShapeDtypeStruct((resident, block, feature), BF)
    half = jax.ShapeDtypeStruct((resident // 2, block, feature), BF)
    out_shape = [jax.ShapeDtypeStruct((resident, hid, total), BF)] * 2
    out_shape += [wide, wide] + [half] * 8 + [wide, wide]
    out_specs = [per_expert(hid, total)] * 2
    out_specs += [whole, whole] + halves * 4 + [whole, whole]
    work = resident * hid * total * feature
    return pl.pallas_call(
        functools.partial(expert_kernel, resident),
        grid=(resident,),
        in_specs=in_specs,
        out_specs=out_specs,
        out_shape=out_shape,
        scratch_shapes=[pltpu.VMEM((2, total, feature), BF)],
        compiler_params=params(60),
        cost_estimate=pl.CostEstimate(flops=8 * work, bytes_accessed=24 * 2**20, transcendentals=0),
        name="expert",
    )(*pieces, w_in, w_out)


def weights_kernel(resident, *refs):
    pieces, (active, d_hidden) = refs[:13], refs[13:15]
    grad_w_out, grad_w_in, rows = refs[15:]
    assemble(pieces, rows, resident)
    grad_w_out[0] = dot(active[0], rows[1], 1, 0).astype(BF)
    grad_w_in[0] = dot(d_hidden[0], rows[0], 1, 0).astype(BF)


def weight_grads(pieces, active, d_hidden):
    resident, hid, total = active.shape
    block, feature = pieces[8].shape[1:]
    whole, first, second = piece_specs(block, feature, resident)
    halves = [first, second]
    in_specs = halves * 4 + [whole, whole] + halves + [whole]
    in_specs += [per_expert(hid, total)] * 2
    out = jax.ShapeDtypeStruct((resident, hid, feature), BF)
    work = resident * hid * total * feature
    return pl.pallas_call(
        functools.partial(weights_kernel, resident),
        grid=(resident,),
        in_specs=in_specs,
        out_specs=[per_expert(hid, feature)] * 2,
        out_shape=[out, out],
        scratch_shapes=[pltpu.VMEM((2, total, feature), BF)],
        compiler_params=params(60),
        cost_estimate=pl.CostEstimate(flops=4 * work, bytes_accessed=20 * 2**20, transcendentals=0),
        name="weight_grads",
    )(*pieces, active, d_hidden)


def add(*values):
    return sum(v.astype(F32) for v in values).astype(BF)


def reduce_back(parts, between):
    own, y_own, low1, low2, far1, far2, high1, high2, yfar1, yfar2, ylow, yhigh = parts
    w1, w2 = across(yfar1), across(yfar2)
    v_up, v_down = up(yhigh), down(ylow)
    w1, w2 = after((w1, w2), between)
    high2, low1 = after((high2, low1), (w1, w2))
    s_up2, s_down1 = up(high2), down(low1)
    h1, h2 = up(add(far1, w1)), down(add(far2, w2))
    wy = across(add(y_own, v_up, v_down))
    s_up1, s_down2 = up(add(high1, h1)), down(add(low2, h2))
    return own, wy, s_up1, s_up2, s_down1, s_down2


def unsort_kernel(n_expert, own, wy, up1, up2, down1, down2, out):
    resident, block, feature = own.shape
    half = resident // 2
    n = resident * block
    wide = lambda ref: ref[...].astype(F32)
    base = wide(own) + wide(wy)
    first = base[:half] + wide(up1) + wide(down1)
    second = base[half:] + wide(up2) + wide(down2)
    total = jnp.concatenate([first, second], axis=0).reshape(n, feature).astype(BF)
    out[...] = dot(one_hot_rows(n, n_expert, resident), total, 0, 0).astype(BF)


def unsort_rows(pieces, n_expert):
    resident, block, feature = pieces[0].shape
    return pl.pallas_call(
        functools.partial(unsort_kernel, n_expert),
        out_shape=jax.ShapeDtypeStruct((resident * block, feature), BF),
        compiler_params=params(),
        name="unsort_rows",
    )(*pieces)


def exchange(rows):
    return lax.all_to_all(rows, EXPERT, split_axis=0, concat_axis=0, tiled=True)


def logits_kernel(n_expert, tokens, grad_out, back, p_dispatch, p_combine, d_logits, local, d_slot):
    t = tokens[0]
    n, feature = back.shape
    wide = back[...].astype(F32).reshape(n_expert, n // n_expert, feature)
    split = n // n_expert // 2
    slot_out = wide[:, :split].reshape(n // 2, feature).astype(BF)
    d_slot_in = wide[:, split:].reshape(n // 2, feature).astype(BF)
    d_slot[...] = d_slot_in
    d_combine = dot(slot_out, grad_out[0], 1, 1)
    d_dispatch = dot(d_slot_in, t, 1, 1)
    pd, pc = p_dispatch[...], p_combine[...]
    grad = pd * (d_dispatch - jnp.sum(pd * d_dispatch, axis=1, keepdims=True)) + pc * (
        d_combine - jnp.sum(pc * d_combine, axis=0, keepdims=True)
    )
    dl = grad.astype(BF)
    d_logits[...] = dl
    local[...] = dot(dl, t, 1, 0)


def logits_back(tokens, grad_out, back, p_dispatch, p_combine, n_expert):
    slots = p_dispatch.shape[0]
    feature = back.shape[1]
    return pl.pallas_call(
        functools.partial(logits_kernel, n_expert),
        out_shape=(
            jax.ShapeDtypeStruct(p_dispatch.shape, BF),
            jax.ShapeDtypeStruct((slots, feature), F32),
            jax.ShapeDtypeStruct((slots, feature), BF),
        ),
        compiler_params=params(),
        name="logits_back",
    )(tokens, grad_out, back, p_dispatch, p_combine)


def tokens_kernel(p_dispatch, d_slot_in, d_logits, slot_params, grad_tokens):
    first = dot(p_dispatch[...].astype(BF), d_slot_in[...], 0, 0)
    second = dot(d_logits[...], slot_params[...], 0, 0)
    grad_tokens[0] = (first + second).astype(BF)


def tokens_back(p_dispatch, d_slot_in, d_logits, slot_params):
    slots, length = p_dispatch.shape
    feature = slot_params.shape[1]
    return pl.pallas_call(
        tokens_kernel,
        out_shape=jax.ShapeDtypeStruct((1, length, feature), BF),
        compiler_params=params(),
        name="tokens_back",
    )(p_dispatch, d_slot_in, d_logits, slot_params)


def sum_over_all(value):
    n = lax.axis_size(NAMES)
    rows, feature = value.shape
    terms = lax.all_to_all(value, NAMES, split_axis=0, concat_axis=0, tiled=True)
    mine = jnp.sum(terms.reshape(n, rows // n, feature), axis=0)
    copies = jnp.broadcast_to(mine[None], (n, rows // n, feature)).reshape(rows, feature)
    return lax.all_to_all(copies, NAMES, split_axis=0, concat_axis=0, tiled=True)


def per_device(tokens, slot_params, expert_in, expert_out, grad_out):
    n_expert = lax.axis_size(EXPERT)
    resident = expert_in.shape[0]
    outgoing, p_dispatch, p_combine = route(tokens, slot_params, grad_out, n_expert)
    pieces = gather(*sort_rows(exchange(outgoing), n_expert, resident))
    active, d_hidden, *partial = expert_call(pieces, expert_in, expert_out)
    grad_w_out, grad_w_in = weight_grads(pieces, active, d_hidden)
    sums = reduce_back(partial, (grad_w_out, grad_w_in))
    back = exchange(unsort_rows(sums, n_expert))
    d_logits, local_params, d_slot_in = logits_back(
        tokens, grad_out, back, p_dispatch, p_combine, n_expert
    )
    grad_params = sum_over_all(local_params)
    grad_tokens = tokens_back(p_dispatch, d_slot_in, d_logits, slot_params)
    return (grad_tokens, grad_params, grad_w_in, grad_w_out)


def solution(mesh):
    parts = Mesh(mesh.devices.reshape(2, 4, 2, 2, 4), NAMES)
    image = P(NAMES, None, None)
    weight = P(EXPERT, GROUP, None)
    return jax.shard_map(
        per_device,
        mesh=parts,
        in_specs=(image, P(), weight, weight, image),
        out_specs=(image, P(), weight, weight),
        check_vma=False,
    )
```

time: 255 us -> 194 us (0.76)
  waiting for transfers between devices: 129 us -> 58.2 us
  blocking collectives: 0 us -> 65.2 us
  matrix products: 44.5 us -> 0 us
  Pallas kernels: 0 us -> 28.6 us
  local copies, waits for them, and re-layouts: 30.2 us -> 8.99 us
  starting transfers between devices: 39.6 us -> 30.5 us
  other arithmetic: 9.31 us -> 0.97 us
    all_to_all x6 -> x1, waiting for transfers between devices: 129 us -> 13.7 us  [sum_over_all(): lax.all_to_all(copies, NAMES, split_axis=0, concat_axis=0, tiled=True)]
    all_to_all x0 -> x3, blocking collectives: none -> 65.2 us  [the longest x2 46.9 us: exchange(): return lax.all_to_all(rows, EXPERT, split_axis=0, concat_axis=0, tiled=True)]
    dot_general x14 -> x0, matrix products: 44.5 us -> none  [the longest x1 6.76 us: per_device(): jnp.einsum('ehr,erd->ehd', active, d_rows, preferred_element_type=jnp.flo...]
    ppermute x0 -> x22, waiting for transfers between devices: none -> 44.4 us  [the longest x8 17 us: up(): return lax.ppermute(value, 'z', [(i, (i + 1) % 4) for i in range(4)])]
    all_to_all x6 -> x1, starting transfers between devices: 39.6 us -> 4.58 us  [sum_over_all(): lax.all_to_all(copies, NAMES, split_axis=0, concat_axis=0, tiled=True)]
    pallas_call x0 -> x7, Pallas kernels: none -> 28.6 us  [the longest x1 15.5 us: expert_call(): pl.pallas_call(functools.partial(expert_kernel, resident), grid=(resident...]
    ppermute x0 -> x22, starting transfers between devices: none -> 25.9 us  [the longest x8 19.2 us: down(): return lax.ppermute(value, 'z', [(i, (i + 3) % 4) for i in range(4)])]
    reduce_sum x3 -> x0, other arithmetic: 7.8 us -> none  [the longest x2 7.61 us: from_experts(): return jnp.sum(returned, axis=2, dtype=jnp.float32).astype(jnp.bfloat16)]
  transfers between devices with their start and end apart: 6 -> 23, of which waited for: 6 -> 12; matrix products, arithmetic and copies ran while one was open for 17% -> 0% of each run, Pallas kernels for 0% -> 5%
where the time goes in v2:
time: 194 us; the launch traced here: 193 us
  blocking collectives  65.2 us (34%)
  waiting for transfers between devices  58.2 us (30%)
  starting transfers between devices  30.5 us (16%)
  Pallas kernels  28.6 us (15%)
  local copies, waits for them, and re-layouts  8.99 us (5%)
    all_to_all x2, blocking collectives, exchange(): return lax.all_to_all(rows, EXPERT, split_axis=0, concat_axis=0, tiled=True)  46.9 us
    ppermute x8, starting transfers between devices, down(): return lax.ppermute(value, 'z', [(i, (i + 3) % 4) for i in range(4)])  19.2 us
    all_to_all x1, blocking collectives, sum_over_all(): lax.all_to_all(value, NAMES, split_axis=0, concat_axis=0, tiled=True)  18.3 us
    ppermute x8, waiting for transfers between devices, up(): return lax.ppermute(value, 'z', [(i, (i + 1) % 4) for i in range(4)])  17 us
    pallas_call x1, Pallas kernels, expert_call(): pl.pallas_call(functools.partial(expert_kernel, resident), grid=(resident...  15.5 us
    ppermute x8, waiting for transfers between devices, down(): return lax.ppermute(value, 'z', [(i, (i + 3) % 4) for i in range(4)])  14.3 us
    all_to_all x1, waiting for transfers between devices, sum_over_all(): lax.all_to_all(copies, NAMES, split_axis=0, concat_axis=0, tiled=True)  13.7 us
    ppermute x6, waiting for transfers between devices, across(): return lax.ppermute(value, 'yl', SWAP)  13.2 us
  transfers between devices with their start and end apart: 23, of which 12 were waited for; matrix products, arithmetic and copies ran while one was open for 0% of the time, Pallas kernels for 5%

profile of v2, /device:TPU:1, one launch (start us, length us, event | category | flops | bytes accessed | tf_op | source)
XLA Modules:
  0.0 193.3 jit_solution(14846623223561894989)
XLA Ops:
  0.6 1.1 copy-done
  1.7 1.1 copy-done.2
  2.8 1.0 copy-done.4
  3.8 1.1 route.1
  4.9 21.4 %all_to_all.40 = bf16[16,16,1280]{2,1,0:T(8,128)(2,1)S(1)} all-to-all(bf16[16,16,1280]{2,1,0:T(8,128)(2,1)S(1)} %bitcast.12), channel_id=1, replica_groups=mesh['yh'=2,'x'=4,'c'=2,'yl'=2,'z'=4] {'yh','x','c'}, dimensions={0} | all-to-all | bytes 1310720 | tf_op jit(solution)/shard_map/all_to_all | solution.py:298
  26.7 0.5 collective-permute-start.6
  27.2 1.6 collective-permute-start
  28.8 2.1 %collective-permute-start.3 = (bf16[2,64,1280]{2,1,0:T(8,128)(2,1)S(1)}, bf16[2,64,1280]{2,1,0:T(8,128)(2,1)S(1)}, u32[]{:S(2)}, u32[]{:S(2)}) collective-permute-start(bf16[2,64,1280]{2,1,0:T(8,128)(2,1)S(1)} %get-tuple-element.37.refs_1_), channel_id=1, source_target_pairs={{0,3},{1,0},{2,1},{3,2},{4,7},{5,4},{6,5},{7,6},{8,11},{9,8},{10,9... | collective-permute-start | bytes 983048 | tf_op jit(solution)/shard_map/ppermute | solution.py:36
  30.9 1.5 collective-permute-start.5
  32.4 5.9 %collective-permute-done.refs_2_ = bf16[2,64,1280]{2,1,0:T(8,128)(2,1)S(1)} collective-permute-done((bf16[2,64,1280]{2,1,0:T(8,128)(2,1)S(1)}, bf16[2,64,1280]{2,1,0:T(8,128)(2,1)S(1)}, u32[]{:S(2)}, u32[]{:S(2)}) %collective-permute-start) | collective-permute-done | bytes 327712 | tf_op jit(solution)/shard_map/ppermute | solution.py:32
  38.4 2.7 %collective-permute-start.4 = (bf16[2,64,1280]{2,1,0:T(8,128)(2,1)S(1)}, bf16[2,64,1280]{2,1,0:T(8,128)(2,1)S(1)}, u32[]{:S(2)}, u32[]{:S(2)}) collective-permute-start(bf16[2,64,1280]{2,1,0:T(8,128)(2,1)S(1)} %collective-permute-done.3.refs_7_), channel_id=1, source_target_pairs={{0,3},{1,0},{2,1},{3,2},{4,7},{5,4},{6,5},{7,6},{8,11},{9,8},{10,9... | collective-permute-start | bytes 983048 | tf_op jit(solution)/shard_map/ppermute | solution.py:36
  41.0 3.4 %collective-permute-done.5.refs_6_ = bf16[2,64,1280]{2,1,0:T(8,128)(2,1)S(1)} collective-permute-done((bf16[2,64,1280]{2,1,0:T(8,128)(2,1)S(1)}, bf16[2,64,1280]{2,1,0:T(8,128)(2,1)S(1)}, u32[]{:S(2)}, u32[]{:S(2)}) %collective-permute-start.5) | collective-permute-done | bytes 327712 | tf_op jit(solution)/shard_map/ppermute | solution.py:36
  44.4 0.9 collective-permute-done.1.refs_3_
  45.4 0.7 copy-done.22
  46.1 2.4 %collective-permute-start.10 = (bf16[4,64,1280]{2,1,0:T(8,128)(2,1)S(1)}, bf16[4,64,1280]{2,1,0:T(8,128)(2,1)S(1)}, u32[]{:S(2)}, u32[]{:S(2)}) collective-permute-start(bf16[4,64,1280]{2,1,0:T(8,128)(2,1)S(1)} %collective-permute-done.6.refs_8_), channel_id=1, source_target_pairs={{0,3},{1,0},{2,1},{3,2},{4,7},{5,4},{6,5},{7,6},{8,11},{9,8},{10,9... | collective-permute-start | bytes 1966088 | tf_op jit(solution)/shard_map/ppermute | solution.py:36
  48.5 3.9 %collective-permute-done.2.refs_4_ = bf16[2,64,1280]{2,1,0:T(8,128)(2,1)S(1)} collective-permute-done((bf16[2,64,1280]{2,1,0:T(8,128)(2,1)S(1)}, bf16[2,64,1280]{2,1,0:T(8,128)(2,1)S(1)}, u32[]{:S(2)}, u32[]{:S(2)}) %collective-permute-start.2) | collective-permute-done | bytes 327712 | tf_op jit(solution)/shard_map/ppermute | solution.py:32
  52.4 1.1 collective-permute-start.8
  53.5 0.4 collective-permute-start.9
  53.9 5.7 %collective-permute-done.8.refs_10_ = bf16[2,64,1280]{2,1,0:T(8,128)(2,1)S(1)} collective-permute-done((bf16[2,64,1280]{2,1,0:T(8,128)(2,1)S(1)}, bf16[2,64,1280]{2,1,0:T(8,128)(2,1)S(1)}, u32[]{:S(2)}, u32[]{:S(2)}) %collective-permute-start.8) | collective-permute-done | bytes 327712 | tf_op jit(solution)/shard_map/ppermute | solution.py:40
  59.6 7.0 %collective-permute-done.9.refs_11_ = bf16[2,64,1280]{2,1,0:T(8,128)(2,1)S(1)} collective-permute-done((bf16[2,64,1280]{2,1,0:T(8,128)(2,1)S(1)}, bf16[2,64,1280]{2,1,0:T(8,128)(2,1)S(1)}, u32[]{:S(2)}, u32[]{:S(2)}) %collective-permute-start.9) | collective-permute-done | bytes 327712 | tf_op jit(solution)/shard_map/ppermute | solution.py:40
  66.6 0.7 copy-done.26
  67.4 0.8 copy-done.15
  68.2 0.8 copy-done.16
  69.0 15.5 %expert.1 = (bf16[4,576,256]{2,1,0:T(8,128)(2,1)}, bf16[4,576,256]{2,1,0:T(8,128)(2,1)}, bf16[4,64,1280]{2,1,0:T(8,128)(2,1)}, bf16[4,64,1280]{2,1,0:T(8,128)(2,...) custom-call(bf16[2,64,1280]{2,1,0:T(8,128)(2,1)} %copy-done.7, ...), custom_call_target="tpu_custom_call" | custom-call | flops 6039797760 | bytes 25165824 | tf_op jit(solution)/shard_map/expert/pallas_call | solution.py:215
  84.5 1.2 collective-permute-start.14
  85.6 0.4 collective-permute-start.15
  86.0 2.7 %collective-permute-start.12 = (bf16[4,64,1280]{2,1,0:T(8,128)(2,1)}, bf16[4,64,1280]{2,1,0:T(8,128)(2,1)S(1)}, u32[]{:S(2)}, u32[]{:S(2)}) collective-permute-start(bf16[4,64,1280]{2,1,0:T(8,128)(2,1)} %get-tuple-element.43), channel_id=1, source_target_pairs={{0,3},{1,0},{2,1},{3,2},{4,7},{5,4},{6,5},{7,6},{8,11},{9,8},{10,9... | collective-permute-start | bytes 1966088 | tf_op jit(solution)/shard_map/ppermute | solution.py:36
  88.7 8.9 %weight_grads.1 = (bf16[4,576,1280]{2,1,0:T(8,128)(2,1)}, bf16[4,576,1280]{2,1,0:T(8,128)(2,1)}) custom-call(bf16[2,64,1280]{2,1,0:T(8,128)(2,1)} %copy-done.7, bf16[2,64,1280]{2,1,0:T(8,128)(2,1)} %copy-done.8, bf16[2,64,1280]{2,1,0:T(8,128)(2,1)} %copy-done.18, bf16[2,64,1280]{2,1,0:T(8,128)(2,1)} %copy-done.22, bf16[2,64,1280]{2,1,0:T(8,128)(2,1)} %copy-done.23, ...), custom_call_target="tpu_custom_call" | custom-call | flops 3019898880 | bytes 20971520 | tf_op jit(solution)/shard_map/weight_grads/pallas_call | solution.py:245
  97.6 0.4 collective-permute-done.15
  98.1 1.9 collective-permute-start.20
  100.2 2.7 %collective-permute-start.19 = (bf16[2,64,1280]{2,1,0:T(8,128)(2,1)S(1)}, bf16[2,64,1280]{2,1,0:T(8,128)(2,1)S(1)}, u32[]{:S(2)}, u32[]{:S(2)}) collective-permute-start(bf16[2,64,1280]{2,1,0:T(8,128)(2,1)S(1)} %copy-done.17), channel_id=1, source_target_pairs={{0,3},{1,0},{2,1},{3,2},{4,7},{5,4},{6,5},{7,6},{8,11},{9,8},{10,9... | collective-permute-start | bytes 983048 | tf_op jit(solution)/shard_map/ppermute | solution.py:36
  102.9 4.8 %collective-permute-done.20 = bf16[2,64,1280]{2,1,0:T(8,128)(2,1)S(1)} collective-permute-done((bf16[2,64,1280]{2,1,0:T(8,128)(2,1)S(1)}, bf16[2,64,1280]{2,1,0:T(8,128)(2,1)S(1)}, u32[]{:S(2)}, u32[]{:S(2)}) %collective-permute-start.20) | collective-permute-done | bytes 327712 | tf_op jit(solution)/shard_map/ppermute | solution.py:36
  108.0 3.4 %collective-permute-start.21 = (bf16[2,64,1280]{2,1,0:T(8,128)(2,1)S(1)}, bf16[2,64,1280]{2,1,0:T(8,128)(2,1)S(1)}, u32[]{:S(2)}, u32[]{:S(2)}) collective-permute-start(bf16[2,64,1280]{2,1,0:T(8,128)(2,1)S(1)} %add_convert_fusion.1), channel_id=1, source_target_pairs={{0,3},{1,0},{2,1},{3,2},{4,7},{5,4},{6,5},{7,6},{8,11},{9,8},{10,9... | collective-permute-start | bytes 983048 | tf_op jit(solution)/shard_map/ppermute | solution.py:36
  111.7 1.2 collective-permute-start.13
  112.8 2.7 %collective-permute-done.16 = bf16[2,64,1280]{2,1,0:T(8,128)(2,1)S(1)} collective-permute-done((bf16[2,64,1280]{2,1,0:T(8,128)(2,1)S(1)}, bf16[2,64,1280]{2,1,0:T(8,128)(2,1)S(1)}, u32[]{:S(2)}, u32[]{:S(2)}) %collective-permute-start.16) | collective-permute-done | bytes 327712 | tf_op jit(solution)/shard_map/ppermute | solution.py:32
  115.7 6.0 %collective-permute-done.21.down2 = bf16[2,64,1280]{2,1,0:T(8,128)(2,1)S(1)} collective-permute-done((bf16[2,64,1280]{2,1,0:T(8,128)(2,1)S(1)}, bf16[2,64,1280]{2,1,0:T(8,128)(2,1)S(1)}, u32[]{:S(2)}, u32[]{:S(2)}) %collective-permute-start.21) | collective-permute-done | bytes 327712 | tf_op jit(solution)/shard_map/ppermute | solution.py:36
  121.7 3.6 %collective-permute-done.17.up1 = bf16[2,64,1280]{2,1,0:T(8,128)(2,1)S(1)} collective-permute-done((bf16[2,64,1280]{2,1,0:T(8,128)(2,1)S(1)}, bf16[2,64,1280]{2,1,0:T(8,128)(2,1)S(1)}, u32[]{:S(2)}, u32[]{:S(2)}) %collective-permute-start.17) | collective-permute-done | bytes 327712 | tf_op jit(solution)/shard_map/ppermute | solution.py:32
  125.3 0.6 unsort_rows.1
  126.0 25.4 %all_to_all.41 = bf16[16,16,1280]{2,1,0:T(8,128)(2,1)S(1)} all-to-all(bf16[16,16,1280]{2,1,0:T(8,128)(2,1)S(1)} %bitcast.9), channel_id=1, replica_groups=mesh['yh'=2,'x'=4,'c'=2,'yl'=2,'z'=4] {'yh','x','c'}, dimensions={0} | all-to-all | bytes 1310720 | tf_op jit(solution)/shard_map/all_to_all | solution.py:298
  151.4 0.8 logits_back.1
  152.2 0.7 copy.9
  152.9 18.3 %all_to_all.42 = f32[128,1,1280]{2,1,0:T(1,128)S(1)} all-to-all(f32[128,1,1280]{2,1,0:T(1,128)S(1)} %copy.9), channel_id=1, replica_groups=mesh['yh'=2,'x'=4,'c'=2,'yl'=2,'z'=4] {'yh','x','c','yl','z'}, dimensions={0} | all-to-all | bytes 1310720 | tf_op jit(solution)/shard_map/all_to_all | solution.py:355
  171.2 0.4 reduce_sum.9
  171.6 1.2 reshape.28
  172.8 4.6 %all-to-all-start.3 = ((f32[128,1,1280]{2,1,0:T(1,128)}), f32[128,1,1280]{2,1,0:T(1,128)S(1)}, u32[]{:S(2)}, u32[]{:S(2)}) async-start(f32[128,1,1280]{2,1,0:T(1,128)} %reshape.28), calls=%async_computation.3 | async-start | bytes 1310720 | tf_op jit(solution)/shard_map/all_to_all | solution.py:358
  177.4 1.4 tokens_back.1
  178.7 13.7 %all-to-all-done.3 = f32[128,1,1280]{2,1,0:T(1,128)S(1)} async-done(((f32[128,1,1280]{2,1,0:T(1,128)}), f32[128,1,1280]{2,1,0:T(1,128)S(1)}, u32[]{:S(2)}, u32[]{:S(2)}) %all-to-all-start.3) | async-done | bytes 655392 | tf_op jit(solution)/shard_map/all_to_all | solution.py:358
  192.5 0.9 copy.12
  (71 shorter events, 1.4 us)
Async XLA Ops:
  0.6 1.1 copy-start
  1.7 1.1 copy-start.2
  2.8 1.0 copy-start.4
  26.7 40.6 %copy-start.7 = (bf16[2,64,1280]{2,1,0:T(8,128)(2,1)}, bf16[2,64,1280]{2,1,0:T(8,128)(2,1)S(1)}, u32[]{:S(2)}) copy-start(bf16[2,64,1280]{2,1,0:T(8,128)(2,1)S(1)} %get-tuple-element.36.refs_0_) | copy-start | bytes 983044
  26.7 40.6 %copy-start.8 = (bf16[2,64,1280]{2,1,0:T(8,128)(2,1)}, bf16[2,64,1280]{2,1,0:T(8,128)(2,1)S(1)}, u32[]{:S(2)}) copy-start(bf16[2,64,1280]{2,1,0:T(8,128)(2,1)S(1)} %get-tuple-element.37.refs_1_) | copy-start | bytes 983044
  26.7 19.4 %collective-permute-start.6 = (bf16[4,64,1280]{2,1,0:T(8,128)(2,1)S(1)}, bf16[4,64,1280]{2,1,0:T(8,128)(2,1)S(1)}, u32[]{:S(2)}, u32[]{:S(2)}) collective-permute-start(bf16[4,64,1280]{2,1,0:T(8,128)(2,1)S(1)} %get-tuple-element.38), channel_id=1, source_target_pairs={{0,4},{4,0},{1,5},{5,1},{2,6},{6,2},{3,7},{7,3},{8,12},{12,8},{9,1... | collective-permute-start | bytes 1966088 | tf_op jit(solution)/shard_map/ppermute | solution.py:40
  27.2 11.2 %collective-permute-start = (bf16[2,64,1280]{2,1,0:T(8,128)(2,1)S(1)}, bf16[2,64,1280]{2,1,0:T(8,128)(2,1)S(1)}, u32[]{:S(2)}, u32[]{:S(2)}) collective-permute-start(bf16[2,64,1280]{2,1,0:T(8,128)(2,1)S(1)} %get-tuple-element.36.refs_0_), channel_id=1, source_target_pairs={{0,1},{1,2},{2,3},{3,0},{4,5},{5,6},{6,7},{7,4},{8,9},{9,10},{10,1... | collective-permute-start | bytes 983048 | tf_op jit(solution)/shard_map/ppermute | solution.py:32
  28.8 9.5 %collective-permute-start.3 = (bf16[2,64,1280]{2,1,0:T(8,128)(2,1)S(1)}, bf16[2,64,1280]{2,1,0:T(8,128)(2,1)S(1)}, u32[]{:S(2)}, u32[]{:S(2)}) collective-permute-start(bf16[2,64,1280]{2,1,0:T(8,128)(2,1)S(1)} %get-tuple-element.37.refs_1_), channel_id=1, source_target_pairs={{0,3},{1,0},{2,1},{3,2},{4,7},{5,4},{6,5},{7,6},{8,11},{9,8},{10,9... | collective-permute-start | bytes 983048 | tf_op jit(solution)/shard_map/ppermute | solution.py:36
  30.9 13.5 %collective-permute-start.5 = (bf16[2,64,1280]{2,1,0:T(8,128)(2,1)S(1)}, bf16[2,64,1280]{2,1,0:T(8,128)(2,1)S(1)}, u32[]{:S(2)}, u32[]{:S(2)}) collective-permute-start(bf16[2,64,1280]{2,1,0:T(8,128)(2,1)S(1)} %get-tuple-element.36.refs_0_), channel_id=1, source_target_pairs={{0,3},{1,0},{2,1},{3,2},{4,7},{5,4},{6,5},{7,6},{8,11},{9,8},{10,9... | collective-permute-start | bytes 983048 | tf_op jit(solution)/shard_map/ppermute | solution.py:36
  32.4 13.0 %collective-permute-start.1 = (bf16[2,64,1280]{2,1,0:T(8,128)(2,1)S(1)}, bf16[2,64,1280]{2,1,0:T(8,128)(2,1)S(1)}, u32[]{:S(2)}, u32[]{:S(2)}) collective-permute-start(bf16[2,64,1280]{2,1,0:T(8,128)(2,1)S(1)} %get-tuple-element.37.refs_1_), channel_id=1, source_target_pairs={{0,1},{1,2},{2,3},{3,0},{4,5},{5,6},{6,7},{7,4},{8,9},{9,10},{10,1... | collective-permute-start | bytes 983048 | tf_op jit(solution)/shard_map/ppermute | solution.py:32
  38.3 29.0 %copy-start.18 = (bf16[2,64,1280]{2,1,0:T(8,128)(2,1)}, bf16[2,64,1280]{2,1,0:T(8,128)(2,1)S(1)}, u32[]{:S(2)}) copy-start(bf16[2,64,1280]{2,1,0:T(8,128)(2,1)S(1)} %collective-permute-done.refs_2_) | copy-start | bytes 983044
  38.3 14.0 %collective-permute-start.2 = (bf16[2,64,1280]{2,1,0:T(8,128)(2,1)S(1)}, bf16[2,64,1280]{2,1,0:T(8,128)(2,1)S(1)}, u32[]{:S(2)}, u32[]{:S(2)}) collective-permute-start(bf16[2,64,1280]{2,1,0:T(8,128)(2,1)S(1)} %collective-permute-done.refs_2_), channel_id=1, source_target_pairs={{0,1},{1,2},{2,3},{3,0},{4,5},{5,6},{6,7},{7,4},{8,9},{9,10},{10,1... | collective-permute-start | bytes 983048 | tf_op jit(solution)/shard_map/ppermute | solution.py:32
  38.4 29.0 %copy-start.20 = (bf16[2,64,1280]{2,1,0:T(8,128)(2,1)}, bf16[2,64,1280]{2,1,0:T(8,128)(2,1)S(1)}, u32[]{:S(2)}) copy-start(bf16[2,64,1280]{2,1,0:T(8,128)(2,1)S(1)} %collective-permute-done.3.refs_7_) | copy-start | bytes 983044
  38.4 15.1 %collective-permute-start.4 = (bf16[2,64,1280]{2,1,0:T(8,128)(2,1)S(1)}, bf16[2,64,1280]{2,1,0:T(8,128)(2,1)S(1)}, u32[]{:S(2)}, u32[]{:S(2)}) collective-permute-start(bf16[2,64,1280]{2,1,0:T(8,128)(2,1)S(1)} %collective-permute-done.3.refs_7_), channel_id=1, source_target_pairs={{0,3},{1,0},{2,1},{3,2},{4,7},{5,4},{6,5},{7,6},{8,11},{9,8},{10,9... | collective-permute-start | bytes 983048 | tf_op jit(solution)/shard_map/ppermute | solution.py:36
  44.4 22.9 %copy-start.21 = (bf16[2,64,1280]{2,1,0:T(8,128)(2,1)}, bf16[2,64,1280]{2,1,0:T(8,128)(2,1)S(1)}, u32[]{:S(2)}) copy-start(bf16[2,64,1280]{2,1,0:T(8,128)(2,1)S(1)} %collective-permute-done.5.refs_6_) | copy-start | bytes 983044
  46.1 21.3 %copy-start.14 = (bf16[4,64,1280]{2,1,0:T(8,128)(2,1)}, bf16[4,64,1280]{2,1,0:T(8,128)(2,1)S(1)}, u32[]{:S(2)}) copy-start(bf16[4,64,1280]{2,1,0:T(8,128)(2,1)S(1)} %collective-permute-done.6.refs_8_) | copy-start | bytes 1966084
  46.1 20.5 %collective-permute-start.10 = (bf16[4,64,1280]{2,1,0:T(8,128)(2,1)S(1)}, bf16[4,64,1280]{2,1,0:T(8,128)(2,1)S(1)}, u32[]{:S(2)}, u32[]{:S(2)}) collective-permute-start(bf16[4,64,1280]{2,1,0:T(8,128)(2,1)S(1)} %collective-permute-done.6.refs_8_), channel_id=1, source_target_pairs={{0,3},{1,0},{2,1},{3,2},{4,7},{5,4},{6,5},{7,6},{8,11},{9,8},{10,9... | collective-permute-start | bytes 1966088 | tf_op jit(solution)/shard_map/ppermute | solution.py:36
  48.5 18.8 %collective-permute-start.7 = (bf16[4,64,1280]{2,1,0:T(8,128)(2,1)S(1)}, bf16[4,64,1280]{2,1,0:T(8,128)(2,1)S(1)}, u32[]{:S(2)}, u32[]{:S(2)}) collective-permute-start(bf16[4,64,1280]{2,1,0:T(8,128)(2,1)S(1)} %collective-permute-done.6.refs_8_), channel_id=1, source_target_pairs={{0,1},{1,2},{2,3},{3,0},{4,5},{5,6},{6,7},{7,4},{8,9},{9,10},{10,1... | collective-permute-start | bytes 1966088 | tf_op jit(solution)/shard_map/ppermute | solution.py:32
  52.4 14.2 %copy-start.23 = (bf16[2,64,1280]{2,1,0:T(8,128)(2,1)}, bf16[2,64,1280]{2,1,0:T(8,128)(2,1)S(1)}, u32[]{:S(2)}) copy-start(bf16[2,64,1280]{2,1,0:T(8,128)(2,1)S(1)} %collective-permute-done.2.refs_4_) | copy-start | bytes 983044
  52.4 7.2 %collective-permute-start.8 = (bf16[2,64,1280]{2,1,0:T(8,128)(2,1)S(1)}, bf16[2,64,1280]{2,1,0:T(8,128)(2,1)S(1)}, u32[]{:S(2)}, u32[]{:S(2)}) collective-permute-start(bf16[2,64,1280]{2,1,0:T(8,128)(2,1)S(1)} %collective-permute-done.2.refs_4_), channel_id=1, source_target_pairs={{0,4},{4,0},{1,5},{5,1},{2,6},{6,2},{3,7},{7,3},{8,12},{12,8},{9,1... | collective-permute-start | bytes 983048 | tf_op jit(solution)/shard_map/ppermute | solution.py:40
  53.5 13.1 %copy-start.24 = (bf16[2,64,1280]{2,1,0:T(8,128)(2,1)}, bf16[2,64,1280]{2,1,0:T(8,128)(2,1)S(1)}, u32[]{:S(2)}) copy-start(bf16[2,64,1280]{2,1,0:T(8,128)(2,1)S(1)} %collective-permute-done.4.refs_5_) | copy-start | bytes 983044
  53.5 13.1 %collective-permute-start.9 = (bf16[2,64,1280]{2,1,0:T(8,128)(2,1)S(1)}, bf16[2,64,1280]{2,1,0:T(8,128)(2,1)S(1)}, u32[]{:S(2)}, u32[]{:S(2)}) collective-permute-start(bf16[2,64,1280]{2,1,0:T(8,128)(2,1)S(1)} %collective-permute-done.4.refs_5_), channel_id=1, source_target_pairs={{0,4},{4,0},{1,5},{5,1},{2,6},{6,2},{3,7},{7,3},{8,12},{12,8},{9,1... | collective-permute-start | bytes 983048 | tf_op jit(solution)/shard_map/ppermute | solution.py:40
  59.6 7.0 %copy-start.25 = (bf16[2,64,1280]{2,1,0:T(8,128)(2,1)}, bf16[2,64,1280]{2,1,0:T(8,128)(2,1)S(1)}, u32[]{:S(2)}) copy-start(bf16[2,64,1280]{2,1,0:T(8,128)(2,1)S(1)} %collective-permute-done.8.refs_10_) | copy-start | bytes 983044
  67.3 0.8 copy-start.15
  68.2 0.8 copy-start.16
  84.5 13.1 %collective-permute-start.14 = (bf16[2,64,1280]{2,1,0:T(8,128)(2,1)}, bf16[2,64,1280]{2,1,0:T(8,128)(2,1)S(1)}, u32[]{:S(2)}, u32[]{:S(2)}) collective-permute-start(bf16[2,64,1280]{2,1,0:T(8,128)(2,1)} %get-tuple-element.46), channel_id=1, source_target_pairs={{0,4},{4,0},{1,5},{5,1},{2,6},{6,2},{3,7},{7,3},{8,12},{12,8},{9,1... | collective-permute-start | bytes 983048 | tf_op jit(solution)/shard_map/ppermute | solution.py:40
  85.6 12.4 %collective-permute-start.15 = (bf16[2,64,1280]{2,1,0:T(8,128)(2,1)}, bf16[2,64,1280]{2,1,0:T(8,128)(2,1)S(1)}, u32[]{:S(2)}, u32[]{:S(2)}) collective-permute-start(bf16[2,64,1280]{2,1,0:T(8,128)(2,1)} %get-tuple-element.47), channel_id=1, source_target_pairs={{0,4},{4,0},{1,5},{5,1},{2,6},{6,2},{3,7},{7,3},{8,12},{12,8},{9,1... | collective-permute-start | bytes 983048 | tf_op jit(solution)/shard_map/ppermute | solution.py:40
  86.0 22.0 %collective-permute-start.11 = (bf16[4,64,1280]{2,1,0:T(8,128)(2,1)}, bf16[4,64,1280]{2,1,0:T(8,128)(2,1)S(1)}, u32[]{:S(2)}, u32[]{:S(2)}) collective-permute-start(bf16[4,64,1280]{2,1,0:T(8,128)(2,1)} %get-tuple-element.42), channel_id=1, source_target_pairs={{0,1},{1,2},{2,3},{3,0},{4,5},{5,6},{6,7},{7,4},{8,9},{9,10},{10,1... | collective-permute-start | bytes 1966088 | tf_op jit(solution)/shard_map/ppermute | solution.py:32
  86.0 25.4 %collective-permute-start.12 = (bf16[4,64,1280]{2,1,0:T(8,128)(2,1)}, bf16[4,64,1280]{2,1,0:T(8,128)(2,1)S(1)}, u32[]{:S(2)}, u32[]{:S(2)}) collective-permute-start(bf16[4,64,1280]{2,1,0:T(8,128)(2,1)} %get-tuple-element.43), channel_id=1, source_target_pairs={{0,3},{1,0},{2,1},{3,2},{4,7},{5,4},{6,5},{7,6},{8,11},{9,8},{10,9... | collective-permute-start | bytes 1966088 | tf_op jit(solution)/shard_map/ppermute | solution.py:36
  88.7 9.3 %copy-start.13 = (bf16[2,64,1280]{2,1,0:T(8,128)(2,1)S(1)}, bf16[2,64,1280]{2,1,0:T(8,128)(2,1)}, u32[]{:S(2)}) copy-start(bf16[2,64,1280]{2,1,0:T(8,128)(2,1)} %get-tuple-element.59) | copy-start | bytes 983044
  88.7 11.3 %copy-start.12 = (bf16[2,64,1280]{2,1,0:T(8,128)(2,1)S(1)}, bf16[2,64,1280]{2,1,0:T(8,128)(2,1)}, u32[]{:S(2)}) copy-start(bf16[2,64,1280]{2,1,0:T(8,128)(2,1)} %get-tuple-element.45) | copy-start | bytes 983044
  97.6 2.6 %copy-start.19 = (bf16[2,64,1280]{2,1,0:T(8,128)(2,1)S(1)}, bf16[2,64,1280]{2,1,0:T(8,128)(2,1)}, u32[]{:S(2)}) copy-start(bf16[2,64,1280]{2,1,0:T(8,128)(2,1)} %get-tuple-element.56) | copy-start | bytes 983044
  97.6 2.6 %copy-start.17 = (bf16[2,64,1280]{2,1,0:T(8,128)(2,1)S(1)}, bf16[2,64,1280]{2,1,0:T(8,128)(2,1)}, u32[]{:S(2)}) copy-start(bf16[2,64,1280]{2,1,0:T(8,128)(2,1)} %get-tuple-element.57) | copy-start | bytes 983044
  97.6 10.3 %copy-start.11 = (bf16[2,64,1280]{2,1,0:T(8,128)(2,1)S(1)}, bf16[2,64,1280]{2,1,0:T(8,128)(2,1)}, u32[]{:S(2)}) copy-start(bf16[2,64,1280]{2,1,0:T(8,128)(2,1)} %get-tuple-element.58) | copy-start | bytes 983044
  98.0 13.4 %copy-start.9 = (bf16[4,64,1280]{2,1,0:T(8,128)(2,1)S(1)}, bf16[4,64,1280]{2,1,0:T(8,128)(2,1)}, u32[]{:S(2)}) copy-start(bf16[4,64,1280]{2,1,0:T(8,128)(2,1)} %get-tuple-element.41) | copy-start | bytes 1966084
  98.1 9.6 %collective-permute-start.20 = (bf16[2,64,1280]{2,1,0:T(8,128)(2,1)S(1)}, bf16[2,64,1280]{2,1,0:T(8,128)(2,1)S(1)}, u32[]{:S(2)}, u32[]{:S(2)}) collective-permute-start(bf16[2,64,1280]{2,1,0:T(8,128)(2,1)S(1)} %add_convert_fusion.2), channel_id=1, source_target_pairs={{0,3},{1,0},{2,1},{3,2},{4,7},{5,4},{6,5},{7,6},{8,11},{9,8},{10,9... | collective-permute-start | bytes 983048 | tf_op jit(solution)/shard_map/ppermute | solution.py:36
  100.1 15.5 %collective-permute-start.18 = (bf16[2,64,1280]{2,1,0:T(8,128)(2,1)S(1)}, bf16[2,64,1280]{2,1,0:T(8,128)(2,1)S(1)}, u32[]{:S(2)}, u32[]{:S(2)}) collective-permute-start(bf16[2,64,1280]{2,1,0:T(8,128)(2,1)S(1)} %copy-done.19), channel_id=1, source_target_pairs={{0,1},{1,2},{2,3},{3,0},{4,5},{5,6},{6,7},{7,4},{8,9},{9,10},{10,1... | collective-permute-start | bytes 983048 | tf_op jit(solution)/shard_map/ppermute | solution.py:32
  100.2 15.5 %collective-permute-start.19 = (bf16[2,64,1280]{2,1,0:T(8,128)(2,1)S(1)}, bf16[2,64,1280]{2,1,0:T(8,128)(2,1)S(1)}, u32[]{:S(2)}, u32[]{:S(2)}) collective-permute-start(bf16[2,64,1280]{2,1,0:T(8,128)(2,1)S(1)} %copy-done.17), channel_id=1, source_target_pairs={{0,3},{1,0},{2,1},{3,2},{4,7},{5,4},{6,5},{7,6},{8,11},{9,8},{10,9... | collective-permute-start | bytes 983048 | tf_op jit(solution)/shard_map/ppermute | solution.py:36
  107.7 7.8 %collective-permute-start.16 = (bf16[2,64,1280]{2,1,0:T(8,128)(2,1)S(1)}, bf16[2,64,1280]{2,1,0:T(8,128)(2,1)S(1)}, u32[]{:S(2)}, u32[]{:S(2)}) collective-permute-start(bf16[2,64,1280]{2,1,0:T(8,128)(2,1)S(1)} %add_convert_fusion.4), channel_id=1, source_target_pairs={{0,1},{1,2},{2,3},{3,0},{4,5},{5,6},{6,7},{7,4},{8,9},{9,10},{10,1... | collective-permute-start | bytes 983048 | tf_op jit(solution)/shard_map/ppermute | solution.py:32
  108.0 13.7 %collective-permute-start.21 = (bf16[2,64,1280]{2,1,0:T(8,128)(2,1)S(1)}, bf16[2,64,1280]{2,1,0:T(8,128)(2,1)S(1)}, u32[]{:S(2)}, u32[]{:S(2)}) collective-permute-start(bf16[2,64,1280]{2,1,0:T(8,128)(2,1)S(1)} %add_convert_fusion.1), channel_id=1, source_target_pairs={{0,3},{1,0},{2,1},{3,2},{4,7},{5,4},{6,5},{7,6},{8,11},{9,8},{10,9... | collective-permute-start | bytes 983048 | tf_op jit(solution)/shard_map/ppermute | solution.py:36
  111.4 4.1 %copy-start.10 = (bf16[2,64,1280]{2,1,0:T(8,128)(2,1)S(1)}, bf16[2,64,1280]{2,1,0:T(8,128)(2,1)}, u32[]{:S(2)}) copy-start(bf16[2,64,1280]{2,1,0:T(8,128)(2,1)} %get-tuple-element.44) | copy-start | bytes 983044
  111.4 13.9 %copy-start.6 = (bf16[4,64,1280]{2,1,0:T(8,128)(2,1)S(1)}, bf16[4,64,1280]{2,1,0:T(8,128)(2,1)}, u32[]{:S(2)}) copy-start(bf16[4,64,1280]{2,1,0:T(8,128)(2,1)} %get-tuple-element.40.own) | copy-start | bytes 1966084
  111.7 13.6 %collective-permute-start.13 = (bf16[4,64,1280]{2,1,0:T(8,128)(2,1)S(1)}, bf16[4,64,1280]{2,1,0:T(8,128)(2,1)S(1)}, u32[]{:S(2)}, u32[]{:S(2)}) collective-permute-start(bf16[4,64,1280]{2,1,0:T(8,128)(2,1)S(1)} %add_convert_fusion), channel_id=1, source_target_pairs={{0,4},{4,0},{1,5},{5,1},{2,6},{6,2},{3,7},{7,3},{8,12},{12,8},{9,1... | collective-permute-start | bytes 1966088 | tf_op jit(solution)/shard_map/ppermute | solution.py:40
  115.6 9.7 %collective-permute-start.17 = (bf16[2,64,1280]{2,1,0:T(8,128)(2,1)S(1)}, bf16[2,64,1280]{2,1,0:T(8,128)(2,1)S(1)}, u32[]{:S(2)}, u32[]{:S(2)}) collective-permute-start(bf16[2,64,1280]{2,1,0:T(8,128)(2,1)S(1)} %add_convert_fusion.3), channel_id=1, source_target_pairs={{0,1},{1,2},{2,3},{3,0},{4,5},{5,6},{6,7},{7,4},{8,9},{9,10},{10,1... | collective-permute-start | bytes 983048 | tf_op jit(solution)/shard_map/ppermute | solution.py:32
  125.9 25.4 %copy-start.1 = (bf16[1,256,1280]{2,1,0:T(8,128)(2,1)S(1)}, bf16[1,256,1280]{2,1,0:T(8,128)(2,1)}, u32[]{:S(2)}) copy-start(bf16[1,256,1280]{2,1,0:T(8,128)(2,1)} %tokens.3) | copy-start | bytes 1966084
  126.0 25.4 %copy-start.3 = (bf16[1,256,1280]{2,1,0:T(8,128)(2,1)S(1)}, bf16[1,256,1280]{2,1,0:T(8,128)(2,1)}, u32[]{:S(2)}) copy-start(bf16[1,256,1280]{2,1,0:T(8,128)(2,1)} %grad_out.3) | copy-start | bytes 1966084
  171.2 6.2 %copy-start.5 = (bf16[128,1280]{1,0:T(8,128)(2,1)S(1)}, bf16[128,1280]{1,0:T(8,128)(2,1)}, u32[]{:S(2)}) copy-start(bf16[128,1280]{1,0:T(8,128)(2,1)} %slot_params.3) | copy-start | bytes 983044
  172.8 19.7 %all-to-all-start.3 = ((f32[128,1,1280]{2,1,0:T(1,128)}), f32[128,1,1280]{2,1,0:T(1,128)S(1)}, u32[]{:S(2)}, u32[]{:S(2)}) async-start(f32[128,1,1280]{2,1,0:T(1,128)} %reshape.28), calls=%async_computation.3 | async-start | bytes 1310720 | tf_op jit(solution)/shard_map/all_to_all | solution.py:358
  (2 other events, 1.4 us)

commit v3 on v2

v3 whole, which is shorter than its diff:
```python
import functools
import math

import jax
import jax.numpy as jnp
from jax import lax
from jax.experimental import pallas as pl
from jax.experimental.pallas import tpu as pltpu
from jax.sharding import Mesh, PartitionSpec as P

SLOTS = 2
NAMES = ("yh", "x", "c", "yl", "z")
EXPERT = ("yh", "x", "c")
GROUP = ("yl", "z")
SWAP = [(0, 1), (1, 0)]
BF = jnp.bfloat16
F32 = jnp.float32

inv_root_two = 1.0 / math.sqrt(2.0)
inv_root_tau = 1.0 / math.sqrt(2.0 * math.pi)


def dot(a, b, ca, cb):
    return lax.dot_general(a, b, (((ca,), (cb,)), ((), ())), preferred_element_type=F32)


def params(limit=24):
    return pltpu.CompilerParams(vmem_limit_bytes=limit * 2**20)


def up(value, name):
    with jax.named_scope(name + "_up"):
        return lax.ppermute(value, "z", [(i, (i + 1) % 4) for i in range(4)])


def down(value, name):
    with jax.named_scope(name + "_down"):
        return lax.ppermute(value, "z", [(i, (i + 3) % 4) for i in range(4)])


def across(value, name):
    with jax.named_scope(name + "_across"):
        return lax.ppermute(value, "yl", SWAP)


def one_hot_rows(rows, n_expert, resident):
    r = lax.broadcasted_iota(jnp.int32, (rows, rows), 0)
    k = lax.broadcasted_iota(jnp.int32, (rows, rows), 1)
    per = n_expert * SLOTS
    e, kind, source, s = r // (2 * per), r // per % 2, r % per // SLOTS, r % SLOTS
    wanted = ((source * 2 + kind) * resident + e) * SLOTS + s
    return (k == wanted).astype(F32).astype(BF)


def route_kernel(n_expert, tokens, slot_params, grad_out, rows, p_dispatch, p_combine):
    t = tokens[0]
    slots, feature = slot_params.shape
    logits = dot(slot_params[...], t, 1, 1)
    wide = jnp.exp(logits - jnp.max(logits, axis=1, keepdims=True))
    pd = wide / jnp.sum(wide, axis=1, keepdims=True)
    p_dispatch[...] = pd
    tall = jnp.exp(logits - jnp.max(logits, axis=0, keepdims=True))
    pc = tall / jnp.sum(tall, axis=0, keepdims=True)
    p_combine[...] = pc
    shape = (n_expert, slots // n_expert, feature)
    slot_in = dot(pd.astype(BF), t, 1, 0).reshape(shape)
    d_slot_out = dot(pc.astype(BF), grad_out[0], 1, 0).reshape(shape)
    both = jnp.concatenate([slot_in, d_slot_out], axis=1).astype(BF)
    rows[...] = both.reshape(rows.shape)


def route(tokens, slot_params, grad_out, n_expert):
    _, length, feature = tokens.shape
    slots = slot_params.shape[0]
    rows = jax.ShapeDtypeStruct((2 * slots, feature), BF)
    probs = jax.ShapeDtypeStruct((slots, length), F32)
    return pl.pallas_call(
        functools.partial(route_kernel, n_expert),
        out_shape=(rows, probs, probs),
        compiler_params=params(60),
        name="route",
    )(tokens, slot_params, grad_out)


def sort_kernel(n_expert, resident, rows, first, second):
    n = rows.shape[0]
    out = dot(one_hot_rows(n, n_expert, resident), rows[...], 1, 0).astype(BF)
    half = out.reshape(2, *first.shape)
    first[...] = half[0]
    second[...] = half[1]


def sort_rows(rows, n_expert, resident):
    n, feature = rows.shape
    half = jax.ShapeDtypeStruct((resident // 2, n // resident, feature), BF)
    return pl.pallas_call(
        functools.partial(sort_kernel, n_expert, resident),
        out_shape=(half, half),
        compiler_params=params(),
        name="sort_rows",
    )(rows)


def after(values, others):
    return lax.optimization_barrier((tuple(values), tuple(others)))[0]


def gather(first, second):
    low1, high1, y1 = up(first, "first"), down(first, "first"), across(first, "first")
    low2, high2, y2 = up(second, "second"), down(second, "second"), across(second, "second")
    far1, far2 = up(low1, "first_on"), down(high2, "second_on")
    y_low1, y_high1 = up(y1, "first_y"), down(y1, "first_y")
    one = (first, low1, far1, high1, y1, y_low1, across(far1, "first_far"), y_high1)
    (y2,) = after((y2,), (far1,))
    y_low2, y_high2 = up(y2, "second_y"), down(y2, "second_y")
    two = (second, low2, far2, high2, y2, y_low2, across(far2, "second_far"), y_high2)
    return one, two


def assemble(refs, into):
    part = refs[0].shape[1] // 2
    for place, ref in enumerate(refs):
        for kind in range(2):
            into[kind, place * part : (place + 1) * part] = ref[0, kind * part : (kind + 1) * part]


def scatter_out(kind, total, refs):
    part = refs[0].shape[1] // 2
    for place, ref in enumerate(refs):
        ref[0, kind * part : (kind + 1) * part] = total[place * part : (place + 1) * part]


def expert_kernel(*refs):
    pieces, (w_in, w_out), (active, d_hidden) = refs[:8], refs[8:10], refs[10:12]
    partial, rows = refs[12:20], refs[20]
    assemble(pieces, rows)
    hidden = dot(w_in[0], rows[0], 1, 1)
    d_active = dot(w_out[0], rows[1], 1, 1)
    bell = 0.5 * (1.0 + lax.erf(hidden * inv_root_two))
    act = (hidden * bell).astype(BF)
    active[0] = act
    slope = bell + hidden * jnp.exp(-0.5 * hidden * hidden) * inv_root_tau
    dh = (d_active * slope).astype(BF)
    d_hidden[0] = dh
    scatter_out(0, dot(act, w_out[0], 0, 0).astype(BF), partial)
    scatter_out(1, dot(dh, w_in[0], 0, 0).astype(BF), partial)


def per_expert(*shape, base=0):
    return pl.BlockSpec((1, *shape), lambda e: (e + base, 0, 0))


def expert_call(pieces, w_in, w_out, base):
    _, hid, feature = w_in.shape
    count, block, _ = pieces[0].shape
    total = 4 * block
    work = count * hid * total * feature
    return pl.pallas_call(
        expert_kernel,
        grid=(count,),
        in_specs=[per_expert(block, feature)] * 8 + [per_expert(hid, feature, base=base)] * 2,
        out_specs=[per_expert(hid, total)] * 2 + [per_expert(block, feature)] * 8,
        out_shape=[jax.ShapeDtypeStruct((count, hid, total), BF)] * 2
        + [jax.ShapeDtypeStruct((count, block, feature), BF)] * 8,
        scratch_shapes=[pltpu.VMEM((2, total, feature), BF)],
        compiler_params=params(60),
        cost_estimate=pl.CostEstimate(flops=8 * work, bytes_accessed=12 * 2**20, transcendentals=0),
        name="expert",
    )(*pieces, w_in, w_out)


def weights_kernel(half, *refs):
    one, two = refs[:10], refs[10:20]
    grad_w_out, grad_w_in, rows = refs[20:]

    def work(pieces, active, d_hidden):
        assemble(pieces, rows)
        grad_w_out[0] = dot(active[0], rows[1], 1, 0).astype(BF)
        grad_w_in[0] = dot(d_hidden[0], rows[0], 1, 0).astype(BF)

    @pl.when(pl.program_id(0) < half)
    def _():
        work(one[:8], *one[8:])

    @pl.when(pl.program_id(0) >= half)
    def _():
        work(two[:8], *two[8:])


def weight_grads(one, two):
    half, hid, total = one[8].shape
    block, feature = one[0].shape[1:]

    def first(*shape):
        return pl.BlockSpec((1, *shape), lambda e: (jnp.minimum(e, half - 1), 0, 0))

    def second(*shape):
        return pl.BlockSpec((1, *shape), lambda e: (jnp.maximum(e - half, 0), 0, 0))

    in_specs = []
    for spec in (first, second):
        in_specs += [spec(block, feature)] * 8 + [spec(hid, total)] * 2
    out = jax.ShapeDtypeStruct((2 * half, hid, feature), BF)
    work = 2 * half * hid * total * feature
    return pl.pallas_call(
        functools.partial(weights_kernel, half),
        grid=(2 * half,),
        in_specs=in_specs,
        out_specs=[per_expert(hid, feature)] * 2,
        out_shape=[out, out],
        scratch_shapes=[pltpu.VMEM((2, total, feature), BF)],
        compiler_params=params(60),
        cost_estimate=pl.CostEstimate(flops=4 * work, bytes_accessed=20 * 2**20, transcendentals=0),
        name="weight_grads",
    )(*one, *two)


def add(*values):
    return sum(v.astype(F32) for v in values).astype(BF)


def reduce(parts, far_way, name):
    own, low, far, high, y, y_low, y_far, y_high = parts
    w = across(y_far, name + "_far")
    v_up, v_down = up(y_high, name + "_y"), down(y_low, name + "_y")
    near, last, other_way = (low, high, down) if far_way is up else (high, low, up)
    direct = other_way(near, name)
    chain = far_way(add(last, far_way(add(far, w), name + "_on")), name)
    return own, direct, chain, across(add(y, v_up, v_down), name)


def unsort_kernel(n_expert, n_first, *refs):
    out = refs[-1]
    half, block, feature = refs[0].shape
    n = 2 * half * block
    first = sum(ref[...].astype(F32) for ref in refs[:n_first])
    second = sum(ref[...].astype(F32) for ref in refs[n_first:-1])
    total = jnp.concatenate([first, second], axis=0).reshape(n, feature).astype(BF)
    out[...] = dot(one_hot_rows(n, n_expert, 2 * half), total, 0, 0).astype(BF)


def unsort_rows(first, second, n_expert):
    half, block, feature = first[0].shape
    return pl.pallas_call(
        functools.partial(unsort_kernel, n_expert, len(first)),
        out_shape=jax.ShapeDtypeStruct((2 * half * block, feature), BF),
        compiler_params=params(),
        name="unsort_rows",
    )(*first, *second)


def exchange(rows):
    return lax.all_to_all(rows, EXPERT, split_axis=0, concat_axis=0, tiled=True)


def logits_kernel(n_expert, tokens, grad_out, back, p_dispatch, p_combine, d_logits, local, d_slot):
    t = tokens[0]
    n, feature = back.shape
    wide = back[...].astype(F32).reshape(n_expert, n // n_expert, feature)
    split = n // n_expert // 2
    slot_out = wide[:, :split].reshape(n // 2, feature).astype(BF)
    d_slot_in = wide[:, split:].reshape(n // 2, feature).astype(BF)
    d_slot[...] = d_slot_in
    d_combine = dot(slot_out, grad_out[0], 1, 1)
    d_dispatch = dot(d_slot_in, t, 1, 1)
    pd, pc = p_dispatch[...], p_combine[...]
    grad = pd * (d_dispatch - jnp.sum(pd * d_dispatch, axis=1, keepdims=True)) + pc * (
        d_combine - jnp.sum(pc * d_combine, axis=0, keepdims=True)
    )
    dl = grad.astype(BF)
    d_logits[...] = dl
    local[...] = dot(dl, t, 1, 0)


def logits_back(tokens, grad_out, back, p_dispatch, p_combine, n_expert):
    slots = p_dispatch.shape[0]
    feature = back.shape[1]
    return pl.pallas_call(
        functools.partial(logits_kernel, n_expert),
        out_shape=(
            jax.ShapeDtypeStruct(p_dispatch.shape, BF),
            jax.ShapeDtypeStruct((slots, feature), F32),
            jax.ShapeDtypeStruct((slots, feature), BF),
        ),
        compiler_params=params(),
        name="logits_back",
    )(tokens, grad_out, back, p_dispatch, p_combine)


def tokens_kernel(p_dispatch, d_slot_in, d_logits, slot_params, grad_tokens):
    first = dot(p_dispatch[...].astype(BF), d_slot_in[...], 0, 0)
    second = dot(d_logits[...], slot_params[...], 0, 0)
    grad_tokens[0] = (first + second).astype(BF)


def tokens_back(p_dispatch, d_slot_in, d_logits, slot_params):
    slots, length = p_dispatch.shape
    feature = slot_params.shape[1]
    return pl.pallas_call(
        tokens_kernel,
        out_shape=jax.ShapeDtypeStruct((1, length, feature), BF),
        compiler_params=params(),
        name="tokens_back",
    )(p_dispatch, d_slot_in, d_logits, slot_params)


def sum_over_all(value):
    n = lax.axis_size(NAMES)
    rows, feature = value.shape
    terms = lax.all_to_all(value, NAMES, split_axis=0, concat_axis=0, tiled=True)
    mine = jnp.sum(terms.reshape(n, rows // n, feature), axis=0)
    copies = jnp.broadcast_to(mine[None], (n, rows // n, feature)).reshape(rows, feature)
    return lax.all_to_all(copies, NAMES, split_axis=0, concat_axis=0, tiled=True)


def split(outputs):
    return outputs[:2], outputs[2:]


def per_device(tokens, slot_params, expert_in, expert_out, grad_out):
    n_expert = lax.axis_size(EXPERT)
    resident = expert_in.shape[0]
    outgoing, p_dispatch, p_combine = route(tokens, slot_params, grad_out, n_expert)
    first, second = sort_rows(exchange(outgoing), n_expert, resident)
    one, two = gather(first, second)
    kept_one, partial_one = split(expert_call(one, expert_in, expert_out, 0))
    sums_one = reduce(partial_one, up, "sum_first")
    kept_two, partial_two = split(expert_call(two, expert_in, expert_out, resident // 2))
    sums_two = reduce(partial_two, down, "sum_second")
    grad_w_out, grad_w_in = weight_grads((*one, *kept_one), (*two, *kept_two))
    back = exchange(unsort_rows(sums_one, sums_two, n_expert))
    d_logits, local_params, d_slot_in = logits_back(
        tokens, grad_out, back, p_dispatch, p_combine, n_expert
    )
    grad_params = sum_over_all(local_params)
    grad_tokens = tokens_back(p_dispatch, d_slot_in, d_logits, slot_params)
    return (grad_tokens, grad_params, grad_w_in, grad_w_out)


def solution(mesh):
    parts = Mesh(mesh.devices.reshape(2, 4, 2, 2, 4), NAMES)
    image = P(NAMES, None, None)
    weight = P(EXPERT, GROUP, None)
    return jax.shard_map(
        per_device,
        mesh=parts,
        in_specs=(image, P(), weight, weight, image),
        out_specs=(image, P(), weight, weight),
        check_vma=False,
    )
```

time: 194 us -> 186 us (0.959)
  waiting for transfers between devices: 58.2 us -> 44.9 us
  local copies, waits for them, and re-layouts: 8.99 us -> 3.84 us
  Pallas kernels: 28.6 us -> 31.7 us
  blocking collectives: 65.2 us -> 68.2 us
  other arithmetic: 0.97 us -> 3.88 us
    ppermute x8 -> x10, waiting for transfers between devices: 17 us -> 28.3 us  [up(): return lax.ppermute(value, 'z', [(i, (i + 1) % 4) for i in range(4)])]
    all_to_all x1, waiting for transfers between devices: 13.7 us -> 3.94 us  [sum_over_all(): lax.all_to_all(copies, NAMES, split_axis=0, concat_axis=0, tiled=True)]
    ppermute x6 -> x8, waiting for transfers between devices: 13.2 us -> 4.49 us  [across(): return lax.ppermute(value, 'yl', SWAP)]
    ppermute x8 -> x10, waiting for transfers between devices: 14.3 us -> 8.14 us  [down(): return lax.ppermute(value, 'z', [(i, (i + 3) % 4) for i in range(4)])]
    unnamed x55 -> x45, local copies, waits for them, and re-layouts: 7.14 us -> 1.99 us
    all_to_all x2, blocking collectives: 46.9 us -> 49.9 us  [exchange(): return lax.all_to_all(rows, EXPERT, split_axis=0, concat_axis=0, tiled=True)]
    convert_element_type x5 -> x6, other arithmetic: 0.56 us -> 3.47 us  [add(): return sum((v.astype(F32) for v in values)).astype(BF)]
    ppermute x8 -> x10, starting transfers between devices: 2.05 us -> 4.78 us  [up(): return lax.ppermute(value, 'z', [(i, (i + 1) % 4) for i in range(4)])]
  transfers between devices with their start and end apart: 23 -> 29, of which waited for: 12 -> 12; matrix products, arithmetic and copies ran while one was open for 0% -> 2% of each run, Pallas kernels for 5% -> 14%
where the time goes in v3:
time: 186 us
  blocking collectives  68.2 us (37%)
  waiting for transfers between devices  44.9 us (24%)
  starting transfers between devices  32.4 us (17%)
  Pallas kernels  31.7 us (17%)
  other arithmetic  3.88 us (2%)
  local copies, waits for them, and re-layouts  3.84 us (2%)
    all_to_all x2, blocking collectives, exchange(): return lax.all_to_all(rows, EXPERT, split_axis=0, concat_axis=0, tiled=True)  49.9 us
    ppermute x10, waiting for transfers between devices, up(): return lax.ppermute(value, 'z', [(i, (i + 1) % 4) for i in range(4)])  28.3 us
    all_to_all x1, blocking collectives, sum_over_all(): lax.all_to_all(value, NAMES, split_axis=0, concat_axis=0, tiled=True)  18.3 us
    ppermute x10, starting transfers between devices, down(): return lax.ppermute(value, 'z', [(i, (i + 3) % 4) for i in range(4)])  17.9 us
    pallas_call x2, Pallas kernels, expert_call(): pl.pallas_call(expert_kernel, grid=(count,), in_specs=[per_expert(block,...  15.4 us
    pallas_call x1, Pallas kernels, weight_grads(): pl.pallas_call(functools.partial(weights_kernel, half), grid=(2 * half,),...  9.77 us
    ppermute x10, waiting for transfers between devices, down(): return lax.ppermute(value, 'z', [(i, (i + 3) % 4) for i in range(4)])  8.14 us
    ppermute x8, starting transfers between devices, across(): return lax.ppermute(value, 'yl', SWAP)  5.14 us
  transfers between devices with their start and end apart: 29, of which 12 were waited for; matrix products, arithmetic and copies ran while one was open for 2% of the time, Pallas kernels for 14%

profile of v3, /device:TPU:1, one launch (start us, length us, event | category | flops | bytes accessed | tf_op | source)
XLA Modules:
  0.0 185.9 jit_solution(9208210682888891016)
XLA Ops:
  0.6 3.3 %route.1 = (bf16[256,1280]{1,0:T(8,128)(2,1)}, f32[128,256]{1,0:T(8,128)}, f32[128,256]{1,0:T(8,128)}) custom-call(bf16[1,256,1280]{2,1,0:T(8,128)(2,1)} %tokens.3, bf16[128,1280]{1,0:T(8,128)(2,1)} %slot_params.3, bf16[1,256,1280]{2,1,0:T(8,128)(2,1)} %grad_out.3), custom_call_target="tpu_custom_call" | custom-call | tf_op jit(solution)/shard_map/route/pallas_call | solution.py:77
  3.9 21.6 %all_to_all.40 = bf16[16,16,1280]{2,1,0:T(8,128)(2,1)S(1)} all-to-all(bf16[16,16,1280]{2,1,0:T(8,128)(2,1)} %bitcast.13), channel_id=1, replica_groups=mesh['yh'=2,'x'=4,'c'=2,'yl'=2,'z'=4] {'yh','x','c'}, dimensions={0} | all-to-all | bytes 1310720 | tf_op jit(solution)/shard_map/all_to_all | solution.py:253
  26.0 1.7 collective-permute-start
  27.7 2.2 %collective-permute-start.15 = (bf16[2,64,1280]{2,1,0:T(8,128)(2,1)S(1)}, bf16[2,64,1280]{2,1,0:T(8,128)(2,1)S(1)}, u32[]{:S(2)}, u32[]{:S(2)}) collective-permute-start(bf16[2,64,1280]{2,1,0:T(8,128)(2,1)S(1)} %get-tuple-element.46.refs_0_.refs_10_), channel_id=1, source_target_pairs={{0,3},{1,0},{2,1},{3,2},{4,7},{5,4},{6,5},{7,6},{8,11},{9,8},{10,9... | collective-permute-start | bytes 983048 | tf_op jit(solution)/shard_map/second_down/ppermute | solution.py:38
  29.9 0.4 collective-permute-start.17
  30.3 7.3 %collective-permute-done.refs_1_ = bf16[2,64,1280]{2,1,0:T(8,128)(2,1)S(1)} collective-permute-done((bf16[2,64,1280]{2,1,0:T(8,128)(2,1)S(1)}, bf16[2,64,1280]{2,1,0:T(8,128)(2,1)S(1)}, u32[]{:S(2)}, u32[]{:S(2)}) %collective-permute-start) | collective-permute-done | bytes 327712 | tf_op jit(solution)/shard_map/first_up/ppermute | solution.py:33
  37.6 2.7 %collective-permute-start.16 = (bf16[2,64,1280]{2,1,0:T(8,128)(2,1)S(1)}, bf16[2,64,1280]{2,1,0:T(8,128)(2,1)S(1)}, u32[]{:S(2)}, u32[]{:S(2)}) collective-permute-start(bf16[2,64,1280]{2,1,0:T(8,128)(2,1)S(1)} %collective-permute-done.15.refs_3_.refs_13_), channel_id=1, source_target_pairs={{0,3},{1,0},{2,1},{3,2},{4,7},{5,4},{6,5},{7,6},{8,11},{9,8},{10,9... | collective-permute-start | bytes 983048 | tf_op jit(solution)/shard_map/second_on_down/ppermute | solution.py:38
  40.2 0.4 collective-permute-start.3
  40.6 6.4 %collective-permute-done.1.refs_2_ = bf16[2,64,1280]{2,1,0:T(8,128)(2,1)S(1)} collective-permute-done((bf16[2,64,1280]{2,1,0:T(8,128)(2,1)S(1)}, bf16[2,64,1280]{2,1,0:T(8,128)(2,1)S(1)}, u32[]{:S(2)}, u32[]{:S(2)}) %collective-permute-start.1) | collective-permute-done | bytes 327712 | tf_op jit(solution)/shard_map/first_on_up/ppermute | solution.py:33
  47.0 1.5 collective-permute-start.18
  48.5 0.4 collective-permute-start.19
  48.9 1.2 collective-permute-start.2
  50.1 3.9 %collective-permute-done.14.refs_1_.refs_11_ = bf16[2,64,1280]{2,1,0:T(8,128)(2,1)S(1)} collective-permute-done((bf16[2,64,1280]{2,1,0:T(8,128)(2,1)S(1)}, bf16[2,64,1280]{2,1,0:T(8,128)(2,1)S(1)}, u32[]{:S(2)}, u32[]{:S(2)}) %collective-permute-start.14) | collective-permute-done | bytes 327712 | tf_op jit(solution)/shard_map/second_up/ppermute | solution.py:33
  54.1 1.5 collective-permute-start.4
  55.5 5.5 %collective-permute-done.18.refs_5_.refs_15_ = bf16[2,64,1280]{2,1,0:T(8,128)(2,1)S(1)} collective-permute-done((bf16[2,64,1280]{2,1,0:T(8,128)(2,1)S(1)}, bf16[2,64,1280]{2,1,0:T(8,128)(2,1)S(1)}, u32[]{:S(2)}, u32[]{:S(2)}) %collective-permute-start.18) | collective-permute-done | bytes 327712 | tf_op jit(solution)/shard_map/second_y_up/ppermute | solution.py:33
  61.8 0.7 copy-done.21
  62.5 7.8 %expert.3 = (bf16[2,576,256]{2,1,0:T(8,128)(2,1)}, bf16[2,576,256]{2,1,0:T(8,128)(2,1)}, bf16[2,64,1280]{2,1,0:T(8,128)(2,1)}, bf16[2,64,1280]{2,1,0:T(8,128)(2,...) custom-call(bf16[2,64,1280]{2,1,0:T(8,128)(2,1)} %copy-done.7, ...), custom_call_target="tpu_custom_call" | custom-call | flops 3019898880 | bytes 12582912 | tf_op jit(solution)/shard_map/expert/pallas_call | solution.py:158
  70.4 2.7 %collective-permute-start.26 = (bf16[2,64,1280]{2,1,0:T(8,128)(2,1)}, bf16[2,64,1280]{2,1,0:T(8,128)(2,1)S(1)}, u32[]{:S(2)}, u32[]{:S(2)}) collective-permute-start(bf16[2,64,1280]{2,1,0:T(8,128)(2,1)} %get-tuple-element.55), channel_id=1, source_target_pairs={{0,3},{1,0},{2,1},{3,2},{4,7},{5,4},{6,5},{7,6},{8,11},{9,8},{10,9... | collective-permute-start | bytes 983048 | tf_op jit(solution)/shard_map/sum_second_y_down/ppermute | solution.py:38
  73.1 0.9 collective-permute-start.22
  74.0 7.7 %expert.2 = (bf16[2,576,256]{2,1,0:T(8,128)(2,1)}, bf16[2,576,256]{2,1,0:T(8,128)(2,1)}, bf16[2,64,1280]{2,1,0:T(8,128)(2,1)}, bf16[2,64,1280]{2,1,0:T(8,128)(2,...) custom-call(bf16[2,64,1280]{2,1,0:T(8,128)(2,1)} %copy-done.6, ...), custom_call_target="tpu_custom_call" | custom-call | flops 3019898880 | bytes 12582912 | tf_op jit(solution)/shard_map/expert/pallas_call | solution.py:158
  81.8 2.7 %collective-permute-start.7 = (bf16[2,64,1280]{2,1,0:T(8,128)(2,1)}, bf16[2,64,1280]{2,1,0:T(8,128)(2,1)S(1)}, u32[]{:S(2)}, u32[]{:S(2)}) collective-permute-start(bf16[2,64,1280]{2,1,0:T(8,128)(2,1)} %get-tuple-element.39), channel_id=1, source_target_pairs={{0,3},{1,0},{2,1},{3,2},{4,7},{5,4},{6,5},{7,6},{8,11},{9,8},{10,9... | collective-permute-start | bytes 983048 | tf_op jit(solution)/shard_map/sum_first_down/ppermute | solution.py:38
  84.5 0.7 collective-permute-start.8
  85.3 2.9 %collective-permute-start.12 = (bf16[2,64,1280]{2,1,0:T(8,128)(2,1)}, bf16[2,64,1280]{2,1,0:T(8,128)(2,1)S(1)}, u32[]{:S(2)}, u32[]{:S(2)}) collective-permute-start(bf16[2,64,1280]{2,1,0:T(8,128)(2,1)} %get-tuple-element.45), channel_id=1, source_target_pairs={{0,3},{1,0},{2,1},{3,2},{4,7},{5,4},{6,5},{7,6},{8,11},{9,8},{10,9... | collective-permute-start | bytes 983048 | tf_op jit(solution)/shard_map/sum_first_y_down/ppermute | solution.py:38
  88.3 2.6 %collective-permute-done.8 = bf16[2,64,1280]{2,1,0:T(8,128)(2,1)S(1)} collective-permute-done((bf16[2,64,1280]{2,1,0:T(8,128)(2,1)}, bf16[2,64,1280]{2,1,0:T(8,128)(2,1)S(1)}, u32[]{:S(2)}, u32[]{:S(2)}) %collective-permute-start.8) | collective-permute-done | bytes 327712 | tf_op jit(solution)/shard_map/sum_first_far_across/ppermute | solution.py:43
  90.9 1.1 add_convert_fusion.5
  92.0 0.5 collective-permute-done.11
  92.5 0.8 collective-permute-start.27
  93.3 1.3 collective-permute-done.12
  94.6 1.1 add_convert_fusion.3
  95.7 5.8 %collective-permute-done.23 = bf16[2,64,1280]{2,1,0:T(8,128)(2,1)S(1)} collective-permute-done((bf16[2,64,1280]{2,1,0:T(8,128)(2,1)S(1)}, bf16[2,64,1280]{2,1,0:T(8,128)(2,1)S(1)}, u32[]{:S(2)}, u32[]{:S(2)}) %collective-permute-start.23) | collective-permute-done | bytes 327712 | tf_op jit(solution)/shard_map/sum_second_on_down/ppermute | solution.py:38
  101.5 1.2 collective-permute-start.13
  102.9 3.5 %collective-permute-start.24 = (bf16[2,64,1280]{2,1,0:T(8,128)(2,1)S(1)}, bf16[2,64,1280]{2,1,0:T(8,128)(2,1)S(1)}, u32[]{:S(2)}, u32[]{:S(2)}) collective-permute-start(bf16[2,64,1280]{2,1,0:T(8,128)(2,1)S(1)} %add_convert_fusion.1), channel_id=1, source_target_pairs={{0,3},{1,0},{2,1},{3,2},{4,7},{5,4},{6,5},{7,6},{8,11},{9,8},{10,9... | collective-permute-start | bytes 983048 | tf_op jit(solution)/shard_map/sum_second_down/ppermute | solution.py:38
  106.3 1.0 add_convert_fusion.4
  107.5 1.9 %collective-permute-done.13.refs_3_ = bf16[2,64,1280]{2,1,0:T(8,128)(2,1)S(1)} collective-permute-done((bf16[2,64,1280]{2,1,0:T(8,128)(2,1)S(1)}, bf16[2,64,1280]{2,1,0:T(8,128)(2,1)S(1)}, u32[]{:S(2)}, u32[]{:S(2)}) %collective-permute-start.13) | collective-permute-done | bytes 327712 | tf_op jit(solution)/shard_map/sum_first_across/ppermute | solution.py:43
  109.4 1.0 collective-permute-done.24.refs_6_
  110.4 4.6 %collective-permute-done.10.refs_2_ = bf16[2,64,1280]{2,1,0:T(8,128)(2,1)S(1)} collective-permute-done((bf16[2,64,1280]{2,1,0:T(8,128)(2,1)S(1)}, bf16[2,64,1280]{2,1,0:T(8,128)(2,1)S(1)}, u32[]{:S(2)}, u32[]{:S(2)}) %collective-permute-start.10) | collective-permute-done | bytes 327712 | tf_op jit(solution)/shard_map/sum_first_up/ppermute | solution.py:33
  115.0 0.6 unsort_rows.1
  115.6 28.3 %all_to_all.41 = bf16[16,16,1280]{2,1,0:T(8,128)(2,1)S(1)} all-to-all(bf16[16,16,1280]{2,1,0:T(8,128)(2,1)S(1)} %bitcast.9), channel_id=1, replica_groups=mesh['yh'=2,'x'=4,'c'=2,'yl'=2,'z'=4] {'yh','x','c'}, dimensions={0} | all-to-all | bytes 1310720 | tf_op jit(solution)/shard_map/all_to_all | solution.py:253
  143.9 0.8 logits_back.1
  144.7 0.7 copy.9
  145.4 18.3 %all_to_all.42 = f32[128,1,1280]{2,1,0:T(1,128)S(1)} all-to-all(f32[128,1,1280]{2,1,0:T(1,128)S(1)} %copy.9), channel_id=1, replica_groups=mesh['yh'=2,'x'=4,'c'=2,'yl'=2,'z'=4] {'yh','x','c','yl','z'}, dimensions={0} | all-to-all | bytes 1310720 | tf_op jit(solution)/shard_map/all_to_all | solution.py:310
  163.7 0.4 reduce_sum.9
  164.1 1.2 reshape.28
  165.3 4.6 %all-to-all-start.3 = ((f32[128,1,1280]{2,1,0:T(1,128)}), f32[128,1,1280]{2,1,0:T(1,128)S(1)}, u32[]{:S(2)}, u32[]{:S(2)}) async-start(f32[128,1,1280]{2,1,0:T(1,128)} %reshape.28), calls=%async_computation.3 | async-start | bytes 1310720 | tf_op jit(solution)/shard_map/all_to_all | solution.py:313
  169.9 9.8 %weight_grads.1 = (bf16[4,576,1280]{2,1,0:T(8,128)(2,1)}, bf16[4,576,1280]{2,1,0:T(8,128)(2,1)}) custom-call(bf16[2,64,1280]{2,1,0:T(8,128)(2,1)} %copy-done.6, bf16[2,64,1280]{2,1,0:T(8,128)(2,1)} %copy-done.12, bf16[2,64,1280]{2,1,0:T(8,128)(2,1)} %copy-done.15, bf16[2,64,1280]{2,1,0:T(8,128)(2,1)} %collective-permute-done.2.refs_3_, ...), custom_call_target="tpu_custom_call" | custom-call | flops 3019898880 | bytes 20971520 | tf_op jit(solution)/shard_map/weight_grads/pallas_call | solution.py:205
  179.7 1.4 tokens_back.1
  181.0 3.9 %all-to-all-done.3 = f32[128,1,1280]{2,1,0:T(1,128)S(1)} async-done(((f32[128,1,1280]{2,1,0:T(1,128)}), f32[128,1,1280]{2,1,0:T(1,128)S(1)}, u32[]{:S(2)}, u32[]{:S(2)}) %all-to-all-start.3) | async-done | bytes 655392 | tf_op jit(solution)/shard_map/all_to_all | solution.py:313
  185.0 0.9 copy.12
  (75 shorter events, 1.6 us)
Async XLA Ops:
  26.0 35.5 %copy-start.7 = (bf16[2,64,1280]{2,1,0:T(8,128)(2,1)}, bf16[2,64,1280]{2,1,0:T(8,128)(2,1)S(1)}, u32[]{:S(2)}) copy-start(bf16[2,64,1280]{2,1,0:T(8,128)(2,1)S(1)} %get-tuple-element.46.refs_0_.refs_10_) | copy-start | bytes 983044
  26.0 44.3 %copy-start.6 = (bf16[2,64,1280]{2,1,0:T(8,128)(2,1)}, bf16[2,64,1280]{2,1,0:T(8,128)(2,1)S(1)}, u32[]{:S(2)}) copy-start(bf16[2,64,1280]{2,1,0:T(8,128)(2,1)S(1)} %get-tuple-element.37.refs_0_) | copy-start | bytes 983044
  26.0 11.6 %collective-permute-start = (bf16[2,64,1280]{2,1,0:T(8,128)(2,1)S(1)}, bf16[2,64,1280]{2,1,0:T(8,128)(2,1)S(1)}, u32[]{:S(2)}, u32[]{:S(2)}) collective-permute-start(bf16[2,64,1280]{2,1,0:T(8,128)(2,1)S(1)} %get-tuple-element.37.refs_0_), channel_id=1, source_target_pairs={{0,1},{1,2},{2,3},{3,0},{4,5},{5,6},{6,7},{7,4},{8,9},{9,10},{10,1... | collective-permute-start | bytes 983048 | tf_op jit(solution)/shard_map/first_up/ppermute | solution.py:33
  27.7 9.9 %collective-permute-start.15 = (bf16[2,64,1280]{2,1,0:T(8,128)(2,1)S(1)}, bf16[2,64,1280]{2,1,0:T(8,128)(2,1)S(1)}, u32[]{:S(2)}, u32[]{:S(2)}) collective-permute-start(bf16[2,64,1280]{2,1,0:T(8,128)(2,1)S(1)} %get-tuple-element.46.refs_0_.refs_10_), channel_id=1, source_target_pairs={{0,3},{1,0},{2,1},{3,2},{4,7},{5,4},{6,5},{7,6},{8,11},{9,8},{10,9... | collective-permute-start | bytes 983048 | tf_op jit(solution)/shard_map/second_down/ppermute | solution.py:38
  29.9 10.7 %collective-permute-start.17 = (bf16[2,64,1280]{2,1,0:T(8,128)(2,1)S(1)}, bf16[2,64,1280]{2,1,0:T(8,128)(2,1)S(1)}, u32[]{:S(2)}, u32[]{:S(2)}) collective-permute-start(bf16[2,64,1280]{2,1,0:T(8,128)(2,1)S(1)} %get-tuple-element.46.refs_0_.refs_10_), channel_id=1, source_target_pairs={{0,4},{4,0},{1,5},{5,1},{2,6},{6,2},{3,7},{7,3},{8,12},{12,8},{9,1... | collective-permute-start | bytes 983048 | tf_op jit(solution)/shard_map/second_across/ppermute | solution.py:43
  37.5 32.8 %copy-start.12 = (bf16[2,64,1280]{2,1,0:T(8,128)(2,1)}, bf16[2,64,1280]{2,1,0:T(8,128)(2,1)S(1)}, u32[]{:S(2)}) copy-start(bf16[2,64,1280]{2,1,0:T(8,128)(2,1)S(1)} %collective-permute-done.refs_1_) | copy-start | bytes 983044
  37.5 9.5 %collective-permute-start.1 = (bf16[2,64,1280]{2,1,0:T(8,128)(2,1)S(1)}, bf16[2,64,1280]{2,1,0:T(8,128)(2,1)S(1)}, u32[]{:S(2)}, u32[]{:S(2)}) collective-permute-start(bf16[2,64,1280]{2,1,0:T(8,128)(2,1)S(1)} %collective-permute-done.refs_1_), channel_id=1, source_target_pairs={{0,1},{1,2},{2,3},{3,0},{4,5},{5,6},{6,7},{7,4},{8,9},{9,10},{10,1... | collective-permute-start | bytes 983048 | tf_op jit(solution)/shard_map/first_on_up/ppermute | solution.py:33
  37.5 23.9 %copy-start.13 = (bf16[2,64,1280]{2,1,0:T(8,128)(2,1)}, bf16[2,64,1280]{2,1,0:T(8,128)(2,1)S(1)}, u32[]{:S(2)}) copy-start(bf16[2,64,1280]{2,1,0:T(8,128)(2,1)S(1)} %collective-permute-done.15.refs_3_.refs_13_) | copy-start | bytes 983044
  37.6 10.9 %collective-permute-start.16 = (bf16[2,64,1280]{2,1,0:T(8,128)(2,1)S(1)}, bf16[2,64,1280]{2,1,0:T(8,128)(2,1)S(1)}, u32[]{:S(2)}, u32[]{:S(2)}) collective-permute-start(bf16[2,64,1280]{2,1,0:T(8,128)(2,1)S(1)} %collective-permute-done.15.refs_3_.refs_13_), channel_id=1, source_target_pairs={{0,3},{1,0},{2,1},{3,2},{4,7},{5,4},{6,5},{7,6},{8,11},{9,8},{10,9... | collective-permute-start | bytes 983048 | tf_op jit(solution)/shard_map/second_on_down/ppermute | solution.py:38
  40.2 8.7 %collective-permute-start.3 = (bf16[2,64,1280]{2,1,0:T(8,128)(2,1)S(1)}, bf16[2,64,1280]{2,1,0:T(8,128)(2,1)S(1)}, u32[]{:S(2)}, u32[]{:S(2)}) collective-permute-start(bf16[2,64,1280]{2,1,0:T(8,128)(2,1)S(1)} %get-tuple-element.37.refs_0_), channel_id=1, source_target_pairs={{0,4},{4,0},{1,5},{5,1},{2,6},{6,2},{3,7},{7,3},{8,12},{12,8},{9,1... | collective-permute-start | bytes 983048 | tf_op jit(solution)/shard_map/first_across/ppermute | solution.py:43
  40.6 13.4 %collective-permute-start.14 = (bf16[2,64,1280]{2,1,0:T(8,128)(2,1)S(1)}, bf16[2,64,1280]{2,1,0:T(8,128)(2,1)S(1)}, u32[]{:S(2)}, u32[]{:S(2)}) collective-permute-start(bf16[2,64,1280]{2,1,0:T(8,128)(2,1)S(1)} %get-tuple-element.46.refs_0_.refs_10_), channel_id=1, source_target_pairs={{0,1},{1,2},{2,3},{3,0},{4,5},{5,6},{6,7},{7,4},{8,9},{9,10},{10,1... | collective-permute-start | bytes 983048 | tf_op jit(solution)/shard_map/second_up/ppermute | solution.py:33
  40.6 20.9 %copy-start.14 = (bf16[2,64,1280]{2,1,0:T(8,128)(2,1)}, bf16[2,64,1280]{2,1,0:T(8,128)(2,1)S(1)}, u32[]{:S(2)}) copy-start(bf16[2,64,1280]{2,1,0:T(8,128)(2,1)S(1)} %collective-permute-done.17.refs_4_.refs_14_) | copy-start | bytes 983044
  47.0 23.3 %copy-start.15 = (bf16[2,64,1280]{2,1,0:T(8,128)(2,1)}, bf16[2,64,1280]{2,1,0:T(8,128)(2,1)S(1)}, u32[]{:S(2)}) copy-start(bf16[2,64,1280]{2,1,0:T(8,128)(2,1)S(1)} %collective-permute-done.1.refs_2_) | copy-start | bytes 983044
  47.0 7.0 %collective-permute-start.20 = (bf16[2,64,1280]{2,1,0:T(8,128)(2,1)S(1)}, bf16[2,64,1280]{2,1,0:T(8,128)(2,1)S(1)}, u32[]{:S(2)}, u32[]{:S(2)}) collective-permute-start(bf16[2,64,1280]{2,1,0:T(8,128)(2,1)S(1)} %collective-permute-done.17.refs_4_.refs_14_), channel_id=1, source_target_pairs={{0,3},{1,0},{2,1},{3,2},{4,7},{5,4},{6,5},{7,6},{8,11},{9,8},{10,9... | collective-permute-start | bytes 983048 | tf_op jit(solution)/shard_map/second_y_down/ppermute | solution.py:38
  47.0 14.0 %collective-permute-start.18 = (bf16[2,64,1280]{2,1,0:T(8,128)(2,1)S(1)}, bf16[2,64,1280]{2,1,0:T(8,128)(2,1)S(1)}, u32[]{:S(2)}, u32[]{:S(2)}) collective-permute-start(bf16[2,64,1280]{2,1,0:T(8,128)(2,1)S(1)} %collective-permute-done.17.refs_4_.refs_14_), channel_id=1, source_target_pairs={{0,1},{1,2},{2,3},{3,0},{4,5},{5,6},{6,7},{7,4},{8,9},{9,10},{10,1... | collective-permute-start | bytes 983048 | tf_op jit(solution)/shard_map/second_y_up/ppermute | solution.py:33
  48.5 13.0 %copy-start.16 = (bf16[2,64,1280]{2,1,0:T(8,128)(2,1)}, bf16[2,64,1280]{2,1,0:T(8,128)(2,1)S(1)}, u32[]{:S(2)}) copy-start(bf16[2,64,1280]{2,1,0:T(8,128)(2,1)S(1)} %collective-permute-done.16.refs_2_.refs_12_) | copy-start | bytes 983044
  48.5 13.0 %collective-permute-start.19 = (bf16[2,64,1280]{2,1,0:T(8,128)(2,1)S(1)}, bf16[2,64,1280]{2,1,0:T(8,128)(2,1)S(1)}, u32[]{:S(2)}, u32[]{:S(2)}) collective-permute-start(bf16[2,64,1280]{2,1,0:T(8,128)(2,1)S(1)} %collective-permute-done.16.refs_2_.refs_12_), channel_id=1, source_target_pairs={{0,4},{4,0},{1,5},{5,1},{2,6},{6,2},{3,7},{7,3},{8,12},{12,8},{9,1... | collective-permute-start | bytes 983048 | tf_op jit(solution)/shard_map/second_far_across/ppermute | solution.py:43
  48.9 21.4 %copy-start.17 = (bf16[2,64,1280]{2,1,0:T(8,128)(2,1)}, bf16[2,64,1280]{2,1,0:T(8,128)(2,1)S(1)}, u32[]{:S(2)}) copy-start(bf16[2,64,1280]{2,1,0:T(8,128)(2,1)S(1)} %collective-permute-done.3.refs_4_) | copy-start | bytes 983044
  48.9 21.5 %collective-permute-start.2 = (bf16[2,64,1280]{2,1,0:T(8,128)(2,1)S(1)}, bf16[2,64,1280]{2,1,0:T(8,128)(2,1)}, u32[]{:S(2)}, u32[]{:S(2)}) collective-permute-start(bf16[2,64,1280]{2,1,0:T(8,128)(2,1)S(1)} %get-tuple-element.37.refs_0_), channel_id=1, source_target_pairs={{0,3},{1,0},{2,1},{3,2},{4,7},{5,4},{6,5},{7,6},{8,11},{9,8},{10,9... | collective-permute-start | bytes 983048 | tf_op jit(solution)/shard_map/first_down/ppermute | solution.py:38
  54.0 7.5 %copy-start.18 = (bf16[2,64,1280]{2,1,0:T(8,128)(2,1)}, bf16[2,64,1280]{2,1,0:T(8,128)(2,1)S(1)}, u32[]{:S(2)}) copy-start(bf16[2,64,1280]{2,1,0:T(8,128)(2,1)S(1)} %collective-permute-done.14.refs_1_.refs_11_) | copy-start | bytes 983044
  54.0 19.0 %collective-permute-start.6 = (bf16[2,64,1280]{2,1,0:T(8,128)(2,1)S(1)}, bf16[2,64,1280]{2,1,0:T(8,128)(2,1)}, u32[]{:S(2)}, u32[]{:S(2)}) collective-permute-start(bf16[2,64,1280]{2,1,0:T(8,128)(2,1)S(1)} %collective-permute-done.3.refs_4_), channel_id=1, source_target_pairs={{0,3},{1,0},{2,1},{3,2},{4,7},{5,4},{6,5},{7,6},{8,11},{9,8},{10,9... | collective-permute-start | bytes 983048 | tf_op jit(solution)/shard_map/first_y_down/ppermute | solution.py:38
  54.1 19.0 %collective-permute-start.4 = (bf16[2,64,1280]{2,1,0:T(8,128)(2,1)S(1)}, bf16[2,64,1280]{2,1,0:T(8,128)(2,1)}, u32[]{:S(2)}, u32[]{:S(2)}) collective-permute-start(bf16[2,64,1280]{2,1,0:T(8,128)(2,1)S(1)} %collective-permute-done.3.refs_4_), channel_id=1, source_target_pairs={{0,1},{1,2},{2,3},{3,0},{4,5},{5,6},{6,7},{7,4},{8,9},{9,10},{10,1... | collective-permute-start | bytes 983048 | tf_op jit(solution)/shard_map/first_y_up/ppermute | solution.py:33
  61.1 12.9 %collective-permute-start.5 = (bf16[2,64,1280]{2,1,0:T(8,128)(2,1)S(1)}, bf16[2,64,1280]{2,1,0:T(8,128)(2,1)}, u32[]{:S(2)}, u32[]{:S(2)}) collective-permute-start(bf16[2,64,1280]{2,1,0:T(8,128)(2,1)S(1)} %collective-permute-done.1.refs_2_), channel_id=1, source_target_pairs={{0,4},{4,0},{1,5},{5,1},{2,6},{6,2},{3,7},{7,3},{8,12},{12,8},{9,1... | collective-permute-start | bytes 983048 | tf_op jit(solution)/shard_map/first_far_across/ppermute | solution.py:43
  70.3 14.1 %collective-permute-start.25 = (bf16[2,64,1280]{2,1,0:T(8,128)(2,1)}, bf16[2,64,1280]{2,1,0:T(8,128)(2,1)S(1)}, u32[]{:S(2)}, u32[]{:S(2)}) collective-permute-start(bf16[2,64,1280]{2,1,0:T(8,128)(2,1)} %get-tuple-element.54), channel_id=1, source_target_pairs={{0,1},{1,2},{2,3},{3,0},{4,5},{5,6},{6,7},{7,4},{8,9},{9,10},{10,1... | collective-permute-start | bytes 983048 | tf_op jit(solution)/shard_map/sum_second_y_up/ppermute | solution.py:33
  70.4 14.7 %collective-permute-start.26 = (bf16[2,64,1280]{2,1,0:T(8,128)(2,1)}, bf16[2,64,1280]{2,1,0:T(8,128)(2,1)S(1)}, u32[]{:S(2)}, u32[]{:S(2)}) collective-permute-start(bf16[2,64,1280]{2,1,0:T(8,128)(2,1)} %get-tuple-element.55), channel_id=1, source_target_pairs={{0,3},{1,0},{2,1},{3,2},{4,7},{5,4},{6,5},{7,6},{8,11},{9,8},{10,9... | collective-permute-start | bytes 983048 | tf_op jit(solution)/shard_map/sum_second_y_down/ppermute | solution.py:38
  73.1 34.3 %collective-permute-start.21 = (bf16[2,64,1280]{2,1,0:T(8,128)(2,1)}, bf16[2,64,1280]{2,1,0:T(8,128)(2,1)S(1)}, u32[]{:S(2)}, u32[]{:S(2)}) collective-permute-start(bf16[2,64,1280]{2,1,0:T(8,128)(2,1)} %get-tuple-element.49), channel_id=1, source_target_pairs={{0,1},{1,2},{2,3},{3,0},{4,5},{5,6},{6,7},{7,4},{8,9},{9,10},{10,1... | collective-permute-start | bytes 983048 | tf_op jit(solution)/shard_map/sum_second_up/ppermute | solution.py:33
  73.1 12.1 %copy-start.9 = (bf16[2,64,1280]{2,1,0:T(8,128)(2,1)S(1)}, bf16[2,64,1280]{2,1,0:T(8,128)(2,1)}, u32[]{:S(2)}) copy-start(bf16[2,64,1280]{2,1,0:T(8,128)(2,1)} %get-tuple-element.53) | copy-start | bytes 983044
  73.1 15.1 %copy-start.11 = (bf16[2,64,1280]{2,1,0:T(8,128)(2,1)S(1)}, bf16[2,64,1280]{2,1,0:T(8,128)(2,1)}, u32[]{:S(2)}) copy-start(bf16[2,64,1280]{2,1,0:T(8,128)(2,1)} %get-tuple-element.51) | copy-start | bytes 983044
  73.1 29.6 %copy-start.10 = (bf16[2,64,1280]{2,1,0:T(8,128)(2,1)S(1)}, bf16[2,64,1280]{2,1,0:T(8,128)(2,1)}, u32[]{:S(2)}) copy-start(bf16[2,64,1280]{2,1,0:T(8,128)(2,1)} %get-tuple-element.50) | copy-start | bytes 983044
  73.1 12.2 %collective-permute-start.22 = (bf16[2,64,1280]{2,1,0:T(8,128)(2,1)}, bf16[2,64,1280]{2,1,0:T(8,128)(2,1)S(1)}, u32[]{:S(2)}, u32[]{:S(2)}) collective-permute-start(bf16[2,64,1280]{2,1,0:T(8,128)(2,1)} %get-tuple-element.52), channel_id=1, source_target_pairs={{0,4},{4,0},{1,5},{5,1},{2,6},{6,2},{3,7},{7,3},{8,12},{12,8},{9,1... | collective-permute-start | bytes 983048 | tf_op jit(solution)/shard_map/sum_second_far_across/ppermute | solution.py:43
  81.7 33.3 %copy-start.4 = (bf16[2,64,1280]{2,1,0:T(8,128)(2,1)S(1)}, bf16[2,64,1280]{2,1,0:T(8,128)(2,1)}, u32[]{:S(2)}) copy-start(bf16[2,64,1280]{2,1,0:T(8,128)(2,1)} %get-tuple-element.48.refs_4_) | copy-start | bytes 983044
  81.7 33.3 %copy-start.5 = (bf16[2,64,1280]{2,1,0:T(8,128)(2,1)S(1)}, bf16[2,64,1280]{2,1,0:T(8,128)(2,1)}, u32[]{:S(2)}) copy-start(bf16[2,64,1280]{2,1,0:T(8,128)(2,1)} %get-tuple-element.38.refs_0_) | copy-start | bytes 983044
  81.7 62.2 %copy-start = (bf16[1,256,1280]{2,1,0:T(8,128)(2,1)S(1)}, bf16[1,256,1280]{2,1,0:T(8,128)(2,1)}, u32[]{:S(2)}) copy-start(bf16[1,256,1280]{2,1,0:T(8,128)(2,1)} %tokens.3) | copy-start | bytes 1966084
  81.7 62.2 %copy-start.1 = (bf16[1,256,1280]{2,1,0:T(8,128)(2,1)S(1)}, bf16[1,256,1280]{2,1,0:T(8,128)(2,1)}, u32[]{:S(2)}) copy-start(bf16[1,256,1280]{2,1,0:T(8,128)(2,1)} %grad_out.3) | copy-start | bytes 1966084
  81.7 62.2 %copy-start.3 = (f32[128,256]{1,0:T(8,128)S(1)}, f32[128,256]{1,0:T(8,128)}, u32[]{:S(2)}) copy-start(f32[128,256]{1,0:T(8,128)} %get-tuple-element.35.p_dispatch) | copy-start | bytes 393220
  81.7 62.2 %copy-start.8 = (f32[128,256]{1,0:T(8,128)S(1)}, f32[128,256]{1,0:T(8,128)}, u32[]{:S(2)}) copy-start(f32[128,256]{1,0:T(8,128)} %get-tuple-element.56.p_combine) | copy-start | bytes 393220
  81.8 25.7 %collective-permute-start.7 = (bf16[2,64,1280]{2,1,0:T(8,128)(2,1)}, bf16[2,64,1280]{2,1,0:T(8,128)(2,1)S(1)}, u32[]{:S(2)}, u32[]{:S(2)}) collective-permute-start(bf16[2,64,1280]{2,1,0:T(8,128)(2,1)} %get-tuple-element.39), channel_id=1, source_target_pairs={{0,3},{1,0},{2,1},{3,2},{4,7},{5,4},{6,5},{7,6},{8,11},{9,8},{10,9... | collective-permute-start | bytes 983048 | tf_op jit(solution)/shard_map/sum_first_down/ppermute | solution.py:38
  84.5 6.4 %collective-permute-start.8 = (bf16[2,64,1280]{2,1,0:T(8,128)(2,1)}, bf16[2,64,1280]{2,1,0:T(8,128)(2,1)S(1)}, u32[]{:S(2)}, u32[]{:S(2)}) collective-permute-start(bf16[2,64,1280]{2,1,0:T(8,128)(2,1)} %get-tuple-element.42), channel_id=1, source_target_pairs={{0,4},{4,0},{1,5},{5,1},{2,6},{6,2},{3,7},{7,3},{8,12},{12,8},{9,1... | collective-permute-start | bytes 983048 | tf_op jit(solution)/shard_map/sum_first_far_across/ppermute | solution.py:43
  85.2 7.3 %collective-permute-start.11 = (bf16[2,64,1280]{2,1,0:T(8,128)(2,1)}, bf16[2,64,1280]{2,1,0:T(8,128)(2,1)S(1)}, u32[]{:S(2)}, u32[]{:S(2)}) collective-permute-start(bf16[2,64,1280]{2,1,0:T(8,128)(2,1)} %get-tuple-element.44), channel_id=1, source_target_pairs={{0,1},{1,2},{2,3},{3,0},{4,5},{5,6},{6,7},{7,4},{8,9},{9,10},{10,1... | collective-permute-start | bytes 983048 | tf_op jit(solution)/shard_map/sum_first_y_up/ppermute | solution.py:33
  85.3 9.3 %collective-permute-start.12 = (bf16[2,64,1280]{2,1,0:T(8,128)(2,1)}, bf16[2,64,1280]{2,1,0:T(8,128)(2,1)S(1)}, u32[]{:S(2)}, u32[]{:S(2)}) collective-permute-start(bf16[2,64,1280]{2,1,0:T(8,128)(2,1)} %get-tuple-element.45), channel_id=1, source_target_pairs={{0,3},{1,0},{2,1},{3,2},{4,7},{5,4},{6,5},{7,6},{8,11},{9,8},{10,9... | collective-permute-start | bytes 983048 | tf_op jit(solution)/shard_map/sum_first_y_down/ppermute | solution.py:38
  90.9 10.6 %collective-permute-start.23 = (bf16[2,64,1280]{2,1,0:T(8,128)(2,1)S(1)}, bf16[2,64,1280]{2,1,0:T(8,128)(2,1)S(1)}, u32[]{:S(2)}, u32[]{:S(2)}) collective-permute-start(bf16[2,64,1280]{2,1,0:T(8,128)(2,1)S(1)} %add_convert_fusion.2), channel_id=1, source_target_pairs={{0,3},{1,0},{2,1},{3,2},{4,7},{5,4},{6,5},{7,6},{8,11},{9,8},{10,9... | collective-permute-start | bytes 983048 | tf_op jit(solution)/shard_map/sum_second_on_down/ppermute | solution.py:38
  92.5 15.0 %collective-permute-start.27 = (bf16[2,64,1280]{2,1,0:T(8,128)(2,1)S(1)}, bf16[2,64,1280]{2,1,0:T(8,128)(2,1)S(1)}, u32[]{:S(2)}, u32[]{:S(2)}) collective-permute-start(bf16[2,64,1280]{2,1,0:T(8,128)(2,1)S(1)} %add_convert_fusion), channel_id=1, source_target_pairs={{0,4},{4,0},{1,5},{5,1},{2,6},{6,2},{3,7},{7,3},{8,12},{12,8},{9,1... | collective-permute-start | bytes 983048 | tf_op jit(solution)/shard_map/sum_second_across/ppermute | solution.py:43
  94.6 8.2 %collective-permute-start.9 = (bf16[2,64,1280]{2,1,0:T(8,128)(2,1)S(1)}, bf16[2,64,1280]{2,1,0:T(8,128)(2,1)S(1)}, u32[]{:S(2)}, u32[]{:S(2)}) collective-permute-start(bf16[2,64,1280]{2,1,0:T(8,128)(2,1)S(1)} %add_convert_fusion.5), channel_id=1, source_target_pairs={{0,1},{1,2},{2,3},{3,0},{4,5},{5,6},{6,7},{7,4},{8,9},{9,10},{10,1... | collective-permute-start | bytes 983048 | tf_op jit(solution)/shard_map/sum_first_on_up/ppermute | solution.py:33
  101.5 7.8 %collective-permute-start.13 = (bf16[2,64,1280]{2,1,0:T(8,128)(2,1)S(1)}, bf16[2,64,1280]{2,1,0:T(8,128)(2,1)S(1)}, u32[]{:S(2)}, u32[]{:S(2)}) collective-permute-start(bf16[2,64,1280]{2,1,0:T(8,128)(2,1)S(1)} %add_convert_fusion.3), channel_id=1, source_target_pairs={{0,4},{4,0},{1,5},{5,1},{2,6},{6,2},{3,7},{7,3},{8,12},{12,8},{9,1... | collective-permute-start | bytes 983048 | tf_op jit(solution)/shard_map/sum_first_across/ppermute | solution.py:43
  102.9 7.5 %collective-permute-start.24 = (bf16[2,64,1280]{2,1,0:T(8,128)(2,1)S(1)}, bf16[2,64,1280]{2,1,0:T(8,128)(2,1)S(1)}, u32[]{:S(2)}, u32[]{:S(2)}) collective-permute-start(bf16[2,64,1280]{2,1,0:T(8,128)(2,1)S(1)} %add_convert_fusion.1), channel_id=1, source_target_pairs={{0,3},{1,0},{2,1},{3,2},{4,7},{5,4},{6,5},{7,6},{8,11},{9,8},{10,9... | collective-permute-start | bytes 983048 | tf_op jit(solution)/shard_map/sum_second_down/ppermute | solution.py:38
  107.4 7.6 %collective-permute-start.10 = (bf16[2,64,1280]{2,1,0:T(8,128)(2,1)S(1)}, bf16[2,64,1280]{2,1,0:T(8,128)(2,1)S(1)}, u32[]{:S(2)}, u32[]{:S(2)}) collective-permute-start(bf16[2,64,1280]{2,1,0:T(8,128)(2,1)S(1)} %add_convert_fusion.4), channel_id=1, source_target_pairs={{0,1},{1,2},{2,3},{3,0},{4,5},{5,6},{6,7},{7,4},{8,9},{9,10},{10,1... | collective-permute-start | bytes 983048 | tf_op jit(solution)/shard_map/sum_first_up/ppermute | solution.py:33
  165.3 19.7 %all-to-all-start.3 = ((f32[128,1,1280]{2,1,0:T(1,128)}), f32[128,1,1280]{2,1,0:T(1,128)S(1)}, u32[]{:S(2)}, u32[]{:S(2)}) async-start(f32[128,1,1280]{2,1,0:T(1,128)} %reshape.28), calls=%async_computation.3 | async-start | bytes 1310720 | tf_op jit(solution)/shard_map/all_to_all | solution.py:313
  169.9 9.8 %copy-start.2 = (bf16[128,1280]{1,0:T(8,128)(2,1)S(1)}, bf16[128,1280]{1,0:T(8,128)(2,1)}, u32[]{:S(2)}) copy-start(bf16[128,1280]{1,0:T(8,128)(2,1)} %slot_params.3) | copy-start | bytes 983044
  (3 other events, 8.9 us)

commit v4 on v3

--- a/solution.py
+++ b/solution.py
@@ -105,16 +105,41 @@
     return lax.optimization_barrier((tuple(values), tuple(others)))[0]
 
 
-def gather(first, second):
+def stage_kernel(w_in, w_out, near_in, near_out, sems):
+    copies = [
+        pltpu.make_async_copy(w_in, near_in, sems.at[0]),
+        pltpu.make_async_copy(w_out, near_out, sems.at[1]),
+    ]
+    for copy in copies:
+        copy.start()
+    for copy in copies:
+        copy.wait()
+
+
+def stage(w_in, w_out):
+    return pl.pallas_call(
+        stage_kernel,
+        in_specs=[pl.BlockSpec(memory_space=pltpu.HBM)] * 2,
+        out_specs=[pl.BlockSpec(memory_space=pl.ANY)] * 2,
+        out_shape=[jax.ShapeDtypeStruct(w.shape, w.dtype) for w in (w_in, w_out)],
+        scratch_shapes=[pltpu.SemaphoreType.DMA((2,))],
+        compiler_params=params(40),
+        name="stage",
+    )(w_in, w_out)
+
+
+def gather(first, second, w_in, w_out):
     low1, high1, y1 = up(first, "first"), down(first, "first"), across(first, "first")
     low2, high2, y2 = up(second, "second"), down(second, "second"), across(second, "second")
     far1, far2 = up(low1, "first_on"), down(high2, "second_on")
+    weights = stage(*after((w_in, w_out), (low1,)))
     y_low1, y_high1 = up(y1, "first_y"), down(y1, "first_y")
-    one = (first, low1, far1, high1, y1, y_low1, across(far1, "first_far"), y_high1)
+    (sent,) = after((far1,), weights)
+    one = (first, low1, far1, high1, y1, y_low1, across(sent, "first_far"), y_high1)
     (y2,) = after((y2,), (far1,))
     y_low2, y_high2 = up(y2, "second_y"), down(y2, "second_y")
     two = (second, low2, far2, high2, y2, y_low2, across(far2, "second_far"), y_high2)
-    return one, two
+    return one, two, weights
 
 
 def assemble(refs, into):
@@ -163,7 +188,7 @@
         out_shape=[jax.ShapeDtypeStruct((count, hid, total), BF)] * 2
         + [jax.ShapeDtypeStruct((count, block, feature), BF)] * 8,
         scratch_shapes=[pltpu.VMEM((2, total, feature), BF)],
-        compiler_params=params(60),
+        compiler_params=params(24),
         cost_estimate=pl.CostEstimate(flops=8 * work, bytes_accessed=12 * 2**20, transcendentals=0),
         name="expert",
     )(*pieces, w_in, w_out)
@@ -322,10 +347,10 @@
     resident = expert_in.shape[0]
     outgoing, p_dispatch, p_combine = route(tokens, slot_params, grad_out, n_expert)
     first, second = sort_rows(exchange(outgoing), n_expert, resident)
-    one, two = gather(first, second)
-    kept_one, partial_one = split(expert_call(one, expert_in, expert_out, 0))
+    one, two, weights = gather(first, second, expert_in, expert_out)
+    kept_one, partial_one = split(expert_call(one, *weights, 0))
     sums_one = reduce(partial_one, up, "sum_first")
-    kept_two, partial_two = split(expert_call(two, expert_in, expert_out, resident // 2))
+    kept_two, partial_two = split(expert_call(two, *weights, resident // 2))
     sums_two = reduce(partial_two, down, "sum_second")
     grad_w_out, grad_w_in = weight_grads((*one, *kept_one), (*two, *kept_two))
     back = exchange(unsort_rows(sums_one, sums_two, n_expert))

time: 186 us -> 180 us (0.968)
  waiting for transfers between devices: 44.9 us -> 40.1 us
  starting transfers between devices: 32.4 us -> 37.1 us
  other arithmetic: 3.88 us -> 0.97 us
  Pallas kernels: 31.7 us -> 29.3 us
    ppermute x10, waiting for transfers between devices: 28.3 us -> 16.4 us  [up(): return lax.ppermute(value, 'z', [(i, (i + 1) % 4) for i in range(4)])]
    pallas_call x2, Pallas kernels: 15.4 us -> 8.67 us  [expert_call(): pl.pallas_call(expert_kernel, grid=(count,), in_specs=[per_expert(block,...]
    pallas_call x0 -> x1, Pallas kernels: none -> 4.42 us  [stage(): pl.pallas_call(stage_kernel, in_specs=[pl.BlockSpec(memory_space=pltpu.HB...]
    ppermute x10, waiting for transfers between devices: 8.14 us -> 12.4 us  [down(): return lax.ppermute(value, 'z', [(i, (i + 3) % 4) for i in range(4)])]
    all_to_all x2, blocking collectives: 49.9 us -> 46.6 us  [exchange(): return lax.all_to_all(rows, EXPERT, split_axis=0, concat_axis=0, tiled=True)]
    ppermute x10, starting transfers between devices: 17.9 us -> 20.9 us  [down(): return lax.ppermute(value, 'z', [(i, (i + 3) % 4) for i in range(4)])]
    convert_element_type x6, other arithmetic: 3.47 us -> 0.55 us  [add(): return sum((v.astype(F32) for v in values)).astype(BF)]
    ppermute x8, waiting for transfers between devices: 4.49 us -> 7.37 us  [across(): return lax.ppermute(value, 'yl', SWAP)]
  transfers between devices with their start and end apart: 29 -> 29, of which waited for: 12 -> 11; matrix products, arithmetic and copies ran while one was open for 2% -> 0% of each run, Pallas kernels for 14% -> 14%
where the time goes in v4:
time: 180 us; the launch traced here: 179 us
  blocking collectives  67 us (37%)
  waiting for transfers between devices  40.1 us (22%)
  starting transfers between devices  37.1 us (21%)
  Pallas kernels  29.3 us (16%)
  local copies, waits for them, and re-layouts  3.64 us (2%)
    all_to_all x2, blocking collectives, exchange(): return lax.all_to_all(rows, EXPERT, split_axis=0, concat_axis=0, tiled=True)  46.6 us
    ppermute x10, starting transfers between devices, down(): return lax.ppermute(value, 'z', [(i, (i + 3) % 4) for i in range(4)])  20.9 us
    all_to_all x1, blocking collectives, sum_over_all(): lax.all_to_all(value, NAMES, split_axis=0, concat_axis=0, tiled=True)  20.4 us
    ppermute x10, waiting for transfers between devices, up(): return lax.ppermute(value, 'z', [(i, (i + 1) % 4) for i in range(4)])  16.4 us
    ppermute x10, waiting for transfers between devices, down(): return lax.ppermute(value, 'z', [(i, (i + 3) % 4) for i in range(4)])  12.4 us
    pallas_call x1, Pallas kernels, weight_grads(): pl.pallas_call(functools.partial(weights_kernel, half), grid=(2 * half,),...  9.77 us
    pallas_call x2, Pallas kernels, expert_call(): pl.pallas_call(expert_kernel, grid=(count,), in_specs=[per_expert(block,...  8.67 us
    ppermute x8, waiting for transfers between devices, across(): return lax.ppermute(value, 'yl', SWAP)  7.37 us
  transfers between devices with their start and end apart: 29, of which 11 were waited for; matrix products, arithmetic and copies ran while one was open for 0% of the time, Pallas kernels for 14%

profile of v4, /device:TPU:1, one launch (start us, length us, event | category | flops | bytes accessed | tf_op | source)
XLA Modules:
  0.0 179.2 jit_solution(14744511945312189570)
XLA Ops:
  0.6 3.3 %route.1 = (bf16[256,1280]{1,0:T(8,128)(2,1)}, f32[128,256]{1,0:T(8,128)}, f32[128,256]{1,0:T(8,128)}) custom-call(bf16[1,256,1280]{2,1,0:T(8,128)(2,1)} %tokens.3, bf16[128,1280]{1,0:T(8,128)(2,1)} %slot_params.3, bf16[1,256,1280]{2,1,0:T(8,128)(2,1)} %grad_out.3), custom_call_target="tpu_custom_call" | custom-call | tf_op jit(solution)/shard_map/route/pallas_call | solution.py:77
  3.9 21.6 %all_to_all.40 = bf16[16,16,1280]{2,1,0:T(8,128)(2,1)S(1)} all-to-all(bf16[16,16,1280]{2,1,0:T(8,128)(2,1)} %bitcast.13), channel_id=1, replica_groups=mesh['yh'=2,'x'=4,'c'=2,'yl'=2,'z'=4] {'yh','x','c'}, dimensions={0} | all-to-all | bytes 1310720 | tf_op jit(solution)/shard_map/all_to_all | solution.py:278
  25.6 0.3 sort_rows.1
  26.0 1.7 collective-permute-start
  27.7 0.4 collective-permute-start.3
  28.1 2.2 %collective-permute-start.15 = (bf16[2,64,1280]{2,1,0:T(8,128)(2,1)S(1)}, bf16[2,64,1280]{2,1,0:T(8,128)(2,1)S(1)}, u32[]{:S(2)}, u32[]{:S(2)}) collective-permute-start(bf16[2,64,1280]{2,1,0:T(8,128)(2,1)S(1)} %get-tuple-element.56.refs_0_.refs_10_), channel_id=1, source_target_pairs={{0,3},{1,0},{2,1},{3,2},{4,7},{5,4},{6,5},{7,6},{8,11},{9,8},{10,9... | collective-permute-start | bytes 983048 | tf_op jit(solution)/shard_map/second_down/ppermute | solution.py:38
  30.3 7.2 %collective-permute-done.refs_1_ = bf16[2,64,1280]{2,1,0:T(8,128)(2,1)S(1)} collective-permute-done((bf16[2,64,1280]{2,1,0:T(8,128)(2,1)S(1)}, bf16[2,64,1280]{2,1,0:T(8,128)(2,1)S(1)}, u32[]{:S(2)}, u32[]{:S(2)}) %collective-permute-start) | collective-permute-done | bytes 327712 | tf_op jit(solution)/shard_map/first_up/ppermute | solution.py:33
  37.5 2.7 %collective-permute-start.2 = (bf16[2,64,1280]{2,1,0:T(8,128)(2,1)S(1)}, bf16[2,64,1280]{2,1,0:T(8,128)(2,1)S(1)}, u32[]{:S(2)}, u32[]{:S(2)}) collective-permute-start(bf16[2,64,1280]{2,1,0:T(8,128)(2,1)S(1)} %get-tuple-element.42.refs_0_), channel_id=1, source_target_pairs={{0,3},{1,0},{2,1},{3,2},{4,7},{5,4},{6,5},{7,6},{8,11},{9,8},{10,9... | collective-permute-start | bytes 983048 | tf_op jit(solution)/shard_map/first_down/ppermute | solution.py:38
  40.2 0.4 collective-permute-start.17
  40.6 4.4 %stage.1 = (bf16[4,576,1280]{2,1,0:T(8,128)(2,1)S(1)}, bf16[4,576,1280]{2,1,0:T(8,128)(2,1)S(1)}) custom-call(bf16[4,576,1280]{2,1,0:T(8,128)(2,1)} %w_in, bf16[4,576,1280]{2,1,0:T(8,128)(2,1)} %w_out), custom_call_target="tpu_custom_call" | custom-call | tf_op jit(solution)/shard_map/stage/pallas_call | solution.py:120
  45.2 2.6 %collective-permute-start.6 = (bf16[2,64,1280]{2,1,0:T(8,128)(2,1)S(1)}, bf16[2,64,1280]{2,1,0:T(8,128)(2,1)S(1)}, u32[]{:S(2)}, u32[]{:S(2)}) collective-permute-start(bf16[2,64,1280]{2,1,0:T(8,128)(2,1)S(1)} %collective-permute-done.3.refs_4_), channel_id=1, source_target_pairs={{0,3},{1,0},{2,1},{3,2},{4,7},{5,4},{6,5},{7,6},{8,11},{9,8},{10,9... | collective-permute-start | bytes 983048 | tf_op jit(solution)/shard_map/first_y_down/ppermute | solution.py:38
  47.9 1.1 collective-permute-start.5
  49.0 1.4 collective-permute-start.14
  50.4 3.4 %collective-permute-done.4.refs_5_ = bf16[2,64,1280]{2,1,0:T(8,128)(2,1)S(1)} collective-permute-done((bf16[2,64,1280]{2,1,0:T(8,128)(2,1)S(1)}, bf16[2,64,1280]{2,1,0:T(8,128)(2,1)S(1)}, u32[]{:S(2)}, u32[]{:S(2)}) %collective-permute-start.4) | collective-permute-done | bytes 327712 | tf_op jit(solution)/shard_map/first_y_up/ppermute | solution.py:33
  53.8 6.0 %collective-permute-done.16.refs_2_.refs_12_ = bf16[2,64,1280]{2,1,0:T(8,128)(2,1)S(1)} collective-permute-done((bf16[2,64,1280]{2,1,0:T(8,128)(2,1)S(1)}, bf16[2,64,1280]{2,1,0:T(8,128)(2,1)S(1)}, u32[]{:S(2)}, u32[]{:S(2)}) %collective-permute-start.16) | collective-permute-done | bytes 327712 | tf_op jit(solution)/shard_map/second_on_down/ppermute | solution.py:38
  59.8 1.1 collective-permute-start.19
  60.9 3.4 %collective-permute-start.20 = (bf16[2,64,1280]{2,1,0:T(8,128)(2,1)S(1)}, bf16[2,64,1280]{2,1,0:T(8,128)(2,1)S(1)}, u32[]{:S(2)}, u32[]{:S(2)}) collective-permute-start(bf16[2,64,1280]{2,1,0:T(8,128)(2,1)S(1)} %collective-permute-done.17.refs_4_.refs_14_), channel_id=1, source_target_pairs={{0,3},{1,0},{2,1},{3,2},{4,7},{5,4},{6,5},{7,6},{8,11},{9,8},{10,9... | collective-permute-start | bytes 983048 | tf_op jit(solution)/shard_map/second_y_down/ppermute | solution.py:38
  64.3 4.3 %expert.2 = (bf16[2,576,256]{2,1,0:T(8,128)(2,1)S(1)}, bf16[2,576,256]{2,1,0:T(8,128)(2,1)S(1)}, bf16[2,64,1280]{2,1,0:T(8,128)(2,1)S(1)}, bf16[2,64,1280]{2,1,0...) custom-call(bf16[2,64,1280]{2,1,0:T(8,128)(2,1)S(1)} %get-tuple-elem, ...), custom_call_target="tpu_custom_call" | custom-call | flops 3019898880 | bytes 12582912 | tf_op jit(solution)/shard_map/expert/pallas_call | solution.py:183
  68.7 0.8 copy-done.21
  69.5 1.4 collective-permute-start.11
  71.0 1.3 collective-permute-start.7
  72.3 0.4 collective-permute-start.8
  72.7 4.3 %expert.3 = (bf16[2,576,256]{2,1,0:T(8,128)(2,1)S(1)}, bf16[2,576,256]{2,1,0:T(8,128)(2,1)S(1)}, bf16[2,64,1280]{2,1,0:T(8,128)(2,1)S(1)}, bf16[2,64,1280]{2,1,0...) custom-call(bf16[2,64,1280]{2,1,0:T(8,128)(2,1)S(1)} %get-tuple-elem, ...), custom_call_target="tpu_custom_call" | custom-call | flops 3019898880 | bytes 12582912 | tf_op jit(solution)/shard_map/expert/pallas_call | solution.py:183
  77.4 1.1 collective-permute-start.22
  78.5 2.5 %collective-permute-start.26 = (bf16[2,64,1280]{2,1,0:T(8,128)(2,1)S(1)}, bf16[2,64,1280]{2,1,0:T(8,128)(2,1)S(1)}, u32[]{:S(2)}, u32[]{:S(2)}) collective-permute-start(bf16[2,64,1280]{2,1,0:T(8,128)(2,1)S(1)} %get-tuple-element.65), channel_id=1, source_target_pairs={{0,3},{1,0},{2,1},{3,2},{4,7},{5,4},{6,5},{7,6},{8,11},{9,8},{10,9... | collective-permute-start | bytes 983048 | tf_op jit(solution)/shard_map/sum_second_y_down/ppermute | solution.py:38
  81.5 5.1 %collective-permute-done.22 = bf16[2,64,1280]{2,1,0:T(8,128)(2,1)S(1)} collective-permute-done((bf16[2,64,1280]{2,1,0:T(8,128)(2,1)S(1)}, bf16[2,64,1280]{2,1,0:T(8,128)(2,1)S(1)}, u32[]{:S(2)}, u32[]{:S(2)}) %collective-permute-start.22) | collective-permute-done | bytes 327712 | tf_op jit(solution)/shard_map/sum_second_far_across/ppermute | solution.py:43
  86.6 0.7 collective-permute-start.9
  87.3 3.8 %collective-permute-done.26 = bf16[2,64,1280]{2,1,0:T(8,128)(2,1)S(1)} collective-permute-done((bf16[2,64,1280]{2,1,0:T(8,128)(2,1)S(1)}, bf16[2,64,1280]{2,1,0:T(8,128)(2,1)S(1)}, u32[]{:S(2)}, u32[]{:S(2)}) %collective-permute-start.26) | collective-permute-done | bytes 327712 | tf_op jit(solution)/shard_map/sum_second_y_down/ppermute | solution.py:38
  91.2 0.4 collective-permute-start.13
  91.7 3.3 %collective-permute-start.23 = (bf16[2,64,1280]{2,1,0:T(8,128)(2,1)S(1)}, bf16[2,64,1280]{2,1,0:T(8,128)(2,1)S(1)}, u32[]{:S(2)}, u32[]{:S(2)}) collective-permute-start(bf16[2,64,1280]{2,1,0:T(8,128)(2,1)S(1)} %add_convert_fusion.2), channel_id=1, source_target_pairs={{0,3},{1,0},{2,1},{3,2},{4,7},{5,4},{6,5},{7,6},{8,11},{9,8},{10,9... | collective-permute-start | bytes 983048 | tf_op jit(solution)/shard_map/sum_second_on_down/ppermute | solution.py:38
  95.1 3.6 %collective-permute-done.9 = bf16[2,64,1280]{2,1,0:T(8,128)(2,1)S(1)} collective-permute-done((bf16[2,64,1280]{2,1,0:T(8,128)(2,1)S(1)}, bf16[2,64,1280]{2,1,0:T(8,128)(2,1)S(1)}, u32[]{:S(2)}, u32[]{:S(2)}) %collective-permute-start.9) | collective-permute-done | bytes 327712 | tf_op jit(solution)/shard_map/sum_first_on_up/ppermute | solution.py:33
  98.7 0.9 collective-permute-start.27
  99.9 2.7 %collective-permute-start.24 = (bf16[2,64,1280]{2,1,0:T(8,128)(2,1)S(1)}, bf16[2,64,1280]{2,1,0:T(8,128)(2,1)S(1)}, u32[]{:S(2)}, u32[]{:S(2)}) collective-permute-start(bf16[2,64,1280]{2,1,0:T(8,128)(2,1)S(1)} %add_convert_fusion.1), channel_id=1, source_target_pairs={{0,3},{1,0},{2,1},{3,2},{4,7},{5,4},{6,5},{7,6},{8,11},{9,8},{10,9... | collective-permute-start | bytes 983048 | tf_op jit(solution)/shard_map/sum_second_down/ppermute | solution.py:38
  102.6 2.3 %collective-permute-done.27.refs_7_ = bf16[2,64,1280]{2,1,0:T(8,128)(2,1)S(1)} collective-permute-done((bf16[2,64,1280]{2,1,0:T(8,128)(2,1)S(1)}, bf16[2,64,1280]{2,1,0:T(8,128)(2,1)S(1)}, u32[]{:S(2)}, u32[]{:S(2)}) %collective-permute-start.27) | collective-permute-done | bytes 327712 | tf_op jit(solution)/shard_map/sum_second_across/ppermute | solution.py:43
  104.9 2.0 %collective-permute-done.10.refs_2_ = bf16[2,64,1280]{2,1,0:T(8,128)(2,1)S(1)} collective-permute-done((bf16[2,64,1280]{2,1,0:T(8,128)(2,1)S(1)}, bf16[2,64,1280]{2,1,0:T(8,128)(2,1)S(1)}, u32[]{:S(2)}, u32[]{:S(2)}) %collective-permute-start.10) | collective-permute-done | bytes 327712 | tf_op jit(solution)/shard_map/sum_first_up/ppermute | solution.py:33
  106.9 2.5 %collective-permute-done.24.refs_6_ = bf16[2,64,1280]{2,1,0:T(8,128)(2,1)S(1)} collective-permute-done((bf16[2,64,1280]{2,1,0:T(8,128)(2,1)S(1)}, bf16[2,64,1280]{2,1,0:T(8,128)(2,1)S(1)}, u32[]{:S(2)}, u32[]{:S(2)}) %collective-permute-start.24) | collective-permute-done | bytes 327712 | tf_op jit(solution)/shard_map/sum_second_down/ppermute | solution.py:38
  109.5 0.6 unsort_rows.1
  110.1 24.9 %all_to_all.41 = bf16[16,16,1280]{2,1,0:T(8,128)(2,1)S(1)} all-to-all(bf16[16,16,1280]{2,1,0:T(8,128)(2,1)S(1)} %bitcast.9), channel_id=1, replica_groups=mesh['yh'=2,'x'=4,'c'=2,'yl'=2,'z'=4] {'yh','x','c'}, dimensions={0} | all-to-all | bytes 1310720 | tf_op jit(solution)/shard_map/all_to_all | solution.py:278
  135.1 0.8 logits_back.1
  135.9 0.7 copy.9
  136.6 20.4 %all_to_all.42 = f32[128,1,1280]{2,1,0:T(1,128)S(1)} all-to-all(f32[128,1,1280]{2,1,0:T(1,128)S(1)} %copy.9), channel_id=1, replica_groups=mesh['yh'=2,'x'=4,'c'=2,'yl'=2,'z'=4] {'yh','x','c','yl','z'}, dimensions={0} | all-to-all | bytes 1310720 | tf_op jit(solution)/shard_map/all_to_all | solution.py:335
  157.0 0.4 reduce_sum.9
  157.4 1.2 reshape.28
  158.6 4.6 %all-to-all-start.3 = ((f32[128,1,1280]{2,1,0:T(1,128)}), f32[128,1,1280]{2,1,0:T(1,128)S(1)}, u32[]{:S(2)}, u32[]{:S(2)}) async-start(f32[128,1,1280]{2,1,0:T(1,128)} %reshape.28), calls=%async_computation.3 | async-start | bytes 1310720 | tf_op jit(solution)/shard_map/all_to_all | solution.py:338
  163.2 9.8 %weight_grads.1 = (bf16[4,576,1280]{2,1,0:T(8,128)(2,1)}, bf16[4,576,1280]{2,1,0:T(8,128)(2,1)}) custom-call(bf16[2,64,1280]{2,1,0:T(8,128)(2,1)} %copy-done.4, bf16[2,64,1280]{2,1,0:T(8,128)(2,1)} %copy-done.6, bf16[2,64,1280]{2,1,0:T(8,128)(2,1)} %copy-done.9, bf16[2,64,1280]{2,1,0:T(8,128)(2,1)} %copy-done.10, bf16[2,64,1280]{2,1,0:T(8,128)(2,1)} %copy-done.7, ...), custom_call_target="tpu_custom_call" | custom-call | flops 3019898880 | bytes 20971520 | tf_op jit(solution)/shard_map/weight_grads/pallas_call | solution.py:230
  173.0 1.4 tokens_back.1
  174.4 3.9 %all-to-all-done.3 = f32[128,1,1280]{2,1,0:T(1,128)S(1)} async-done(((f32[128,1,1280]{2,1,0:T(1,128)}), f32[128,1,1280]{2,1,0:T(1,128)S(1)}, u32[]{:S(2)}, u32[]{:S(2)}) %all-to-all-start.3) | async-done | bytes 655392 | tf_op jit(solution)/shard_map/all_to_all | solution.py:338
  178.3 0.9 copy.12
  (82 shorter events, 1.6 us)
Async XLA Ops:
  26.0 38.3 %copy-start.4 = (bf16[2,64,1280]{2,1,0:T(8,128)(2,1)}, bf16[2,64,1280]{2,1,0:T(8,128)(2,1)S(1)}, u32[]{:S(2)}) copy-start(bf16[2,64,1280]{2,1,0:T(8,128)(2,1)S(1)} %get-tuple-element.42.refs_0_) | copy-start | bytes 983044
  26.0 46.7 %copy-start.5 = (bf16[2,64,1280]{2,1,0:T(8,128)(2,1)}, bf16[2,64,1280]{2,1,0:T(8,128)(2,1)S(1)}, u32[]{:S(2)}) copy-start(bf16[2,64,1280]{2,1,0:T(8,128)(2,1)S(1)} %get-tuple-element.56.refs_0_.refs_10_) | copy-start | bytes 983044
  26.0 11.6 %collective-permute-start = (bf16[2,64,1280]{2,1,0:T(8,128)(2,1)S(1)}, bf16[2,64,1280]{2,1,0:T(8,128)(2,1)S(1)}, u32[]{:S(2)}, u32[]{:S(2)}) collective-permute-start(bf16[2,64,1280]{2,1,0:T(8,128)(2,1)S(1)} %get-tuple-element.42.refs_0_), channel_id=1, source_target_pairs={{0,1},{1,2},{2,3},{3,0},{4,5},{5,6},{6,7},{7,4},{8,9},{9,10},{10,1... | collective-permute-start | bytes 983048 | tf_op jit(solution)/shard_map/first_up/ppermute | solution.py:33
  27.7 17.4 %collective-permute-start.3 = (bf16[2,64,1280]{2,1,0:T(8,128)(2,1)S(1)}, bf16[2,64,1280]{2,1,0:T(8,128)(2,1)S(1)}, u32[]{:S(2)}, u32[]{:S(2)}) collective-permute-start(bf16[2,64,1280]{2,1,0:T(8,128)(2,1)S(1)} %get-tuple-element.42.refs_0_), channel_id=1, source_target_pairs={{0,4},{4,0},{1,5},{5,1},{2,6},{6,2},{3,7},{7,3},{8,12},{12,8},{9,1... | collective-permute-start | bytes 983048 | tf_op jit(solution)/shard_map/first_across/ppermute | solution.py:43
  28.1 17.1 %collective-permute-start.15 = (bf16[2,64,1280]{2,1,0:T(8,128)(2,1)S(1)}, bf16[2,64,1280]{2,1,0:T(8,128)(2,1)S(1)}, u32[]{:S(2)}, u32[]{:S(2)}) collective-permute-start(bf16[2,64,1280]{2,1,0:T(8,128)(2,1)S(1)} %get-tuple-element.56.refs_0_.refs_10_), channel_id=1, source_target_pairs={{0,3},{1,0},{2,1},{3,2},{4,7},{5,4},{6,5},{7,6},{8,11},{9,8},{10,9... | collective-permute-start | bytes 983048 | tf_op jit(solution)/shard_map/second_down/ppermute | solution.py:38
  37.5 26.7 %copy-start.6 = (bf16[2,64,1280]{2,1,0:T(8,128)(2,1)}, bf16[2,64,1280]{2,1,0:T(8,128)(2,1)S(1)}, u32[]{:S(2)}) copy-start(bf16[2,64,1280]{2,1,0:T(8,128)(2,1)S(1)} %collective-permute-done.refs_1_) | copy-start | bytes 983044
  37.5 10.3 %collective-permute-start.1 = (bf16[2,64,1280]{2,1,0:T(8,128)(2,1)S(1)}, bf16[2,64,1280]{2,1,0:T(8,128)(2,1)S(1)}, u32[]{:S(2)}, u32[]{:S(2)}) collective-permute-start(bf16[2,64,1280]{2,1,0:T(8,128)(2,1)S(1)} %collective-permute-done.refs_1_), channel_id=1, source_target_pairs={{0,1},{1,2},{2,3},{3,0},{4,5},{5,6},{6,7},{7,4},{8,9},{9,10},{10,1... | collective-permute-start | bytes 983048 | tf_op jit(solution)/shard_map/first_on_up/ppermute | solution.py:33
  37.5 10.4 %collective-permute-start.2 = (bf16[2,64,1280]{2,1,0:T(8,128)(2,1)S(1)}, bf16[2,64,1280]{2,1,0:T(8,128)(2,1)S(1)}, u32[]{:S(2)}, u32[]{:S(2)}) collective-permute-start(bf16[2,64,1280]{2,1,0:T(8,128)(2,1)S(1)} %get-tuple-element.42.refs_0_), channel_id=1, source_target_pairs={{0,3},{1,0},{2,1},{3,2},{4,7},{5,4},{6,5},{7,6},{8,11},{9,8},{10,9... | collective-permute-start | bytes 983048 | tf_op jit(solution)/shard_map/first_down/ppermute | solution.py:38
  40.2 8.8 %collective-permute-start.17 = (bf16[2,64,1280]{2,1,0:T(8,128)(2,1)S(1)}, bf16[2,64,1280]{2,1,0:T(8,128)(2,1)S(1)}, u32[]{:S(2)}, u32[]{:S(2)}) collective-permute-start(bf16[2,64,1280]{2,1,0:T(8,128)(2,1)S(1)} %get-tuple-element.56.refs_0_.refs_10_), channel_id=1, source_target_pairs={{0,4},{4,0},{1,5},{5,1},{2,6},{6,2},{3,7},{7,3},{8,12},{12,8},{9,1... | collective-permute-start | bytes 983048 | tf_op jit(solution)/shard_map/second_across/ppermute | solution.py:43
  45.0 23.6 %copy-start.7 = (bf16[2,64,1280]{2,1,0:T(8,128)(2,1)}, bf16[2,64,1280]{2,1,0:T(8,128)(2,1)S(1)}, u32[]{:S(2)}) copy-start(bf16[2,64,1280]{2,1,0:T(8,128)(2,1)S(1)} %collective-permute-done.3.refs_4_) | copy-start | bytes 983044
  45.1 8.7 %collective-permute-start.4 = (bf16[2,64,1280]{2,1,0:T(8,128)(2,1)S(1)}, bf16[2,64,1280]{2,1,0:T(8,128)(2,1)S(1)}, u32[]{:S(2)}, u32[]{:S(2)}) collective-permute-start(bf16[2,64,1280]{2,1,0:T(8,128)(2,1)S(1)} %collective-permute-done.3.refs_4_), channel_id=1, source_target_pairs={{0,1},{1,2},{2,3},{3,0},{4,5},{5,6},{6,7},{7,4},{8,9},{9,10},{10,1... | collective-permute-start | bytes 983048 | tf_op jit(solution)/shard_map/first_y_up/ppermute | solution.py:33
  45.1 27.5 %copy-start.8 = (bf16[2,64,1280]{2,1,0:T(8,128)(2,1)}, bf16[2,64,1280]{2,1,0:T(8,128)(2,1)S(1)}, u32[]{:S(2)}) copy-start(bf16[2,64,1280]{2,1,0:T(8,128)(2,1)S(1)} %collective-permute-done.15.refs_3_.refs_13_) | copy-start | bytes 983044
  45.2 15.7 %collective-permute-start.6 = (bf16[2,64,1280]{2,1,0:T(8,128)(2,1)S(1)}, bf16[2,64,1280]{2,1,0:T(8,128)(2,1)S(1)}, u32[]{:S(2)}, u32[]{:S(2)}) collective-permute-start(bf16[2,64,1280]{2,1,0:T(8,128)(2,1)S(1)} %collective-permute-done.3.refs_4_), channel_id=1, source_target_pairs={{0,3},{1,0},{2,1},{3,2},{4,7},{5,4},{6,5},{7,6},{8,11},{9,8},{10,9... | collective-permute-start | bytes 983048 | tf_op jit(solution)/shard_map/first_y_down/ppermute | solution.py:38
  47.8 20.8 %copy-start.9 = (bf16[2,64,1280]{2,1,0:T(8,128)(2,1)}, bf16[2,64,1280]{2,1,0:T(8,128)(2,1)S(1)}, u32[]{:S(2)}) copy-start(bf16[2,64,1280]{2,1,0:T(8,128)(2,1)S(1)} %collective-permute-done.1.refs_2_) | copy-start | bytes 983044
  47.8 12.0 %collective-permute-start.16 = (bf16[2,64,1280]{2,1,0:T(8,128)(2,1)S(1)}, bf16[2,64,1280]{2,1,0:T(8,128)(2,1)S(1)}, u32[]{:S(2)}, u32[]{:S(2)}) collective-permute-start(bf16[2,64,1280]{2,1,0:T(8,128)(2,1)S(1)} %collective-permute-done.15.refs_3_.refs_13_), channel_id=1, source_target_pairs={{0,3},{1,0},{2,1},{3,2},{4,7},{5,4},{6,5},{7,6},{8,11},{9,8},{10,9... | collective-permute-start | bytes 983048 | tf_op jit(solution)/shard_map/second_on_down/ppermute | solution.py:38
  47.9 20.7 %copy-start.10 = (bf16[2,64,1280]{2,1,0:T(8,128)(2,1)}, bf16[2,64,1280]{2,1,0:T(8,128)(2,1)S(1)}, u32[]{:S(2)}) copy-start(bf16[2,64,1280]{2,1,0:T(8,128)(2,1)S(1)} %collective-permute-done.2.refs_3_) | copy-start | bytes 983044
  47.9 16.4 %collective-permute-start.5 = (bf16[2,64,1280]{2,1,0:T(8,128)(2,1)S(1)}, bf16[2,64,1280]{2,1,0:T(8,128)(2,1)S(1)}, u32[]{:S(2)}, u32[]{:S(2)}) collective-permute-start(bf16[2,64,1280]{2,1,0:T(8,128)(2,1)S(1)} %collective-permute-done.1.refs_2_), channel_id=1, source_target_pairs={{0,4},{4,0},{1,5},{5,1},{2,6},{6,2},{3,7},{7,3},{8,12},{12,8},{9,1... | collective-permute-start | bytes 983048 | tf_op jit(solution)/shard_map/first_far_across/ppermute | solution.py:43
  49.0 23.7 %copy-start.11 = (bf16[2,64,1280]{2,1,0:T(8,128)(2,1)}, bf16[2,64,1280]{2,1,0:T(8,128)(2,1)S(1)}, u32[]{:S(2)}) copy-start(bf16[2,64,1280]{2,1,0:T(8,128)(2,1)S(1)} %collective-permute-done.17.refs_4_.refs_14_) | copy-start | bytes 983044
  49.0 20.5 %collective-permute-start.14 = (bf16[2,64,1280]{2,1,0:T(8,128)(2,1)S(1)}, bf16[2,64,1280]{2,1,0:T(8,128)(2,1)S(1)}, u32[]{:S(2)}, u32[]{:S(2)}) collective-permute-start(bf16[2,64,1280]{2,1,0:T(8,128)(2,1)S(1)} %get-tuple-element.56.refs_0_.refs_10_), channel_id=1, source_target_pairs={{0,1},{1,2},{2,3},{3,0},{4,5},{5,6},{6,7},{7,4},{8,9},{9,10},{10,1... | collective-permute-start | bytes 983048 | tf_op jit(solution)/shard_map/second_up/ppermute | solution.py:33
  53.8 14.9 %copy-start.12 = (bf16[2,64,1280]{2,1,0:T(8,128)(2,1)}, bf16[2,64,1280]{2,1,0:T(8,128)(2,1)S(1)}, u32[]{:S(2)}) copy-start(bf16[2,64,1280]{2,1,0:T(8,128)(2,1)S(1)} %collective-permute-done.4.refs_5_) | copy-start | bytes 983044
  53.8 17.2 %collective-permute-start.18 = (bf16[2,64,1280]{2,1,0:T(8,128)(2,1)S(1)}, bf16[2,64,1280]{2,1,0:T(8,128)(2,1)S(1)}, u32[]{:S(2)}, u32[]{:S(2)}) collective-permute-start(bf16[2,64,1280]{2,1,0:T(8,128)(2,1)S(1)} %collective-permute-done.17.refs_4_.refs_14_), channel_id=1, source_target_pairs={{0,1},{1,2},{2,3},{3,0},{4,5},{5,6},{6,7},{7,4},{8,9},{9,10},{10,1... | collective-permute-start | bytes 983048 | tf_op jit(solution)/shard_map/second_y_up/ppermute | solution.py:33
  59.8 12.9 %copy-start.14 = (bf16[2,64,1280]{2,1,0:T(8,128)(2,1)}, bf16[2,64,1280]{2,1,0:T(8,128)(2,1)S(1)}, u32[]{:S(2)}) copy-start(bf16[2,64,1280]{2,1,0:T(8,128)(2,1)S(1)} %collective-permute-done.16.refs_2_.refs_12_) | copy-start | bytes 983044
  59.8 12.5 %collective-permute-start.19 = (bf16[2,64,1280]{2,1,0:T(8,128)(2,1)S(1)}, bf16[2,64,1280]{2,1,0:T(8,128)(2,1)S(1)}, u32[]{:S(2)}, u32[]{:S(2)}) collective-permute-start(bf16[2,64,1280]{2,1,0:T(8,128)(2,1)S(1)} %collective-permute-done.16.refs_2_.refs_12_), channel_id=1, source_target_pairs={{0,4},{4,0},{1,5},{5,1},{2,6},{6,2},{3,7},{7,3},{8,12},{12,8},{9,1... | collective-permute-start | bytes 983048 | tf_op jit(solution)/shard_map/second_far_across/ppermute | solution.py:43
  60.8 7.8 %copy-start.13 = (bf16[2,64,1280]{2,1,0:T(8,128)(2,1)}, bf16[2,64,1280]{2,1,0:T(8,128)(2,1)S(1)}, u32[]{:S(2)}) copy-start(bf16[2,64,1280]{2,1,0:T(8,128)(2,1)S(1)} %collective-permute-done.6.refs_7_) | copy-start | bytes 983044
  60.9 11.8 %collective-permute-start.20 = (bf16[2,64,1280]{2,1,0:T(8,128)(2,1)S(1)}, bf16[2,64,1280]{2,1,0:T(8,128)(2,1)S(1)}, u32[]{:S(2)}, u32[]{:S(2)}) collective-permute-start(bf16[2,64,1280]{2,1,0:T(8,128)(2,1)S(1)} %collective-permute-done.17.refs_4_.refs_14_), channel_id=1, source_target_pairs={{0,3},{1,0},{2,1},{3,2},{4,7},{5,4},{6,5},{7,6},{8,11},{9,8},{10,9... | collective-permute-start | bytes 983048 | tf_op jit(solution)/shard_map/second_y_down/ppermute | solution.py:38
  69.5 7.6 %copy-start.22 = (bf16[2,576,256]{2,1,0:T(8,128)(2,1)}, bf16[2,576,256]{2,1,0:T(8,128)(2,1)S(1)}, u32[]{:S(2)}) copy-start(bf16[2,576,256]{2,1,0:T(8,128)(2,1)S(1)} %get-tuple-element.71.refs_9_) | copy-start | bytes 1769476
  69.5 7.9 %collective-permute-start.12 = (bf16[2,64,1280]{2,1,0:T(8,128)(2,1)S(1)}, bf16[2,64,1280]{2,1,0:T(8,128)(2,1)S(1)}, u32[]{:S(2)}, u32[]{:S(2)}) collective-permute-start(bf16[2,64,1280]{2,1,0:T(8,128)(2,1)S(1)} %get-tuple-element.55), channel_id=1, source_target_pairs={{0,3},{1,0},{2,1},{3,2},{4,7},{5,4},{6,5},{7,6},{8,11},{9,8},{10,9... | collective-permute-start | bytes 983048 | tf_op jit(solution)/shard_map/sum_first_y_down/ppermute | solution.py:38
  69.5 9.0 %collective-permute-start.11 = (bf16[2,64,1280]{2,1,0:T(8,128)(2,1)S(1)}, bf16[2,64,1280]{2,1,0:T(8,128)(2,1)S(1)}, u32[]{:S(2)}, u32[]{:S(2)}) collective-permute-start(bf16[2,64,1280]{2,1,0:T(8,128)(2,1)S(1)} %get-tuple-element.54), channel_id=1, source_target_pairs={{0,1},{1,2},{2,3},{3,0},{4,5},{5,6},{6,7},{7,4},{8,9},{9,10},{10,1... | collective-permute-start | bytes 983048 | tf_op jit(solution)/shard_map/sum_first_y_up/ppermute | solution.py:33
  71.0 28.9 %collective-permute-start.7 = (bf16[2,64,1280]{2,1,0:T(8,128)(2,1)S(1)}, bf16[2,64,1280]{2,1,0:T(8,128)(2,1)S(1)}, u32[]{:S(2)}, u32[]{:S(2)}) collective-permute-start(bf16[2,64,1280]{2,1,0:T(8,128)(2,1)S(1)} %get-tuple-element.49), channel_id=1, source_target_pairs={{0,3},{1,0},{2,1},{3,2},{4,7},{5,4},{6,5},{7,6},{8,11},{9,8},{10,9... | collective-permute-start | bytes 983048 | tf_op jit(solution)/shard_map/sum_first_down/ppermute | solution.py:38
  72.3 8.9 %collective-permute-start.8 = (bf16[2,64,1280]{2,1,0:T(8,128)(2,1)S(1)}, bf16[2,64,1280]{2,1,0:T(8,128)(2,1)S(1)}, u32[]{:S(2)}, u32[]{:S(2)}) collective-permute-start(bf16[2,64,1280]{2,1,0:T(8,128)(2,1)S(1)} %get-tuple-element.52), channel_id=1, source_target_pairs={{0,4},{4,0},{1,5},{5,1},{2,6},{6,2},{3,7},{7,3},{8,12},{12,8},{9,1... | collective-permute-start | bytes 983048 | tf_op jit(solution)/shard_map/sum_first_far_across/ppermute | solution.py:43
  77.1 58.8 %copy-start.23 = (bf16[2,576,256]{2,1,0:T(8,128)(2,1)}, bf16[2,576,256]{2,1,0:T(8,128)(2,1)S(1)}, u32[]{:S(2)}) copy-start(bf16[2,576,256]{2,1,0:T(8,128)(2,1)S(1)} %get-tuple-element.72.refs_18_) | copy-start | bytes 1769476
  77.1 58.8 %copy-start.24 = (bf16[2,576,256]{2,1,0:T(8,128)(2,1)}, bf16[2,576,256]{2,1,0:T(8,128)(2,1)S(1)}, u32[]{:S(2)}) copy-start(bf16[2,576,256]{2,1,0:T(8,128)(2,1)S(1)} %get-tuple-element.73.refs_19_) | copy-start | bytes 1769476
  77.1 57.9 %copy-start = (bf16[1,256,1280]{2,1,0:T(8,128)(2,1)S(1)}, bf16[1,256,1280]{2,1,0:T(8,128)(2,1)}, u32[]{:S(2)}) copy-start(bf16[1,256,1280]{2,1,0:T(8,128)(2,1)} %tokens.3) | copy-start | bytes 1966084
  77.1 57.9 %copy-start.1 = (bf16[1,256,1280]{2,1,0:T(8,128)(2,1)S(1)}, bf16[1,256,1280]{2,1,0:T(8,128)(2,1)}, u32[]{:S(2)}) copy-start(bf16[1,256,1280]{2,1,0:T(8,128)(2,1)} %grad_out.3) | copy-start | bytes 1966084
  77.2 57.9 %copy-start.3 = (f32[128,256]{1,0:T(8,128)S(1)}, f32[128,256]{1,0:T(8,128)}, u32[]{:S(2)}) copy-start(f32[128,256]{1,0:T(8,128)} %get-tuple-element.40.p_dispatch) | copy-start | bytes 393220
  77.2 57.9 %copy-start.20 = (f32[128,256]{1,0:T(8,128)S(1)}, f32[128,256]{1,0:T(8,128)}, u32[]{:S(2)}) copy-start(f32[128,256]{1,0:T(8,128)} %get-tuple-element.66.p_combine) | copy-start | bytes 393220
  77.2 25.5 %collective-permute-start.21 = (bf16[2,64,1280]{2,1,0:T(8,128)(2,1)S(1)}, bf16[2,64,1280]{2,1,0:T(8,128)(2,1)S(1)}, u32[]{:S(2)}, u32[]{:S(2)}) collective-permute-start(bf16[2,64,1280]{2,1,0:T(8,128)(2,1)S(1)} %get-tuple-element.59), channel_id=1, source_target_pairs={{0,1},{1,2},{2,3},{3,0},{4,5},{5,6},{6,7},{7,4},{8,9},{9,10},{10,1... | collective-permute-start | bytes 983048 | tf_op jit(solution)/shard_map/sum_second_up/ppermute | solution.py:33
  77.4 9.1 %collective-permute-start.22 = (bf16[2,64,1280]{2,1,0:T(8,128)(2,1)S(1)}, bf16[2,64,1280]{2,1,0:T(8,128)(2,1)S(1)}, u32[]{:S(2)}, u32[]{:S(2)}) collective-permute-start(bf16[2,64,1280]{2,1,0:T(8,128)(2,1)S(1)} %get-tuple-element.62), channel_id=1, source_target_pairs={{0,4},{4,0},{1,5},{5,1},{2,6},{6,2},{3,7},{7,3},{8,12},{12,8},{9,1... | collective-permute-start | bytes 983048 | tf_op jit(solution)/shard_map/sum_second_far_across/ppermute | solution.py:43
  78.5 12.7 %collective-permute-start.26 = (bf16[2,64,1280]{2,1,0:T(8,128)(2,1)S(1)}, bf16[2,64,1280]{2,1,0:T(8,128)(2,1)S(1)}, u32[]{:S(2)}, u32[]{:S(2)}) collective-permute-start(bf16[2,64,1280]{2,1,0:T(8,128)(2,1)S(1)} %get-tuple-element.65), channel_id=1, source_target_pairs={{0,3},{1,0},{2,1},{3,2},{4,7},{5,4},{6,5},{7,6},{8,11},{9,8},{10,9... | collective-permute-start | bytes 983048 | tf_op jit(solution)/shard_map/sum_second_y_down/ppermute | solution.py:38
  81.1 10.5 %collective-permute-start.25 = (bf16[2,64,1280]{2,1,0:T(8,128)(2,1)S(1)}, bf16[2,64,1280]{2,1,0:T(8,128)(2,1)S(1)}, u32[]{:S(2)}, u32[]{:S(2)}) collective-permute-start(bf16[2,64,1280]{2,1,0:T(8,128)(2,1)S(1)} %get-tuple-element.64), channel_id=1, source_target_pairs={{0,1},{1,2},{2,3},{3,0},{4,5},{5,6},{6,7},{7,4},{8,9},{9,10},{10,1... | collective-permute-start | bytes 983048 | tf_op jit(solution)/shard_map/sum_second_y_up/ppermute | solution.py:33
  86.6 12.1 %collective-permute-start.9 = (bf16[2,64,1280]{2,1,0:T(8,128)(2,1)S(1)}, bf16[2,64,1280]{2,1,0:T(8,128)(2,1)S(1)}, u32[]{:S(2)}, u32[]{:S(2)}) collective-permute-start(bf16[2,64,1280]{2,1,0:T(8,128)(2,1)S(1)} %add_convert_fusion.5), channel_id=1, source_target_pairs={{0,1},{1,2},{2,3},{3,0},{4,5},{5,6},{6,7},{7,4},{8,9},{9,10},{10,1... | collective-permute-start | bytes 983048 | tf_op jit(solution)/shard_map/sum_first_on_up/ppermute | solution.py:33
  91.2 11.5 %collective-permute-start.13 = (bf16[2,64,1280]{2,1,0:T(8,128)(2,1)S(1)}, bf16[2,64,1280]{2,1,0:T(8,128)(2,1)S(1)}, u32[]{:S(2)}, u32[]{:S(2)}) collective-permute-start(bf16[2,64,1280]{2,1,0:T(8,128)(2,1)S(1)} %add_convert_fusion.3), channel_id=1, source_target_pairs={{0,4},{4,0},{1,5},{5,1},{2,6},{6,2},{3,7},{7,3},{8,12},{12,8},{9,1... | collective-permute-start | bytes 983048 | tf_op jit(solution)/shard_map/sum_first_across/ppermute | solution.py:43
  91.7 8.0 %collective-permute-start.23 = (bf16[2,64,1280]{2,1,0:T(8,128)(2,1)S(1)}, bf16[2,64,1280]{2,1,0:T(8,128)(2,1)S(1)}, u32[]{:S(2)}, u32[]{:S(2)}) collective-permute-start(bf16[2,64,1280]{2,1,0:T(8,128)(2,1)S(1)} %add_convert_fusion.2), channel_id=1, source_target_pairs={{0,3},{1,0},{2,1},{3,2},{4,7},{5,4},{6,5},{7,6},{8,11},{9,8},{10,9... | collective-permute-start | bytes 983048 | tf_op jit(solution)/shard_map/sum_second_on_down/ppermute | solution.py:38
  98.7 6.2 %collective-permute-start.27 = (bf16[2,64,1280]{2,1,0:T(8,128)(2,1)S(1)}, bf16[2,64,1280]{2,1,0:T(8,128)(2,1)S(1)}, u32[]{:S(2)}, u32[]{:S(2)}) collective-permute-start(bf16[2,64,1280]{2,1,0:T(8,128)(2,1)S(1)} %add_convert_fusion), channel_id=1, source_target_pairs={{0,4},{4,0},{1,5},{5,1},{2,6},{6,2},{3,7},{7,3},{8,12},{12,8},{9,1... | collective-permute-start | bytes 983048 | tf_op jit(solution)/shard_map/sum_second_across/ppermute | solution.py:43
  99.7 7.2 %collective-permute-start.10 = (bf16[2,64,1280]{2,1,0:T(8,128)(2,1)S(1)}, bf16[2,64,1280]{2,1,0:T(8,128)(2,1)S(1)}, u32[]{:S(2)}, u32[]{:S(2)}) collective-permute-start(bf16[2,64,1280]{2,1,0:T(8,128)(2,1)S(1)} %add_convert_fusion.4), channel_id=1, source_target_pairs={{0,1},{1,2},{2,3},{3,0},{4,5},{5,6},{6,7},{7,4},{8,9},{9,10},{10,1... | collective-permute-start | bytes 983048 | tf_op jit(solution)/shard_map/sum_first_up/ppermute | solution.py:33
  99.9 9.6 %collective-permute-start.24 = (bf16[2,64,1280]{2,1,0:T(8,128)(2,1)S(1)}, bf16[2,64,1280]{2,1,0:T(8,128)(2,1)S(1)}, u32[]{:S(2)}, u32[]{:S(2)}) collective-permute-start(bf16[2,64,1280]{2,1,0:T(8,128)(2,1)S(1)} %add_convert_fusion.1), channel_id=1, source_target_pairs={{0,3},{1,0},{2,1},{3,2},{4,7},{5,4},{6,5},{7,6},{8,11},{9,8},{10,9... | collective-permute-start | bytes 983048 | tf_op jit(solution)/shard_map/sum_second_down/ppermute | solution.py:38
  158.6 19.7 %all-to-all-start.3 = ((f32[128,1,1280]{2,1,0:T(1,128)}), f32[128,1,1280]{2,1,0:T(1,128)S(1)}, u32[]{:S(2)}, u32[]{:S(2)}) async-start(f32[128,1,1280]{2,1,0:T(1,128)} %reshape.28), calls=%async_computation.3 | async-start | bytes 1310720 | tf_op jit(solution)/shard_map/all_to_all | solution.py:338
  163.2 9.8 %copy-start.2 = (bf16[128,1280]{1,0:T(8,128)(2,1)S(1)}, bf16[128,1280]{1,0:T(8,128)(2,1)}, u32[]{:S(2)}) copy-start(bf16[128,1280]{1,0:T(8,128)(2,1)} %slot_params.3) | copy-start | bytes 983044
  (6 other events, 28.1 us)

commit v5 on v4

--- a/solution.py
+++ b/solution.py
@@ -28,14 +28,18 @@
     return pltpu.CompilerParams(vmem_limit_bytes=limit * 2**20)
 
 
+def turn(core, z, step):
+    return (core * 4 + z, core * 4 + (z + (step if core == 0 else -step)) % 4)
+
+
 def up(value, name):
     with jax.named_scope(name + "_up"):
-        return lax.ppermute(value, "z", [(i, (i + 1) % 4) for i in range(4)])
+        return lax.ppermute(value, ("c", "z"), [turn(c, z, 1) for c in range(2) for z in range(4)])
 
 
 def down(value, name):
     with jax.named_scope(name + "_down"):
-        return lax.ppermute(value, "z", [(i, (i + 3) % 4) for i in range(4)])
+        return lax.ppermute(value, ("c", "z"), [turn(c, z, -1) for c in range(2) for z in range(4)])
 
 
 def across(value, name):
@@ -132,7 +136,7 @@
     low1, high1, y1 = up(first, "first"), down(first, "first"), across(first, "first")
     low2, high2, y2 = up(second, "second"), down(second, "second"), across(second, "second")
     far1, far2 = up(low1, "first_on"), down(high2, "second_on")
-    weights = stage(*after((w_in, w_out), (low1,)))
+    weights = stage(*after((w_in, w_out), (low1, high1)))
     y_low1, y_high1 = up(y1, "first_y"), down(y1, "first_y")
     (sent,) = after((far1,), weights)
     one = (first, low1, far1, high1, y1, y_low1, across(sent, "first_far"), y_high1)
@@ -244,13 +248,18 @@
     return sum(v.astype(F32) for v in values).astype(BF)
 
 
-def reduce(parts, far_way, name):
+def reduce(parts, far_way, name, wait=False):
     own, low, far, high, y, y_low, y_far, y_high = parts
     w = across(y_far, name + "_far")
     v_up, v_down = up(y_high, name + "_y"), down(y_low, name + "_y")
     near, last, other_way = (low, high, down) if far_way is up else (high, low, up)
+    h = far_way(add(far, w), name + "_on")
+    if wait:
+        (near,) = after((near,), (h,))
     direct = other_way(near, name)
-    chain = far_way(add(last, far_way(add(far, w), name + "_on")), name)
+    chain = far_way(add(last, h), name)
+    if not wait:
+        y, v_up, v_down = after((y, v_up, v_down), (direct,))
     return own, direct, chain, across(add(y, v_up, v_down), name)
 
 
@@ -351,7 +360,7 @@
     kept_one, partial_one = split(expert_call(one, *weights, 0))
     sums_one = reduce(partial_one, up, "sum_first")
     kept_two, partial_two = split(expert_call(two, *weights, resident // 2))
-    sums_two = reduce(partial_two, down, "sum_second")
+    sums_two = reduce(partial_two, down, "sum_second", True)
     grad_w_out, grad_w_in = weight_grads((*one, *kept_one), (*two, *kept_two))
     back = exchange(unsort_rows(sums_one, sums_two, n_expert))
     d_logits, local_params, d_slot_in = logits_back(

time: 180 us -> 174 us (0.967)
  blocking collectives: 67 us -> 60 us
  waiting for transfers between devices: 40.1 us -> 43.6 us
  starting transfers between devices: 37.1 us -> 34.5 us
    ppermute x20, waiting for transfers between devices: 28.7 us -> 38.5 us  [the longest x10 24.7 us: up(): lax.ppermute(value, ('c', 'z'), [turn(c, z, 1) for c in range(2) for z in...]
    ppermute x8, waiting for transfers between devices: 7.37 us -> 1.11 us  [across(): return lax.ppermute(value, 'yl', SWAP)]
    all_to_all x2, blocking collectives: 46.6 us -> 41.7 us  [exchange(): return lax.all_to_all(rows, EXPERT, split_axis=0, concat_axis=0, tiled=True)]
    ppermute x20, starting transfers between devices: 26.8 us -> 23.8 us  [the longest x10 19.9 us: up(): lax.ppermute(value, ('c', 'z'), [turn(c, z, 1) for c in range(2) for z in...]
    all_to_all x1, blocking collectives: 20.4 us -> 18.3 us  [sum_over_all(): lax.all_to_all(value, NAMES, split_axis=0, concat_axis=0, tiled=True)]
  transfers between devices with their start and end apart: 29 -> 29, of which waited for: 11 -> 12; matrix products, arithmetic and copies ran while one was open for 0% -> 0% of each run, Pallas kernels for 14% -> 14%
where the time goes in v5:
time: 174 us; the launch traced here: 173 us
  blocking collectives  60 us (34%)
  waiting for transfers between devices  43.6 us (25%)
  starting transfers between devices  34.5 us (20%)
  Pallas kernels  29.5 us (17%)
  local copies, waits for them, and re-layouts  3.64 us (2%)
    all_to_all x2, blocking collectives, exchange(): return lax.all_to_all(rows, EXPERT, split_axis=0, concat_axis=0, tiled=True)  41.7 us
    ppermute x10, waiting for transfers between devices, up(): lax.ppermute(value, ('c', 'z'), [turn(c, z, 1) for c in range(2) for z in...  24.7 us
    ppermute x10, starting transfers between devices, up(): lax.ppermute(value, ('c', 'z'), [turn(c, z, 1) for c in range(2) for z in...  19.9 us
    all_to_all x1, blocking collectives, sum_over_all(): lax.all_to_all(value, NAMES, split_axis=0, concat_axis=0, tiled=True)  18.3 us
    ppermute x10, waiting for transfers between devices, down(): lax.ppermute(value, ('c', 'z'), [turn(c, z, -1) for c in range(2) for z i...  13.8 us
    pallas_call x1, Pallas kernels, weight_grads(): pl.pallas_call(functools.partial(weights_kernel, half), grid=(2 * half,),...  9.77 us
    pallas_call x2, Pallas kernels, expert_call(): pl.pallas_call(expert_kernel, grid=(count,), in_specs=[per_expert(block,...  8.67 us
    ppermute x8, starting transfers between devices, across(): return lax.ppermute(value, 'yl', SWAP)  6.17 us
  transfers between devices with their start and end apart: 29, of which 12 were waited for; matrix products, arithmetic and copies ran while one was open for 0% of the time, Pallas kernels for 14%

profile of v5, /device:TPU:1, one launch (start us, length us, event | category | flops | bytes accessed | tf_op | source)
XLA Modules:
  0.0 173.2 jit_solution(18360911887557312952)
XLA Ops:
  0.6 3.3 %route.1 = (bf16[256,1280]{1,0:T(8,128)(2,1)}, f32[128,256]{1,0:T(8,128)}, f32[128,256]{1,0:T(8,128)}) custom-call(bf16[1,256,1280]{2,1,0:T(8,128)(2,1)} %tokens.3, bf16[128,1280]{1,0:T(8,128)(2,1)} %slot_params.3, bf16[1,256,1280]{2,1,0:T(8,128)(2,1)} %grad_out.3), custom_call_target="tpu_custom_call" | custom-call | tf_op jit(solution)/shard_map/route/pallas_call | solution.py:81
  3.9 21.6 %all_to_all.40 = bf16[16,16,1280]{2,1,0:T(8,128)(2,1)S(1)} all-to-all(bf16[16,16,1280]{2,1,0:T(8,128)(2,1)} %bitcast.13), channel_id=1, replica_groups=mesh['yh'=2,'x'=4,'c'=2,'yl'=2,'z'=4] {'yh','x','c'}, dimensions={0} | all-to-all | bytes 1310720 | tf_op jit(solution)/shard_map/all_to_all | solution.py:287
  25.6 0.3 sort_rows.1
  26.0 3.8 %collective-permute-start = (bf16[2,64,1280]{2,1,0:T(8,128)(2,1)S(1)}, bf16[2,64,1280]{2,1,0:T(8,128)(2,1)S(1)}, u32[]{:S(2)}, u32[]{:S(2)}) collective-permute-start(bf16[2,64,1280]{2,1,0:T(8,128)(2,1)S(1)} %get-tuple-element.46.refs_0_), channel_id=1, source_target_pairs={{0,1},{1,2},{2,3},{3,0},{8,11},{9,8},{10,9},{11,10},{4,5},{5,6},{6... | collective-permute-start | bytes 983048 | tf_op jit(solution)/shard_map/first_up/ppermute | solution.py:37
  29.8 0.4 collective-permute-start.3
  30.2 6.2 %collective-permute-done.refs_1_ = bf16[2,64,1280]{2,1,0:T(8,128)(2,1)S(1)} collective-permute-done((bf16[2,64,1280]{2,1,0:T(8,128)(2,1)S(1)}, bf16[2,64,1280]{2,1,0:T(8,128)(2,1)S(1)}, u32[]{:S(2)}, u32[]{:S(2)}) %collective-permute-start) | collective-permute-done | bytes 327712 | tf_op jit(solution)/shard_map/first_up/ppermute | solution.py:37
  36.4 3.4 %collective-permute-start.1 = (bf16[2,64,1280]{2,1,0:T(8,128)(2,1)S(1)}, bf16[2,64,1280]{2,1,0:T(8,128)(2,1)S(1)}, u32[]{:S(2)}, u32[]{:S(2)}) collective-permute-start(bf16[2,64,1280]{2,1,0:T(8,128)(2,1)S(1)} %collective-permute-done.refs_1_), channel_id=1, source_target_pairs={{0,1},{1,2},{2,3},{3,0},{8,11},{9,8},{10,9},{11,10},{4,5},{5,6},{6... | collective-permute-start | bytes 983048 | tf_op jit(solution)/shard_map/first_on_up/ppermute | solution.py:37
  39.8 0.4 collective-permute-start.17
  40.2 4.5 %stage.1 = (bf16[4,576,1280]{2,1,0:T(8,128)(2,1)S(1)}, bf16[4,576,1280]{2,1,0:T(8,128)(2,1)S(1)}) custom-call(bf16[4,576,1280]{2,1,0:T(8,128)(2,1)} %w_in, bf16[4,576,1280]{2,1,0:T(8,128)(2,1)} %w_out), custom_call_target="tpu_custom_call" | custom-call | tf_op jit(solution)/shard_map/stage/pallas_call | solution.py:124
  44.8 1.5 collective-permute-start.6
  46.4 1.1 collective-permute-start.5
  47.5 1.1 collective-permute-done.17.refs_4_.refs_14_
  48.6 1.5 collective-permute-start.14
  50.0 2.6 %collective-permute-done.4.refs_5_ = bf16[2,64,1280]{2,1,0:T(8,128)(2,1)S(1)} collective-permute-done((bf16[2,64,1280]{2,1,0:T(8,128)(2,1)S(1)}, bf16[2,64,1280]{2,1,0:T(8,128)(2,1)S(1)}, u32[]{:S(2)}, u32[]{:S(2)}) %collective-permute-start.4) | collective-permute-done | bytes 327712 | tf_op jit(solution)/shard_map/first_y_up/ppermute | solution.py:37
  52.7 0.7 collective-permute-start.18
  53.4 9.4 %collective-permute-done.16.refs_2_.refs_12_ = bf16[2,64,1280]{2,1,0:T(8,128)(2,1)S(1)} collective-permute-done((bf16[2,64,1280]{2,1,0:T(8,128)(2,1)S(1)}, bf16[2,64,1280]{2,1,0:T(8,128)(2,1)S(1)}, u32[]{:S(2)}, u32[]{:S(2)}) %collective-permute-start.16) | collective-permute-done | bytes 327712 | tf_op jit(solution)/shard_map/second_on_down/ppermute | solution.py:42
  62.8 1.1 collective-permute-start.19
  64.1 4.3 %expert.2 = (bf16[2,576,256]{2,1,0:T(8,128)(2,1)S(1)}, bf16[2,576,256]{2,1,0:T(8,128)(2,1)S(1)}, bf16[2,64,1280]{2,1,0:T(8,128)(2,1)S(1)}, bf16[2,64,1280]{2,1,0...) custom-call(bf16[2,64,1280]{2,1,0:T(8,128)(2,1)S(1)} %get-tuple-elem, ...), custom_call_target="tpu_custom_call" | custom-call | flops 3019898880 | bytes 12582912 | tf_op jit(solution)/shard_map/expert/pallas_call | solution.py:187
  68.5 0.8 copy-done.21
  69.3 0.4 collective-permute-start.8
  69.7 2.7 %collective-permute-start.11 = (bf16[2,64,1280]{2,1,0:T(8,128)(2,1)S(1)}, bf16[2,64,1280]{2,1,0:T(8,128)(2,1)S(1)}, u32[]{:S(2)}, u32[]{:S(2)}) collective-permute-start(bf16[2,64,1280]{2,1,0:T(8,128)(2,1)S(1)} %get-tuple-element.58), channel_id=1, source_target_pairs={{0,1},{1,2},{2,3},{3,0},{8,11},{9,8},{10,9},{11,10},{4,5},{5,6},{6... | collective-permute-start | bytes 983048 | tf_op jit(solution)/shard_map/sum_first_y_up/ppermute | solution.py:37
  72.5 4.3 %expert.3 = (bf16[2,576,256]{2,1,0:T(8,128)(2,1)S(1)}, bf16[2,576,256]{2,1,0:T(8,128)(2,1)S(1)}, bf16[2,64,1280]{2,1,0:T(8,128)(2,1)S(1)}, bf16[2,64,1280]{2,1,0...) custom-call(bf16[2,64,1280]{2,1,0:T(8,128)(2,1)S(1)} %get-tuple-elem, ...), custom_call_target="tpu_custom_call" | custom-call | flops 3019898880 | bytes 12582912 | tf_op jit(solution)/shard_map/expert/pallas_call | solution.py:187
  76.9 1.2 collective-permute-start.21
  78.1 0.8 collective-permute-start.26
  78.9 2.0 %collective-permute-start.25 = (bf16[2,64,1280]{2,1,0:T(8,128)(2,1)S(1)}, bf16[2,64,1280]{2,1,0:T(8,128)(2,1)S(1)}, u32[]{:S(2)}, u32[]{:S(2)}) collective-permute-start(bf16[2,64,1280]{2,1,0:T(8,128)(2,1)S(1)} %get-tuple-element.72), channel_id=1, source_target_pairs={{0,1},{1,2},{2,3},{3,0},{8,11},{9,8},{10,9},{11,10},{4,5},{5,6},{6... | collective-permute-start | bytes 983048 | tf_op jit(solution)/shard_map/sum_second_y_up/ppermute | solution.py:37
  81.0 2.0 %collective-permute-start.9 = (bf16[2,64,1280]{2,1,0:T(8,128)(2,1)S(1)}, bf16[2,64,1280]{2,1,0:T(8,128)(2,1)S(1)}, u32[]{:S(2)}, u32[]{:S(2)}) collective-permute-start(bf16[2,64,1280]{2,1,0:T(8,128)(2,1)S(1)} %add_convert_fusion.5), channel_id=1, source_target_pairs={{0,1},{1,2},{2,3},{3,0},{8,11},{9,8},{10,9},{11,10},{4,5},{5,6},{6... | collective-permute-start | bytes 983048 | tf_op jit(solution)/shard_map/sum_first_on_up/ppermute | solution.py:37
  83.0 1.2 collective-permute-done.12
  84.3 0.7 collective-permute-start.13
  85.1 2.9 %collective-permute-done.26 = bf16[2,64,1280]{2,1,0:T(8,128)(2,1)S(1)} collective-permute-done((bf16[2,64,1280]{2,1,0:T(8,128)(2,1)S(1)}, bf16[2,64,1280]{2,1,0:T(8,128)(2,1)S(1)}, u32[]{:S(2)}, u32[]{:S(2)}) %collective-permute-start.26) | collective-permute-done | bytes 327712 | tf_op jit(solution)/shard_map/sum_second_y_down/ppermute | solution.py:42
  88.0 0.5 collective-permute-done.25
  88.7 1.0 collective-permute-start.27
  89.7 5.9 %collective-permute-done.9 = bf16[2,64,1280]{2,1,0:T(8,128)(2,1)S(1)} collective-permute-done((bf16[2,64,1280]{2,1,0:T(8,128)(2,1)S(1)}, bf16[2,64,1280]{2,1,0:T(8,128)(2,1)S(1)}, u32[]{:S(2)}, u32[]{:S(2)}) %collective-permute-start.9) | collective-permute-done | bytes 327712 | tf_op jit(solution)/shard_map/sum_first_on_up/ppermute | solution.py:37
  95.7 3.5 %collective-permute-start.10 = (bf16[2,64,1280]{2,1,0:T(8,128)(2,1)S(1)}, bf16[2,64,1280]{2,1,0:T(8,128)(2,1)S(1)}, u32[]{:S(2)}, u32[]{:S(2)}) collective-permute-start(bf16[2,64,1280]{2,1,0:T(8,128)(2,1)S(1)} %add_convert_fusion.4), channel_id=1, source_target_pairs={{0,1},{1,2},{2,3},{3,0},{8,11},{9,8},{10,9},{11,10},{4,5},{5,6},{6... | collective-permute-start | bytes 983048 | tf_op jit(solution)/shard_map/sum_first_up/ppermute | solution.py:37
  99.5 1.3 collective-permute-start.24
  100.8 2.4 %collective-permute-done.10.refs_2_ = bf16[2,64,1280]{2,1,0:T(8,128)(2,1)S(1)} collective-permute-done((bf16[2,64,1280]{2,1,0:T(8,128)(2,1)S(1)}, bf16[2,64,1280]{2,1,0:T(8,128)(2,1)S(1)}, u32[]{:S(2)}, u32[]{:S(2)}) %collective-permute-start.10) | collective-permute-done | bytes 327712 | tf_op jit(solution)/shard_map/sum_first_up/ppermute | solution.py:37
  103.2 7.0 %collective-permute-done.23.refs_5_ = bf16[2,64,1280]{2,1,0:T(8,128)(2,1)S(1)} collective-permute-done((bf16[2,64,1280]{2,1,0:T(8,128)(2,1)S(1)}, bf16[2,64,1280]{2,1,0:T(8,128)(2,1)S(1)}, u32[]{:S(2)}, u32[]{:S(2)}) %collective-permute-start.23) | collective-permute-done | bytes 327712 | tf_op jit(solution)/shard_map/sum_second_up/ppermute | solution.py:37
  110.5 0.6 unsort_rows.1
  111.1 20.0 %all_to_all.41 = bf16[16,16,1280]{2,1,0:T(8,128)(2,1)S(1)} all-to-all(bf16[16,16,1280]{2,1,0:T(8,128)(2,1)S(1)} %bitcast.9), channel_id=1, replica_groups=mesh['yh'=2,'x'=4,'c'=2,'yl'=2,'z'=4] {'yh','x','c'}, dimensions={0} | all-to-all | bytes 1310720 | tf_op jit(solution)/shard_map/all_to_all | solution.py:287
  131.2 0.8 logits_back.1
  132.1 0.7 copy.9
  132.7 18.3 %all_to_all.42 = f32[128,1,1280]{2,1,0:T(1,128)S(1)} all-to-all(f32[128,1,1280]{2,1,0:T(1,128)S(1)} %copy.9), channel_id=1, replica_groups=mesh['yh'=2,'x'=4,'c'=2,'yl'=2,'z'=4] {'yh','x','c','yl','z'}, dimensions={0} | all-to-all | bytes 1310720 | tf_op jit(solution)/shard_map/all_to_all | solution.py:344
  151.0 0.4 reduce_sum.9
  151.4 1.2 reshape.28
  152.6 4.6 %all-to-all-start.3 = ((f32[128,1,1280]{2,1,0:T(1,128)}), f32[128,1,1280]{2,1,0:T(1,128)S(1)}, u32[]{:S(2)}, u32[]{:S(2)}) async-start(f32[128,1,1280]{2,1,0:T(1,128)} %reshape.28), calls=%async_computation.3 | async-start | bytes 1310720 | tf_op jit(solution)/shard_map/all_to_all | solution.py:347
  157.2 9.8 %weight_grads.1 = (bf16[4,576,1280]{2,1,0:T(8,128)(2,1)}, bf16[4,576,1280]{2,1,0:T(8,128)(2,1)}) custom-call(bf16[2,64,1280]{2,1,0:T(8,128)(2,1)} %copy-done.4, bf16[2,64,1280]{2,1,0:T(8,128)(2,1)} %copy-done.6, bf16[2,64,1280]{2,1,0:T(8,128)(2,1)} %copy-done.10, bf16[2,64,1280]{2,1,0:T(8,128)(2,1)} %copy-done.7, bf16[2,64,1280]{2,1,0:T(8,128)(2,1)} %copy-done.8, ...), custom_call_target="tpu_custom_call" | custom-call | flops 3019898880 | bytes 20971520 | tf_op jit(solution)/shard_map/weight_grads/pallas_call | solution.py:234
  167.0 1.4 tokens_back.1
  168.3 3.9 %all-to-all-done.3 = f32[128,1,1280]{2,1,0:T(1,128)S(1)} async-done(((f32[128,1,1280]{2,1,0:T(1,128)}), f32[128,1,1280]{2,1,0:T(1,128)S(1)}, u32[]{:S(2)}, u32[]{:S(2)}) %all-to-all-start.3) | async-done | bytes 655392 | tf_op jit(solution)/shard_map/all_to_all | solution.py:347
  172.3 0.9 copy.12
  (82 shorter events, 1.7 us)
Async XLA Ops:
  26.0 38.1 %copy-start.4 = (bf16[2,64,1280]{2,1,0:T(8,128)(2,1)}, bf16[2,64,1280]{2,1,0:T(8,128)(2,1)S(1)}, u32[]{:S(2)}) copy-start(bf16[2,64,1280]{2,1,0:T(8,128)(2,1)S(1)} %get-tuple-element.46.refs_0_) | copy-start | bytes 983044
  26.0 46.5 %copy-start.5 = (bf16[2,64,1280]{2,1,0:T(8,128)(2,1)}, bf16[2,64,1280]{2,1,0:T(8,128)(2,1)S(1)}, u32[]{:S(2)}) copy-start(bf16[2,64,1280]{2,1,0:T(8,128)(2,1)S(1)} %get-tuple-element.63.refs_0_.refs_10_) | copy-start | bytes 983044
  26.0 10.4 %collective-permute-start = (bf16[2,64,1280]{2,1,0:T(8,128)(2,1)S(1)}, bf16[2,64,1280]{2,1,0:T(8,128)(2,1)S(1)}, u32[]{:S(2)}, u32[]{:S(2)}) collective-permute-start(bf16[2,64,1280]{2,1,0:T(8,128)(2,1)S(1)} %get-tuple-element.46.refs_0_), channel_id=1, source_target_pairs={{0,1},{1,2},{2,3},{3,0},{8,11},{9,8},{10,9},{11,10},{4,5},{5,6},{6... | collective-permute-start | bytes 983048 | tf_op jit(solution)/shard_map/first_up/ppermute | solution.py:37
  29.8 10.4 %collective-permute-start.2 = (bf16[2,64,1280]{2,1,0:T(8,128)(2,1)S(1)}, bf16[2,64,1280]{2,1,0:T(8,128)(2,1)S(1)}, u32[]{:S(2)}, u32[]{:S(2)}) collective-permute-start(bf16[2,64,1280]{2,1,0:T(8,128)(2,1)S(1)} %get-tuple-element.46.refs_0_), channel_id=1, source_target_pairs={{0,3},{1,0},{2,1},{3,2},{8,9},{9,10},{10,11},{11,8},{4,7},{5,4},{6... | collective-permute-start | bytes 983048 | tf_op jit(solution)/shard_map/first_down/ppermute | solution.py:42
  29.8 14.9 %collective-permute-start.3 = (bf16[2,64,1280]{2,1,0:T(8,128)(2,1)S(1)}, bf16[2,64,1280]{2,1,0:T(8,128)(2,1)S(1)}, u32[]{:S(2)}, u32[]{:S(2)}) collective-permute-start(bf16[2,64,1280]{2,1,0:T(8,128)(2,1)S(1)} %get-tuple-element.46.refs_0_), channel_id=1, source_target_pairs={{0,4},{4,0},{1,5},{5,1},{2,6},{6,2},{3,7},{7,3},{8,12},{12,8},{9,1... | collective-permute-start | bytes 983048 | tf_op jit(solution)/shard_map/first_across/ppermute | solution.py:47
  30.2 16.1 %collective-permute-start.15 = (bf16[2,64,1280]{2,1,0:T(8,128)(2,1)S(1)}, bf16[2,64,1280]{2,1,0:T(8,128)(2,1)S(1)}, u32[]{:S(2)}, u32[]{:S(2)}) collective-permute-start(bf16[2,64,1280]{2,1,0:T(8,128)(2,1)S(1)} %get-tuple-element.63.refs_0_.refs_10_), channel_id=1, source_target_pairs={{0,3},{1,0},{2,1},{3,2},{8,9},{9,10},{10,11},{11,8},{4,7},{5,4},{6... | collective-permute-start | bytes 983048 | tf_op jit(solution)/shard_map/second_down/ppermute | solution.py:42
  36.4 27.7 %copy-start.6 = (bf16[2,64,1280]{2,1,0:T(8,128)(2,1)}, bf16[2,64,1280]{2,1,0:T(8,128)(2,1)S(1)}, u32[]{:S(2)}) copy-start(bf16[2,64,1280]{2,1,0:T(8,128)(2,1)S(1)} %collective-permute-done.refs_1_) | copy-start | bytes 983044
  36.4 10.0 %collective-permute-start.1 = (bf16[2,64,1280]{2,1,0:T(8,128)(2,1)S(1)}, bf16[2,64,1280]{2,1,0:T(8,128)(2,1)S(1)}, u32[]{:S(2)}, u32[]{:S(2)}) collective-permute-start(bf16[2,64,1280]{2,1,0:T(8,128)(2,1)S(1)} %collective-permute-done.refs_1_), channel_id=1, source_target_pairs={{0,1},{1,2},{2,3},{3,0},{8,11},{9,8},{10,9},{11,10},{4,5},{5,6},{6... | collective-permute-start | bytes 983048 | tf_op jit(solution)/shard_map/first_on_up/ppermute | solution.py:37
  39.8 8.8 %collective-permute-start.17 = (bf16[2,64,1280]{2,1,0:T(8,128)(2,1)S(1)}, bf16[2,64,1280]{2,1,0:T(8,128)(2,1)S(1)}, u32[]{:S(2)}, u32[]{:S(2)}) collective-permute-start(bf16[2,64,1280]{2,1,0:T(8,128)(2,1)S(1)} %get-tuple-element.63.refs_0_.refs_10_), channel_id=1, source_target_pairs={{0,4},{4,0},{1,5},{5,1},{2,6},{6,2},{3,7},{7,3},{8,12},{12,8},{9,1... | collective-permute-start | bytes 983048 | tf_op jit(solution)/shard_map/second_across/ppermute | solution.py:47
  40.2 23.9 %copy-start.7 = (bf16[2,64,1280]{2,1,0:T(8,128)(2,1)}, bf16[2,64,1280]{2,1,0:T(8,128)(2,1)S(1)}, u32[]{:S(2)}) copy-start(bf16[2,64,1280]{2,1,0:T(8,128)(2,1)S(1)} %collective-permute-done.2.refs_3_) | copy-start | bytes 983044
  44.7 23.7 %copy-start.8 = (bf16[2,64,1280]{2,1,0:T(8,128)(2,1)}, bf16[2,64,1280]{2,1,0:T(8,128)(2,1)S(1)}, u32[]{:S(2)}) copy-start(bf16[2,64,1280]{2,1,0:T(8,128)(2,1)S(1)} %collective-permute-done.3.refs_4_) | copy-start | bytes 983044
  44.7 7.9 %collective-permute-start.4 = (bf16[2,64,1280]{2,1,0:T(8,128)(2,1)S(1)}, bf16[2,64,1280]{2,1,0:T(8,128)(2,1)S(1)}, u32[]{:S(2)}, u32[]{:S(2)}) collective-permute-start(bf16[2,64,1280]{2,1,0:T(8,128)(2,1)S(1)} %collective-permute-done.3.refs_4_), channel_id=1, source_target_pairs={{0,1},{1,2},{2,3},{3,0},{8,11},{9,8},{10,9},{11,10},{4,5},{5,6},{6... | collective-permute-start | bytes 983048 | tf_op jit(solution)/shard_map/first_y_up/ppermute | solution.py:37
  44.8 19.1 %collective-permute-start.6 = (bf16[2,64,1280]{2,1,0:T(8,128)(2,1)S(1)}, bf16[2,64,1280]{2,1,0:T(8,128)(2,1)S(1)}, u32[]{:S(2)}, u32[]{:S(2)}) collective-permute-start(bf16[2,64,1280]{2,1,0:T(8,128)(2,1)S(1)} %collective-permute-done.3.refs_4_), channel_id=1, source_target_pairs={{0,3},{1,0},{2,1},{3,2},{8,9},{9,10},{10,11},{11,8},{4,7},{5,4},{6... | collective-permute-start | bytes 983048 | tf_op jit(solution)/shard_map/first_y_down/ppermute | solution.py:42
  46.3 26.1 %copy-start.9 = (bf16[2,64,1280]{2,1,0:T(8,128)(2,1)}, bf16[2,64,1280]{2,1,0:T(8,128)(2,1)S(1)}, u32[]{:S(2)}) copy-start(bf16[2,64,1280]{2,1,0:T(8,128)(2,1)S(1)} %collective-permute-done.15.refs_3_.refs_13_) | copy-start | bytes 983044
  46.3 16.5 %collective-permute-start.16 = (bf16[2,64,1280]{2,1,0:T(8,128)(2,1)S(1)}, bf16[2,64,1280]{2,1,0:T(8,128)(2,1)S(1)}, u32[]{:S(2)}, u32[]{:S(2)}) collective-permute-start(bf16[2,64,1280]{2,1,0:T(8,128)(2,1)S(1)} %collective-permute-done.15.refs_3_.refs_13_), channel_id=1, source_target_pairs={{0,3},{1,0},{2,1},{3,2},{8,9},{9,10},{10,11},{11,8},{4,7},{5,4},{6... | collective-permute-start | bytes 983048 | tf_op jit(solution)/shard_map/second_on_down/ppermute | solution.py:42
  46.4 22.1 %copy-start.10 = (bf16[2,64,1280]{2,1,0:T(8,128)(2,1)}, bf16[2,64,1280]{2,1,0:T(8,128)(2,1)S(1)}, u32[]{:S(2)}) copy-start(bf16[2,64,1280]{2,1,0:T(8,128)(2,1)S(1)} %collective-permute-done.1.refs_2_) | copy-start | bytes 983044
  46.4 17.7 %collective-permute-start.5 = (bf16[2,64,1280]{2,1,0:T(8,128)(2,1)S(1)}, bf16[2,64,1280]{2,1,0:T(8,128)(2,1)S(1)}, u32[]{:S(2)}, u32[]{:S(2)}) collective-permute-start(bf16[2,64,1280]{2,1,0:T(8,128)(2,1)S(1)} %collective-permute-done.1.refs_2_), channel_id=1, source_target_pairs={{0,4},{4,0},{1,5},{5,1},{2,6},{6,2},{3,7},{7,3},{8,12},{12,8},{9,1... | collective-permute-start | bytes 983048 | tf_op jit(solution)/shard_map/first_far_across/ppermute | solution.py:47
  48.6 23.9 %copy-start.11 = (bf16[2,64,1280]{2,1,0:T(8,128)(2,1)}, bf16[2,64,1280]{2,1,0:T(8,128)(2,1)S(1)}, u32[]{:S(2)}) copy-start(bf16[2,64,1280]{2,1,0:T(8,128)(2,1)S(1)} %collective-permute-done.17.refs_4_.refs_14_) | copy-start | bytes 983044
  48.6 21.2 %collective-permute-start.14 = (bf16[2,64,1280]{2,1,0:T(8,128)(2,1)S(1)}, bf16[2,64,1280]{2,1,0:T(8,128)(2,1)S(1)}, u32[]{:S(2)}, u32[]{:S(2)}) collective-permute-start(bf16[2,64,1280]{2,1,0:T(8,128)(2,1)S(1)} %get-tuple-element.63.refs_0_.refs_10_), channel_id=1, source_target_pairs={{0,1},{1,2},{2,3},{3,0},{8,11},{9,8},{10,9},{11,10},{4,5},{5,6},{6... | collective-permute-start | bytes 983048 | tf_op jit(solution)/shard_map/second_up/ppermute | solution.py:37
  52.7 15.8 %copy-start.12 = (bf16[2,64,1280]{2,1,0:T(8,128)(2,1)}, bf16[2,64,1280]{2,1,0:T(8,128)(2,1)S(1)}, u32[]{:S(2)}) copy-start(bf16[2,64,1280]{2,1,0:T(8,128)(2,1)S(1)} %collective-permute-done.4.refs_5_) | copy-start | bytes 983044
  52.7 17.1 %collective-permute-start.18 = (bf16[2,64,1280]{2,1,0:T(8,128)(2,1)S(1)}, bf16[2,64,1280]{2,1,0:T(8,128)(2,1)S(1)}, u32[]{:S(2)}, u32[]{:S(2)}) collective-permute-start(bf16[2,64,1280]{2,1,0:T(8,128)(2,1)S(1)} %collective-permute-done.17.refs_4_.refs_14_), channel_id=1, source_target_pairs={{0,1},{1,2},{2,3},{3,0},{8,11},{9,8},{10,9},{11,10},{4,5},{5,6},{6... | collective-permute-start | bytes 983048 | tf_op jit(solution)/shard_map/second_y_up/ppermute | solution.py:37
  62.8 9.6 %copy-start.14 = (bf16[2,64,1280]{2,1,0:T(8,128)(2,1)}, bf16[2,64,1280]{2,1,0:T(8,128)(2,1)S(1)}, u32[]{:S(2)}) copy-start(bf16[2,64,1280]{2,1,0:T(8,128)(2,1)S(1)} %collective-permute-done.16.refs_2_.refs_12_) | copy-start | bytes 983044
  62.8 9.6 %collective-permute-start.19 = (bf16[2,64,1280]{2,1,0:T(8,128)(2,1)S(1)}, bf16[2,64,1280]{2,1,0:T(8,128)(2,1)S(1)}, u32[]{:S(2)}, u32[]{:S(2)}) collective-permute-start(bf16[2,64,1280]{2,1,0:T(8,128)(2,1)S(1)} %collective-permute-done.16.refs_2_.refs_12_), channel_id=1, source_target_pairs={{0,4},{4,0},{1,5},{5,1},{2,6},{6,2},{3,7},{7,3},{8,12},{12,8},{9,1... | collective-permute-start | bytes 983048 | tf_op jit(solution)/shard_map/second_far_across/ppermute | solution.py:47
  63.9 8.5 %collective-permute-start.20 = (bf16[2,64,1280]{2,1,0:T(8,128)(2,1)S(1)}, bf16[2,64,1280]{2,1,0:T(8,128)(2,1)S(1)}, u32[]{:S(2)}, u32[]{:S(2)}) collective-permute-start(bf16[2,64,1280]{2,1,0:T(8,128)(2,1)S(1)} %collective-permute-done.17.refs_4_.refs_14_), channel_id=1, source_target_pairs={{0,3},{1,0},{2,1},{3,2},{8,9},{9,10},{10,11},{11,8},{4,7},{5,4},{6... | collective-permute-start | bytes 983048 | tf_op jit(solution)/shard_map/second_y_down/ppermute | solution.py:42
  69.3 7.5 %copy-start.22 = (bf16[2,576,256]{2,1,0:T(8,128)(2,1)}, bf16[2,576,256]{2,1,0:T(8,128)(2,1)S(1)}, u32[]{:S(2)}) copy-start(bf16[2,576,256]{2,1,0:T(8,128)(2,1)S(1)} %get-tuple-element.79.refs_9_) | copy-start | bytes 1769476
  69.3 8.8 %collective-permute-start.8 = (bf16[2,64,1280]{2,1,0:T(8,128)(2,1)S(1)}, bf16[2,64,1280]{2,1,0:T(8,128)(2,1)S(1)}, u32[]{:S(2)}, u32[]{:S(2)}) collective-permute-start(bf16[2,64,1280]{2,1,0:T(8,128)(2,1)S(1)} %get-tuple-element.56), channel_id=1, source_target_pairs={{0,4},{4,0},{1,5},{5,1},{2,6},{6,2},{3,7},{7,3},{8,12},{12,8},{9,1... | collective-permute-start | bytes 983048 | tf_op jit(solution)/shard_map/sum_first_far_across/ppermute | solution.py:47
  69.7 7.1 %copy-start.16 = (bf16[2,64,1280]{2,1,0:T(8,128)(2,1)}, bf16[2,64,1280]{2,1,0:T(8,128)(2,1)S(1)}, u32[]{:S(2)}) copy-start(bf16[2,64,1280]{2,1,0:T(8,128)(2,1)S(1)} %collective-permute-done.14.refs_1_.refs_11_) | copy-start | bytes 983044
  69.7 9.2 %collective-permute-start.7 = (bf16[2,64,1280]{2,1,0:T(8,128)(2,1)S(1)}, bf16[2,64,1280]{2,1,0:T(8,128)(2,1)S(1)}, u32[]{:S(2)}, u32[]{:S(2)}) collective-permute-start(bf16[2,64,1280]{2,1,0:T(8,128)(2,1)S(1)} %get-tuple-element.53), channel_id=1, source_target_pairs={{0,3},{1,0},{2,1},{3,2},{8,9},{9,10},{10,11},{11,8},{4,7},{5,4},{6... | collective-permute-start | bytes 983048 | tf_op jit(solution)/shard_map/sum_first_down/ppermute | solution.py:42
  69.7 11.2 %collective-permute-start.11 = (bf16[2,64,1280]{2,1,0:T(8,128)(2,1)S(1)}, bf16[2,64,1280]{2,1,0:T(8,128)(2,1)S(1)}, u32[]{:S(2)}, u32[]{:S(2)}) collective-permute-start(bf16[2,64,1280]{2,1,0:T(8,128)(2,1)S(1)} %get-tuple-element.58), channel_id=1, source_target_pairs={{0,1},{1,2},{2,3},{3,0},{8,11},{9,8},{10,9},{11,10},{4,5},{5,6},{6... | collective-permute-start | bytes 983048 | tf_op jit(solution)/shard_map/sum_first_y_up/ppermute | solution.py:37
  72.4 11.7 %collective-permute-start.12 = (bf16[2,64,1280]{2,1,0:T(8,128)(2,1)S(1)}, bf16[2,64,1280]{2,1,0:T(8,128)(2,1)S(1)}, u32[]{:S(2)}, u32[]{:S(2)}) collective-permute-start(bf16[2,64,1280]{2,1,0:T(8,128)(2,1)S(1)} %get-tuple-element.59), channel_id=1, source_target_pairs={{0,3},{1,0},{2,1},{3,2},{8,9},{9,10},{10,11},{11,8},{4,7},{5,4},{6... | collective-permute-start | bytes 983048 | tf_op jit(solution)/shard_map/sum_first_y_down/ppermute | solution.py:42
  76.9 55.2 %copy-start.23 = (bf16[2,576,256]{2,1,0:T(8,128)(2,1)}, bf16[2,576,256]{2,1,0:T(8,128)(2,1)S(1)}, u32[]{:S(2)}) copy-start(bf16[2,576,256]{2,1,0:T(8,128)(2,1)S(1)} %get-tuple-element.80.refs_18_) | copy-start | bytes 1769476
  76.9 55.2 %copy-start.24 = (bf16[2,576,256]{2,1,0:T(8,128)(2,1)}, bf16[2,576,256]{2,1,0:T(8,128)(2,1)S(1)}, u32[]{:S(2)}) copy-start(bf16[2,576,256]{2,1,0:T(8,128)(2,1)S(1)} %get-tuple-element.81.refs_19_) | copy-start | bytes 1769476
  76.9 54.3 %copy-start = (bf16[1,256,1280]{2,1,0:T(8,128)(2,1)S(1)}, bf16[1,256,1280]{2,1,0:T(8,128)(2,1)}, u32[]{:S(2)}) copy-start(bf16[1,256,1280]{2,1,0:T(8,128)(2,1)} %tokens.3) | copy-start | bytes 1966084
  76.9 54.3 %copy-start.1 = (bf16[1,256,1280]{2,1,0:T(8,128)(2,1)S(1)}, bf16[1,256,1280]{2,1,0:T(8,128)(2,1)}, u32[]{:S(2)}) copy-start(bf16[1,256,1280]{2,1,0:T(8,128)(2,1)} %grad_out.3) | copy-start | bytes 1966084
  76.9 54.3 %copy-start.3 = (f32[128,256]{1,0:T(8,128)S(1)}, f32[128,256]{1,0:T(8,128)}, u32[]{:S(2)}) copy-start(f32[128,256]{1,0:T(8,128)} %get-tuple-element.44.p_dispatch) | copy-start | bytes 393220
  76.9 54.3 %copy-start.20 = (f32[128,256]{1,0:T(8,128)S(1)}, f32[128,256]{1,0:T(8,128)}, u32[]{:S(2)}) copy-start(f32[128,256]{1,0:T(8,128)} %get-tuple-element.74.p_combine) | copy-start | bytes 393220
  76.9 8.1 %collective-permute-start.21 = (bf16[2,64,1280]{2,1,0:T(8,128)(2,1)S(1)}, bf16[2,64,1280]{2,1,0:T(8,128)(2,1)S(1)}, u32[]{:S(2)}, u32[]{:S(2)}) collective-permute-start(bf16[2,64,1280]{2,1,0:T(8,128)(2,1)S(1)} %get-tuple-element.68), channel_id=1, source_target_pairs={{0,4},{4,0},{1,5},{5,1},{2,6},{6,2},{3,7},{7,3},{8,12},{12,8},{9,1... | collective-permute-start | bytes 983048 | tf_op jit(solution)/shard_map/sum_second_far_across/ppermute | solution.py:47
  78.1 10.0 %collective-permute-start.26 = (bf16[2,64,1280]{2,1,0:T(8,128)(2,1)S(1)}, bf16[2,64,1280]{2,1,0:T(8,128)(2,1)S(1)}, u32[]{:S(2)}, u32[]{:S(2)}) collective-permute-start(bf16[2,64,1280]{2,1,0:T(8,128)(2,1)S(1)} %get-tuple-element.73), channel_id=1, source_target_pairs={{0,3},{1,0},{2,1},{3,2},{8,9},{9,10},{10,11},{11,8},{4,7},{5,4},{6... | collective-permute-start | bytes 983048 | tf_op jit(solution)/shard_map/sum_second_y_down/ppermute | solution.py:42
  78.9 9.6 %collective-permute-start.25 = (bf16[2,64,1280]{2,1,0:T(8,128)(2,1)S(1)}, bf16[2,64,1280]{2,1,0:T(8,128)(2,1)S(1)}, u32[]{:S(2)}, u32[]{:S(2)}) collective-permute-start(bf16[2,64,1280]{2,1,0:T(8,128)(2,1)S(1)} %get-tuple-element.72), channel_id=1, source_target_pairs={{0,1},{1,2},{2,3},{3,0},{8,11},{9,8},{10,9},{11,10},{4,5},{5,6},{6... | collective-permute-start | bytes 983048 | tf_op jit(solution)/shard_map/sum_second_y_up/ppermute | solution.py:37
  81.0 14.6 %collective-permute-start.9 = (bf16[2,64,1280]{2,1,0:T(8,128)(2,1)S(1)}, bf16[2,64,1280]{2,1,0:T(8,128)(2,1)S(1)}, u32[]{:S(2)}, u32[]{:S(2)}) collective-permute-start(bf16[2,64,1280]{2,1,0:T(8,128)(2,1)S(1)} %add_convert_fusion.5), channel_id=1, source_target_pairs={{0,1},{1,2},{2,3},{3,0},{8,11},{9,8},{10,9},{11,10},{4,5},{5,6},{6... | collective-permute-start | bytes 983048 | tf_op jit(solution)/shard_map/sum_first_on_up/ppermute | solution.py:37
  84.3 16.5 %collective-permute-start.13 = (bf16[2,64,1280]{2,1,0:T(8,128)(2,1)S(1)}, bf16[2,64,1280]{2,1,0:T(8,128)(2,1)S(1)}, u32[]{:S(2)}, u32[]{:S(2)}) collective-permute-start(bf16[2,64,1280]{2,1,0:T(8,128)(2,1)S(1)} %add_convert_fusion.3), channel_id=1, source_target_pairs={{0,4},{4,0},{1,5},{5,1},{2,6},{6,2},{3,7},{7,3},{8,12},{12,8},{9,1... | collective-permute-start | bytes 983048 | tf_op jit(solution)/shard_map/sum_first_across/ppermute | solution.py:47
  85.1 14.1 %collective-permute-start.22 = (bf16[2,64,1280]{2,1,0:T(8,128)(2,1)S(1)}, bf16[2,64,1280]{2,1,0:T(8,128)(2,1)S(1)}, u32[]{:S(2)}, u32[]{:S(2)}) collective-permute-start(bf16[2,64,1280]{2,1,0:T(8,128)(2,1)S(1)} %add_convert_fusion.2), channel_id=1, source_target_pairs={{0,3},{1,0},{2,1},{3,2},{8,9},{9,10},{10,11},{11,8},{4,7},{5,4},{6... | collective-permute-start | bytes 983048 | tf_op jit(solution)/shard_map/sum_second_on_down/ppermute | solution.py:42
  88.7 12.1 %collective-permute-start.27 = (bf16[2,64,1280]{2,1,0:T(8,128)(2,1)S(1)}, bf16[2,64,1280]{2,1,0:T(8,128)(2,1)S(1)}, u32[]{:S(2)}, u32[]{:S(2)}) collective-permute-start(bf16[2,64,1280]{2,1,0:T(8,128)(2,1)S(1)} %add_convert_fusion), channel_id=1, source_target_pairs={{0,4},{4,0},{1,5},{5,1},{2,6},{6,2},{3,7},{7,3},{8,12},{12,8},{9,1... | collective-permute-start | bytes 983048 | tf_op jit(solution)/shard_map/sum_second_across/ppermute | solution.py:47
  95.7 7.5 %collective-permute-start.10 = (bf16[2,64,1280]{2,1,0:T(8,128)(2,1)S(1)}, bf16[2,64,1280]{2,1,0:T(8,128)(2,1)S(1)}, u32[]{:S(2)}, u32[]{:S(2)}) collective-permute-start(bf16[2,64,1280]{2,1,0:T(8,128)(2,1)S(1)} %add_convert_fusion.4), channel_id=1, source_target_pairs={{0,1},{1,2},{2,3},{3,0},{8,11},{9,8},{10,9},{11,10},{4,5},{5,6},{6... | collective-permute-start | bytes 983048 | tf_op jit(solution)/shard_map/sum_first_up/ppermute | solution.py:37
  99.2 11.0 %collective-permute-start.23 = (bf16[2,64,1280]{2,1,0:T(8,128)(2,1)S(1)}, bf16[2,64,1280]{2,1,0:T(8,128)(2,1)S(1)}, u32[]{:S(2)}, u32[]{:S(2)}) collective-permute-start(bf16[2,64,1280]{2,1,0:T(8,128)(2,1)S(1)} %get-tuple-element.69), channel_id=1, source_target_pairs={{0,1},{1,2},{2,3},{3,0},{8,11},{9,8},{10,9},{11,10},{4,5},{5,6},{6... | collective-permute-start | bytes 983048 | tf_op jit(solution)/shard_map/sum_second_up/ppermute | solution.py:37
  99.5 11.0 %collective-permute-start.24 = (bf16[2,64,1280]{2,1,0:T(8,128)(2,1)S(1)}, bf16[2,64,1280]{2,1,0:T(8,128)(2,1)S(1)}, u32[]{:S(2)}, u32[]{:S(2)}) collective-permute-start(bf16[2,64,1280]{2,1,0:T(8,128)(2,1)S(1)} %add_convert_fusion.1), channel_id=1, source_target_pairs={{0,3},{1,0},{2,1},{3,2},{8,9},{9,10},{10,11},{11,8},{4,7},{5,4},{6... | collective-permute-start | bytes 983048 | tf_op jit(solution)/shard_map/sum_second_down/ppermute | solution.py:42
  152.6 19.7 %all-to-all-start.3 = ((f32[128,1,1280]{2,1,0:T(1,128)}), f32[128,1,1280]{2,1,0:T(1,128)S(1)}, u32[]{:S(2)}, u32[]{:S(2)}) async-start(f32[128,1,1280]{2,1,0:T(1,128)} %reshape.28), calls=%async_computation.3 | async-start | bytes 1310720 | tf_op jit(solution)/shard_map/all_to_all | solution.py:347
  157.2 9.8 %copy-start.2 = (bf16[128,1280]{1,0:T(8,128)(2,1)S(1)}, bf16[128,1280]{1,0:T(8,128)(2,1)}, u32[]{:S(2)}) copy-start(bf16[128,1280]{1,0:T(8,128)(2,1)} %slot_params.3) | copy-start | bytes 983044
  (6 other events, 25.7 us)

commit v6 on v5

--- a/solution.py
+++ b/solution.py
@@ -136,12 +136,13 @@
     low1, high1, y1 = up(first, "first"), down(first, "first"), across(first, "first")
     low2, high2, y2 = up(second, "second"), down(second, "second"), across(second, "second")
     far1, far2 = up(low1, "first_on"), down(high2, "second_on")
-    weights = stage(*after((w_in, w_out), (low1, high1)))
+    (y1,) = after((y1,), (high1,))
     y_low1, y_high1 = up(y1, "first_y"), down(y1, "first_y")
-    (sent,) = after((far1,), weights)
-    one = (first, low1, far1, high1, y1, y_low1, across(sent, "first_far"), y_high1)
+    weights = stage(*after((w_in, w_out), (y_low1,)))
+    one = (first, low1, far1, high1, y1, y_low1, across(far1, "first_far"), y_high1)
     (y2,) = after((y2,), (far1,))
     y_low2, y_high2 = up(y2, "second_y"), down(y2, "second_y")
+    (far2,) = after((far2,), weights)
     two = (second, low2, far2, high2, y2, y_low2, across(far2, "second_far"), y_high2)
     return one, two, weights
 

time: 174 us -> 167 us (0.960)
  waiting for transfers between devices: 43.6 us -> 35 us
    ppermute x10, waiting for transfers between devices: 13.8 us -> 3.9 us  [down(): lax.ppermute(value, ('c', 'z'), [turn(c, z, -1) for c in range(2) for z i...]
    ppermute x10, starting transfers between devices: 19.9 us -> 22.2 us  [up(): lax.ppermute(value, ('c', 'z'), [turn(c, z, 1) for c in range(2) for z in...]
    ppermute x10, waiting for transfers between devices: 24.7 us -> 26.6 us  [up(): lax.ppermute(value, ('c', 'z'), [turn(c, z, 1) for c in range(2) for z in...]
  transfers between devices with their start and end apart: 29 -> 29, of which waited for: 12 -> 12; matrix products, arithmetic and copies ran while one was open for 0% -> 0% of each run, Pallas kernels for 14% -> 15%
where the time goes in v6:
time: 167 us
  blocking collectives  61.2 us (37%)
  starting transfers between devices  36.2 us (22%)
  waiting for transfers between devices  35 us (21%)
  Pallas kernels  29.4 us (18%)
  local copies, waits for them, and re-layouts  2.84 us (2%)
    all_to_all x2, blocking collectives, exchange(): return lax.all_to_all(rows, EXPERT, split_axis=0, concat_axis=0, tiled=True)  42.9 us
    ppermute x10, waiting for transfers between devices, up(): lax.ppermute(value, ('c', 'z'), [turn(c, z, 1) for c in range(2) for z in...  26.6 us
    ppermute x10, starting transfers between devices, up(): lax.ppermute(value, ('c', 'z'), [turn(c, z, 1) for c in range(2) for z in...  22.2 us
    all_to_all x1, blocking collectives, sum_over_all(): lax.all_to_all(value, NAMES, split_axis=0, concat_axis=0, tiled=True)  18.3 us
    pallas_call x1, Pallas kernels, weight_grads(): pl.pallas_call(functools.partial(weights_kernel, half), grid=(2 * half,),...  9.77 us
    pallas_call x2, Pallas kernels, expert_call(): pl.pallas_call(expert_kernel, grid=(count,), in_specs=[per_expert(block,...  8.67 us
    ppermute x8, starting transfers between devices, across(): return lax.ppermute(value, 'yl', SWAP)  4.86 us
    all_to_all x1, starting transfers between devices, sum_over_all(): lax.all_to_all(copies, NAMES, split_axis=0, concat_axis=0, tiled=True)  4.58 us
  transfers between devices with their start and end apart: 29, of which 12 were waited for; matrix products, arithmetic and copies ran while one was open for 0% of the time, Pallas kernels for 15%

profile of v6, /device:TPU:1, one launch (start us, length us, event | category | flops | bytes accessed | tf_op | source)
XLA Modules:
  0.0 166.7 jit_solution(6270399563269327567)
XLA Ops:
  0.6 3.3 %route.1 = (bf16[256,1280]{1,0:T(8,128)(2,1)}, f32[128,256]{1,0:T(8,128)}, f32[128,256]{1,0:T(8,128)}) custom-call(bf16[1,256,1280]{2,1,0:T(8,128)(2,1)} %tokens.3, bf16[128,1280]{1,0:T(8,128)(2,1)} %slot_params.3, bf16[1,256,1280]{2,1,0:T(8,128)(2,1)} %grad_out.3), custom_call_target="tpu_custom_call" | custom-call | tf_op jit(solution)/shard_map/route/pallas_call | solution.py:81
  3.9 21.6 %all_to_all.40 = bf16[16,16,1280]{2,1,0:T(8,128)(2,1)S(1)} all-to-all(bf16[16,16,1280]{2,1,0:T(8,128)(2,1)} %bitcast.13), channel_id=1, replica_groups=mesh['yh'=2,'x'=4,'c'=2,'yl'=2,'z'=4] {'yh','x','c'}, dimensions={0} | all-to-all | bytes 1310720 | tf_op jit(solution)/shard_map/all_to_all | solution.py:288
  25.6 0.3 sort_rows.1
  26.0 3.8 %collective-permute-start = (bf16[2,64,1280]{2,1,0:T(8,128)(2,1)S(1)}, bf16[2,64,1280]{2,1,0:T(8,128)(2,1)S(1)}, u32[]{:S(2)}, u32[]{:S(2)}) collective-permute-start(bf16[2,64,1280]{2,1,0:T(8,128)(2,1)S(1)} %get-tuple-element.47.refs_0_), channel_id=1, source_target_pairs={{0,1},{1,2},{2,3},{3,0},{8,11},{9,8},{10,9},{11,10},{4,5},{5,6},{6... | collective-permute-start | bytes 983048 | tf_op jit(solution)/shard_map/first_up/ppermute | solution.py:37
  29.8 0.4 collective-permute-start.3
  30.2 6.2 %collective-permute-done.refs_1_ = bf16[2,64,1280]{2,1,0:T(8,128)(2,1)S(1)} collective-permute-done((bf16[2,64,1280]{2,1,0:T(8,128)(2,1)S(1)}, bf16[2,64,1280]{2,1,0:T(8,128)(2,1)S(1)}, u32[]{:S(2)}, u32[]{:S(2)}) %collective-permute-start) | collective-permute-done | bytes 327712 | tf_op jit(solution)/shard_map/first_up/ppermute | solution.py:37
  36.4 3.4 %collective-permute-start.1 = (bf16[2,64,1280]{2,1,0:T(8,128)(2,1)S(1)}, bf16[2,64,1280]{2,1,0:T(8,128)(2,1)S(1)}, u32[]{:S(2)}, u32[]{:S(2)}) collective-permute-start(bf16[2,64,1280]{2,1,0:T(8,128)(2,1)S(1)} %collective-permute-done.refs_1_), channel_id=1, source_target_pairs={{0,1},{1,2},{2,3},{3,0},{8,11},{9,8},{10,9},{11,10},{4,5},{5,6},{6... | collective-permute-start | bytes 983048 | tf_op jit(solution)/shard_map/first_on_up/ppermute | solution.py:37
  39.8 2.2 %collective-permute-start.4 = (bf16[2,64,1280]{2,1,0:T(8,128)(2,1)S(1)}, bf16[2,64,1280]{2,1,0:T(8,128)(2,1)S(1)}, u32[]{:S(2)}, u32[]{:S(2)}) collective-permute-start(bf16[2,64,1280]{2,1,0:T(8,128)(2,1)S(1)} %collective-permute-done.3.refs_4_), channel_id=1, source_target_pairs={{0,1},{1,2},{2,3},{3,0},{8,11},{9,8},{10,9},{11,10},{4,5},{5,6},{6... | collective-permute-start | bytes 983048 | tf_op jit(solution)/shard_map/first_y_up/ppermute | solution.py:37
  42.0 0.4 collective-permute-start.17
  42.6 1.7 %collective-permute-done.1.refs_2_ = bf16[2,64,1280]{2,1,0:T(8,128)(2,1)S(1)} collective-permute-done((bf16[2,64,1280]{2,1,0:T(8,128)(2,1)S(1)}, bf16[2,64,1280]{2,1,0:T(8,128)(2,1)S(1)}, u32[]{:S(2)}, u32[]{:S(2)}) %collective-permute-start.1) | collective-permute-done | bytes 327712 | tf_op jit(solution)/shard_map/first_on_up/ppermute | solution.py:37
  44.4 0.4 collective-permute-start.5
  44.8 4.8 %collective-permute-done.4.refs_5_ = bf16[2,64,1280]{2,1,0:T(8,128)(2,1)S(1)} collective-permute-done((bf16[2,64,1280]{2,1,0:T(8,128)(2,1)S(1)}, bf16[2,64,1280]{2,1,0:T(8,128)(2,1)S(1)}, u32[]{:S(2)}, u32[]{:S(2)}) %collective-permute-start.4) | collective-permute-done | bytes 327712 | tf_op jit(solution)/shard_map/first_y_up/ppermute | solution.py:37
  49.6 3.4 %collective-permute-start.14 = (bf16[2,64,1280]{2,1,0:T(8,128)(2,1)S(1)}, bf16[2,64,1280]{2,1,0:T(8,128)(2,1)S(1)}, u32[]{:S(2)}, u32[]{:S(2)}) collective-permute-start(bf16[2,64,1280]{2,1,0:T(8,128)(2,1)S(1)} %get-tuple-element.64.refs_0_.refs_10_), channel_id=1, source_target_pairs={{0,1},{1,2},{2,3},{3,0},{8,11},{9,8},{10,9},{11,10},{4,5},{5,6},{6... | collective-permute-start | bytes 983048 | tf_op jit(solution)/shard_map/second_up/ppermute | solution.py:37
  53.1 4.5 %stage.1 = (bf16[4,576,1280]{2,1,0:T(8,128)(2,1)S(1)}, bf16[4,576,1280]{2,1,0:T(8,128)(2,1)S(1)}) custom-call(bf16[4,576,1280]{2,1,0:T(8,128)(2,1)} %w_in, bf16[4,576,1280]{2,1,0:T(8,128)(2,1)} %w_out), custom_call_target="tpu_custom_call" | custom-call | tf_op jit(solution)/shard_map/stage/pallas_call | solution.py:124
  57.6 0.5 collective-permute-start.19
  58.0 1.3 collective-permute-start.20
  59.4 4.3 %expert.2 = (bf16[2,576,256]{2,1,0:T(8,128)(2,1)S(1)}, bf16[2,576,256]{2,1,0:T(8,128)(2,1)S(1)}, bf16[2,64,1280]{2,1,0:T(8,128)(2,1)S(1)}, bf16[2,64,1280]{2,1,0...) custom-call(bf16[2,64,1280]{2,1,0:T(8,128)(2,1)S(1)} %get-tuple-elem, ...), custom_call_target="tpu_custom_call" | custom-call | flops 3019898880 | bytes 12582912 | tf_op jit(solution)/shard_map/expert/pallas_call | solution.py:188
  63.8 1.1 collective-permute-start.8
  65.0 2.7 %collective-permute-start.11 = (bf16[2,64,1280]{2,1,0:T(8,128)(2,1)S(1)}, bf16[2,64,1280]{2,1,0:T(8,128)(2,1)S(1)}, u32[]{:S(2)}, u32[]{:S(2)}) collective-permute-start(bf16[2,64,1280]{2,1,0:T(8,128)(2,1)S(1)} %get-tuple-element.59), channel_id=1, source_target_pairs={{0,1},{1,2},{2,3},{3,0},{8,11},{9,8},{10,9},{11,10},{4,5},{5,6},{6... | collective-permute-start | bytes 983048 | tf_op jit(solution)/shard_map/sum_first_y_up/ppermute | solution.py:37
  68.0 4.3 %expert.3 = (bf16[2,576,256]{2,1,0:T(8,128)(2,1)S(1)}, bf16[2,576,256]{2,1,0:T(8,128)(2,1)S(1)}, bf16[2,64,1280]{2,1,0:T(8,128)(2,1)S(1)}, bf16[2,64,1280]{2,1,0...) custom-call(bf16[2,64,1280]{2,1,0:T(8,128)(2,1)S(1)} %get-tuple-elem, ...), custom_call_target="tpu_custom_call" | custom-call | flops 3019898880 | bytes 12582912 | tf_op jit(solution)/shard_map/expert/pallas_call | solution.py:188
  72.5 0.5 collective-permute-start.21
  73.0 0.7 collective-permute-start.26
  73.8 2.0 %collective-permute-start.25 = (bf16[2,64,1280]{2,1,0:T(8,128)(2,1)S(1)}, bf16[2,64,1280]{2,1,0:T(8,128)(2,1)S(1)}, u32[]{:S(2)}, u32[]{:S(2)}) collective-permute-start(bf16[2,64,1280]{2,1,0:T(8,128)(2,1)S(1)} %get-tuple-element.74), channel_id=1, source_target_pairs={{0,1},{1,2},{2,3},{3,0},{8,11},{9,8},{10,9},{11,10},{4,5},{5,6},{6... | collective-permute-start | bytes 983048 | tf_op jit(solution)/shard_map/sum_second_y_up/ppermute | solution.py:37
  75.8 1.1 collective-permute-start.9
  77.0 0.6 collective-permute-done.12
  77.7 0.6 collective-permute-start.13
  78.2 0.6 collective-permute-done.21
  78.9 0.8 collective-permute-start.22
  79.7 3.0 %collective-permute-done.26 = bf16[2,64,1280]{2,1,0:T(8,128)(2,1)S(1)} collective-permute-done((bf16[2,64,1280]{2,1,0:T(8,128)(2,1)S(1)}, bf16[2,64,1280]{2,1,0:T(8,128)(2,1)S(1)}, u32[]{:S(2)}, u32[]{:S(2)}) %collective-permute-start.26) | collective-permute-done | bytes 327712 | tf_op jit(solution)/shard_map/sum_second_y_down/ppermute | solution.py:42
  82.7 0.8 collective-permute-done.25
  83.5 1.0 collective-permute-start.27
  84.5 4.9 %collective-permute-done.9 = bf16[2,64,1280]{2,1,0:T(8,128)(2,1)S(1)} collective-permute-done((bf16[2,64,1280]{2,1,0:T(8,128)(2,1)S(1)}, bf16[2,64,1280]{2,1,0:T(8,128)(2,1)S(1)}, u32[]{:S(2)}, u32[]{:S(2)}) %collective-permute-start.9) | collective-permute-done | bytes 327712 | tf_op jit(solution)/shard_map/sum_first_on_up/ppermute | solution.py:37
  89.5 3.4 %collective-permute-start.10 = (bf16[2,64,1280]{2,1,0:T(8,128)(2,1)S(1)}, bf16[2,64,1280]{2,1,0:T(8,128)(2,1)S(1)}, u32[]{:S(2)}, u32[]{:S(2)}) collective-permute-start(bf16[2,64,1280]{2,1,0:T(8,128)(2,1)S(1)} %add_convert_fusion.4), channel_id=1, source_target_pairs={{0,1},{1,2},{2,3},{3,0},{8,11},{9,8},{10,9},{11,10},{4,5},{5,6},{6... | collective-permute-start | bytes 983048 | tf_op jit(solution)/shard_map/sum_first_up/ppermute | solution.py:37
  93.1 1.4 collective-permute-start.24
  94.5 4.0 %collective-permute-done.10.refs_2_ = bf16[2,64,1280]{2,1,0:T(8,128)(2,1)S(1)} collective-permute-done((bf16[2,64,1280]{2,1,0:T(8,128)(2,1)S(1)}, bf16[2,64,1280]{2,1,0:T(8,128)(2,1)S(1)}, u32[]{:S(2)}, u32[]{:S(2)}) %collective-permute-start.10) | collective-permute-done | bytes 327712 | tf_op jit(solution)/shard_map/sum_first_up/ppermute | solution.py:37
  98.6 4.2 %collective-permute-done.23.refs_5_ = bf16[2,64,1280]{2,1,0:T(8,128)(2,1)S(1)} collective-permute-done((bf16[2,64,1280]{2,1,0:T(8,128)(2,1)S(1)}, bf16[2,64,1280]{2,1,0:T(8,128)(2,1)S(1)}, u32[]{:S(2)}, u32[]{:S(2)}) %collective-permute-start.23) | collective-permute-done | bytes 327712 | tf_op jit(solution)/shard_map/sum_second_up/ppermute | solution.py:37
  102.8 0.6 unsort_rows.1
  103.4 21.3 %all_to_all.41 = bf16[16,16,1280]{2,1,0:T(8,128)(2,1)S(1)} all-to-all(bf16[16,16,1280]{2,1,0:T(8,128)(2,1)S(1)} %bitcast.9), channel_id=1, replica_groups=mesh['yh'=2,'x'=4,'c'=2,'yl'=2,'z'=4] {'yh','x','c'}, dimensions={0} | all-to-all | bytes 1310720 | tf_op jit(solution)/shard_map/all_to_all | solution.py:288
  124.7 0.8 logits_back.1
  125.6 0.7 copy.9
  126.2 18.3 %all_to_all.42 = f32[128,1,1280]{2,1,0:T(1,128)S(1)} all-to-all(f32[128,1,1280]{2,1,0:T(1,128)S(1)} %copy.9), channel_id=1, replica_groups=mesh['yh'=2,'x'=4,'c'=2,'yl'=2,'z'=4] {'yh','x','c','yl','z'}, dimensions={0} | all-to-all | bytes 1310720 | tf_op jit(solution)/shard_map/all_to_all | solution.py:345
  144.5 0.4 reduce_sum.9
  145.0 1.2 reshape.28
  146.1 4.6 %all-to-all-start.3 = ((f32[128,1,1280]{2,1,0:T(1,128)}), f32[128,1,1280]{2,1,0:T(1,128)S(1)}, u32[]{:S(2)}, u32[]{:S(2)}) async-start(f32[128,1,1280]{2,1,0:T(1,128)} %reshape.28), calls=%async_computation.3 | async-start | bytes 1310720 | tf_op jit(solution)/shard_map/all_to_all | solution.py:348
  150.7 9.8 %weight_grads.1 = (bf16[4,576,1280]{2,1,0:T(8,128)(2,1)}, bf16[4,576,1280]{2,1,0:T(8,128)(2,1)}) custom-call(bf16[2,64,1280]{2,1,0:T(8,128)(2,1)} %copy-done.4, bf16[2,64,1280]{2,1,0:T(8,128)(2,1)} %copy-done.6, bf16[2,64,1280]{2,1,0:T(8,128)(2,1)} %copy-done.10, bf16[2,64,1280]{2,1,0:T(8,128)(2,1)} %copy-done.7, bf16[2,64,1280]{2,1,0:T(8,128)(2,1)} %copy-done.8, ...), custom_call_target="tpu_custom_call" | custom-call | flops 3019898880 | bytes 20971520 | tf_op jit(solution)/shard_map/weight_grads/pallas_call | solution.py:235
  160.5 1.4 tokens_back.1
  161.9 3.9 %all-to-all-done.3 = f32[128,1,1280]{2,1,0:T(1,128)S(1)} async-done(((f32[128,1,1280]{2,1,0:T(1,128)}), f32[128,1,1280]{2,1,0:T(1,128)S(1)}, u32[]{:S(2)}, u32[]{:S(2)}) %all-to-all-start.3) | async-done | bytes 655392 | tf_op jit(solution)/shard_map/all_to_all | solution.py:348
  165.8 0.9 copy.12
  (82 shorter events, 1.5 us)
Async XLA Ops:
  26.0 33.4 %copy-start.4 = (bf16[2,64,1280]{2,1,0:T(8,128)(2,1)}, bf16[2,64,1280]{2,1,0:T(8,128)(2,1)S(1)}, u32[]{:S(2)}) copy-start(bf16[2,64,1280]{2,1,0:T(8,128)(2,1)S(1)} %get-tuple-element.47.refs_0_) | copy-start | bytes 983044
  26.0 42.1 %copy-start.5 = (bf16[2,64,1280]{2,1,0:T(8,128)(2,1)}, bf16[2,64,1280]{2,1,0:T(8,128)(2,1)S(1)}, u32[]{:S(2)}) copy-start(bf16[2,64,1280]{2,1,0:T(8,128)(2,1)S(1)} %get-tuple-element.64.refs_0_.refs_10_) | copy-start | bytes 983044
  26.0 10.4 %collective-permute-start = (bf16[2,64,1280]{2,1,0:T(8,128)(2,1)S(1)}, bf16[2,64,1280]{2,1,0:T(8,128)(2,1)S(1)}, u32[]{:S(2)}, u32[]{:S(2)}) collective-permute-start(bf16[2,64,1280]{2,1,0:T(8,128)(2,1)S(1)} %get-tuple-element.47.refs_0_), channel_id=1, source_target_pairs={{0,1},{1,2},{2,3},{3,0},{8,11},{9,8},{10,9},{11,10},{4,5},{5,6},{6... | collective-permute-start | bytes 983048 | tf_op jit(solution)/shard_map/first_up/ppermute | solution.py:37
  29.8 10.0 %collective-permute-start.2 = (bf16[2,64,1280]{2,1,0:T(8,128)(2,1)S(1)}, bf16[2,64,1280]{2,1,0:T(8,128)(2,1)S(1)}, u32[]{:S(2)}, u32[]{:S(2)}) collective-permute-start(bf16[2,64,1280]{2,1,0:T(8,128)(2,1)S(1)} %get-tuple-element.47.refs_0_), channel_id=1, source_target_pairs={{0,3},{1,0},{2,1},{3,2},{8,9},{9,10},{10,11},{11,8},{4,7},{5,4},{6... | collective-permute-start | bytes 983048 | tf_op jit(solution)/shard_map/first_down/ppermute | solution.py:42
  29.8 10.0 %collective-permute-start.3 = (bf16[2,64,1280]{2,1,0:T(8,128)(2,1)S(1)}, bf16[2,64,1280]{2,1,0:T(8,128)(2,1)S(1)}, u32[]{:S(2)}, u32[]{:S(2)}) collective-permute-start(bf16[2,64,1280]{2,1,0:T(8,128)(2,1)S(1)} %get-tuple-element.47.refs_0_), channel_id=1, source_target_pairs={{0,4},{4,0},{1,5},{5,1},{2,6},{6,2},{3,7},{7,3},{8,12},{12,8},{9,1... | collective-permute-start | bytes 983048 | tf_op jit(solution)/shard_map/first_across/ppermute | solution.py:47
  30.2 12.2 %collective-permute-start.15 = (bf16[2,64,1280]{2,1,0:T(8,128)(2,1)S(1)}, bf16[2,64,1280]{2,1,0:T(8,128)(2,1)S(1)}, u32[]{:S(2)}, u32[]{:S(2)}) collective-permute-start(bf16[2,64,1280]{2,1,0:T(8,128)(2,1)S(1)} %get-tuple-element.64.refs_0_.refs_10_), channel_id=1, source_target_pairs={{0,3},{1,0},{2,1},{3,2},{8,9},{9,10},{10,11},{11,8},{4,7},{5,4},{6... | collective-permute-start | bytes 983048 | tf_op jit(solution)/shard_map/second_down/ppermute | solution.py:42
  36.4 23.0 %copy-start.6 = (bf16[2,64,1280]{2,1,0:T(8,128)(2,1)}, bf16[2,64,1280]{2,1,0:T(8,128)(2,1)S(1)}, u32[]{:S(2)}) copy-start(bf16[2,64,1280]{2,1,0:T(8,128)(2,1)S(1)} %collective-permute-done.refs_1_) | copy-start | bytes 983044
  36.4 8.0 %collective-permute-start.1 = (bf16[2,64,1280]{2,1,0:T(8,128)(2,1)S(1)}, bf16[2,64,1280]{2,1,0:T(8,128)(2,1)S(1)}, u32[]{:S(2)}, u32[]{:S(2)}) collective-permute-start(bf16[2,64,1280]{2,1,0:T(8,128)(2,1)S(1)} %collective-permute-done.refs_1_), channel_id=1, source_target_pairs={{0,1},{1,2},{2,3},{3,0},{8,11},{9,8},{10,9},{11,10},{4,5},{5,6},{6... | collective-permute-start | bytes 983048 | tf_op jit(solution)/shard_map/first_on_up/ppermute | solution.py:37
  39.8 19.6 %copy-start.7 = (bf16[2,64,1280]{2,1,0:T(8,128)(2,1)}, bf16[2,64,1280]{2,1,0:T(8,128)(2,1)S(1)}, u32[]{:S(2)}) copy-start(bf16[2,64,1280]{2,1,0:T(8,128)(2,1)S(1)} %collective-permute-done.2.refs_3_) | copy-start | bytes 983044
  39.8 19.6 %copy-start.8 = (bf16[2,64,1280]{2,1,0:T(8,128)(2,1)}, bf16[2,64,1280]{2,1,0:T(8,128)(2,1)S(1)}, u32[]{:S(2)}) copy-start(bf16[2,64,1280]{2,1,0:T(8,128)(2,1)S(1)} %collective-permute-done.3.refs_4_) | copy-start | bytes 983044
  39.8 9.8 %collective-permute-start.4 = (bf16[2,64,1280]{2,1,0:T(8,128)(2,1)S(1)}, bf16[2,64,1280]{2,1,0:T(8,128)(2,1)S(1)}, u32[]{:S(2)}, u32[]{:S(2)}) collective-permute-start(bf16[2,64,1280]{2,1,0:T(8,128)(2,1)S(1)} %collective-permute-done.3.refs_4_), channel_id=1, source_target_pairs={{0,1},{1,2},{2,3},{3,0},{8,11},{9,8},{10,9},{11,10},{4,5},{5,6},{6... | collective-permute-start | bytes 983048 | tf_op jit(solution)/shard_map/first_y_up/ppermute | solution.py:37
  42.0 11.0 %collective-permute-start.17 = (bf16[2,64,1280]{2,1,0:T(8,128)(2,1)S(1)}, bf16[2,64,1280]{2,1,0:T(8,128)(2,1)S(1)}, u32[]{:S(2)}, u32[]{:S(2)}) collective-permute-start(bf16[2,64,1280]{2,1,0:T(8,128)(2,1)S(1)} %get-tuple-element.64.refs_0_.refs_10_), channel_id=1, source_target_pairs={{0,4},{4,0},{1,5},{5,1},{2,6},{6,2},{3,7},{7,3},{8,12},{12,8},{9,1... | collective-permute-start | bytes 983048 | tf_op jit(solution)/shard_map/second_across/ppermute | solution.py:47
  42.4 25.6 %copy-start.9 = (bf16[2,64,1280]{2,1,0:T(8,128)(2,1)}, bf16[2,64,1280]{2,1,0:T(8,128)(2,1)S(1)}, u32[]{:S(2)}) copy-start(bf16[2,64,1280]{2,1,0:T(8,128)(2,1)S(1)} %collective-permute-done.15.refs_3_.refs_13_) | copy-start | bytes 983044
  42.4 15.2 %collective-permute-start.16 = (bf16[2,64,1280]{2,1,0:T(8,128)(2,1)S(1)}, bf16[2,64,1280]{2,1,0:T(8,128)(2,1)S(1)}, u32[]{:S(2)}, u32[]{:S(2)}) collective-permute-start(bf16[2,64,1280]{2,1,0:T(8,128)(2,1)S(1)} %collective-permute-done.15.refs_3_.refs_13_), channel_id=1, source_target_pairs={{0,3},{1,0},{2,1},{3,2},{8,9},{9,10},{10,11},{11,8},{4,7},{5,4},{6... | collective-permute-start | bytes 983048 | tf_op jit(solution)/shard_map/second_on_down/ppermute | solution.py:42
  42.4 15.6 %collective-permute-start.6 = (bf16[2,64,1280]{2,1,0:T(8,128)(2,1)S(1)}, bf16[2,64,1280]{2,1,0:T(8,128)(2,1)S(1)}, u32[]{:S(2)}, u32[]{:S(2)}) collective-permute-start(bf16[2,64,1280]{2,1,0:T(8,128)(2,1)S(1)} %collective-permute-done.3.refs_4_), channel_id=1, source_target_pairs={{0,3},{1,0},{2,1},{3,2},{8,9},{9,10},{10,11},{11,8},{4,7},{5,4},{6... | collective-permute-start | bytes 983048 | tf_op jit(solution)/shard_map/first_y_down/ppermute | solution.py:42
  44.4 15.1 %copy-start.10 = (bf16[2,64,1280]{2,1,0:T(8,128)(2,1)}, bf16[2,64,1280]{2,1,0:T(8,128)(2,1)S(1)}, u32[]{:S(2)}) copy-start(bf16[2,64,1280]{2,1,0:T(8,128)(2,1)S(1)} %collective-permute-done.1.refs_2_) | copy-start | bytes 983044
  44.4 15.0 %collective-permute-start.5 = (bf16[2,64,1280]{2,1,0:T(8,128)(2,1)S(1)}, bf16[2,64,1280]{2,1,0:T(8,128)(2,1)S(1)}, u32[]{:S(2)}, u32[]{:S(2)}) collective-permute-start(bf16[2,64,1280]{2,1,0:T(8,128)(2,1)S(1)} %collective-permute-done.1.refs_2_), channel_id=1, source_target_pairs={{0,4},{4,0},{1,5},{5,1},{2,6},{6,2},{3,7},{7,3},{8,12},{12,8},{9,1... | collective-permute-start | bytes 983048 | tf_op jit(solution)/shard_map/first_far_across/ppermute | solution.py:47
  49.6 9.9 %copy-start.11 = (bf16[2,64,1280]{2,1,0:T(8,128)(2,1)}, bf16[2,64,1280]{2,1,0:T(8,128)(2,1)S(1)}, u32[]{:S(2)}) copy-start(bf16[2,64,1280]{2,1,0:T(8,128)(2,1)S(1)} %collective-permute-done.4.refs_5_) | copy-start | bytes 983044
  49.6 15.4 %collective-permute-start.14 = (bf16[2,64,1280]{2,1,0:T(8,128)(2,1)S(1)}, bf16[2,64,1280]{2,1,0:T(8,128)(2,1)S(1)}, u32[]{:S(2)}, u32[]{:S(2)}) collective-permute-start(bf16[2,64,1280]{2,1,0:T(8,128)(2,1)S(1)} %get-tuple-element.64.refs_0_.refs_10_), channel_id=1, source_target_pairs={{0,1},{1,2},{2,3},{3,0},{8,11},{9,8},{10,9},{11,10},{4,5},{5,6},{6... | collective-permute-start | bytes 983048 | tf_op jit(solution)/shard_map/second_up/ppermute | solution.py:37
  53.0 15.0 %copy-start.12 = (bf16[2,64,1280]{2,1,0:T(8,128)(2,1)}, bf16[2,64,1280]{2,1,0:T(8,128)(2,1)S(1)}, u32[]{:S(2)}) copy-start(bf16[2,64,1280]{2,1,0:T(8,128)(2,1)S(1)} %collective-permute-done.17.refs_4_.refs_14_) | copy-start | bytes 983044
  53.0 12.0 %collective-permute-start.18 = (bf16[2,64,1280]{2,1,0:T(8,128)(2,1)S(1)}, bf16[2,64,1280]{2,1,0:T(8,128)(2,1)S(1)}, u32[]{:S(2)}, u32[]{:S(2)}) collective-permute-start(bf16[2,64,1280]{2,1,0:T(8,128)(2,1)S(1)} %collective-permute-done.17.refs_4_.refs_14_), channel_id=1, source_target_pairs={{0,1},{1,2},{2,3},{3,0},{8,11},{9,8},{10,9},{11,10},{4,5},{5,6},{6... | collective-permute-start | bytes 983048 | tf_op jit(solution)/shard_map/second_y_up/ppermute | solution.py:37
  57.5 10.5 %copy-start.13 = (bf16[2,64,1280]{2,1,0:T(8,128)(2,1)}, bf16[2,64,1280]{2,1,0:T(8,128)(2,1)S(1)}, u32[]{:S(2)}) copy-start(bf16[2,64,1280]{2,1,0:T(8,128)(2,1)S(1)} %collective-permute-done.16.refs_2_.refs_12_) | copy-start | bytes 983044
  57.6 10.1 %collective-permute-start.19 = (bf16[2,64,1280]{2,1,0:T(8,128)(2,1)S(1)}, bf16[2,64,1280]{2,1,0:T(8,128)(2,1)S(1)}, u32[]{:S(2)}, u32[]{:S(2)}) collective-permute-start(bf16[2,64,1280]{2,1,0:T(8,128)(2,1)S(1)} %collective-permute-done.16.refs_2_.refs_12_), channel_id=1, source_target_pairs={{0,4},{4,0},{1,5},{5,1},{2,6},{6,2},{3,7},{7,3},{8,12},{12,8},{9,1... | collective-permute-start | bytes 983048 | tf_op jit(solution)/shard_map/second_far_across/ppermute | solution.py:47
  58.0 10.0 %collective-permute-start.20 = (bf16[2,64,1280]{2,1,0:T(8,128)(2,1)S(1)}, bf16[2,64,1280]{2,1,0:T(8,128)(2,1)S(1)}, u32[]{:S(2)}, u32[]{:S(2)}) collective-permute-start(bf16[2,64,1280]{2,1,0:T(8,128)(2,1)S(1)} %collective-permute-done.17.refs_4_.refs_14_), channel_id=1, source_target_pairs={{0,3},{1,0},{2,1},{3,2},{8,9},{9,10},{10,11},{11,8},{4,7},{5,4},{6... | collective-permute-start | bytes 983048 | tf_op jit(solution)/shard_map/second_y_down/ppermute | solution.py:42
  63.8 8.6 %copy-start.21 = (bf16[2,576,256]{2,1,0:T(8,128)(2,1)}, bf16[2,576,256]{2,1,0:T(8,128)(2,1)S(1)}, u32[]{:S(2)}) copy-start(bf16[2,576,256]{2,1,0:T(8,128)(2,1)S(1)} %get-tuple-element.80.refs_8_) | copy-start | bytes 1769476
  63.8 8.6 %copy-start.22 = (bf16[2,576,256]{2,1,0:T(8,128)(2,1)}, bf16[2,576,256]{2,1,0:T(8,128)(2,1)S(1)}, u32[]{:S(2)}) copy-start(bf16[2,576,256]{2,1,0:T(8,128)(2,1)S(1)} %get-tuple-element.81.refs_9_) | copy-start | bytes 1769476
  63.8 9.2 %collective-permute-start.8 = (bf16[2,64,1280]{2,1,0:T(8,128)(2,1)S(1)}, bf16[2,64,1280]{2,1,0:T(8,128)(2,1)S(1)}, u32[]{:S(2)}, u32[]{:S(2)}) collective-permute-start(bf16[2,64,1280]{2,1,0:T(8,128)(2,1)S(1)} %get-tuple-element.57), channel_id=1, source_target_pairs={{0,4},{4,0},{1,5},{5,1},{2,6},{6,2},{3,7},{7,3},{8,12},{12,8},{9,1... | collective-permute-start | bytes 983048 | tf_op jit(solution)/shard_map/sum_first_far_across/ppermute | solution.py:47
  65.0 8.8 %collective-permute-start.7 = (bf16[2,64,1280]{2,1,0:T(8,128)(2,1)S(1)}, bf16[2,64,1280]{2,1,0:T(8,128)(2,1)S(1)}, u32[]{:S(2)}, u32[]{:S(2)}) collective-permute-start(bf16[2,64,1280]{2,1,0:T(8,128)(2,1)S(1)} %get-tuple-element.54), channel_id=1, source_target_pairs={{0,3},{1,0},{2,1},{3,2},{8,9},{9,10},{10,11},{11,8},{4,7},{5,4},{6... | collective-permute-start | bytes 983048 | tf_op jit(solution)/shard_map/sum_first_down/ppermute | solution.py:42
  65.0 10.8 %collective-permute-start.11 = (bf16[2,64,1280]{2,1,0:T(8,128)(2,1)S(1)}, bf16[2,64,1280]{2,1,0:T(8,128)(2,1)S(1)}, u32[]{:S(2)}, u32[]{:S(2)}) collective-permute-start(bf16[2,64,1280]{2,1,0:T(8,128)(2,1)S(1)} %get-tuple-element.59), channel_id=1, source_target_pairs={{0,1},{1,2},{2,3},{3,0},{8,11},{9,8},{10,9},{11,10},{4,5},{5,6},{6... | collective-permute-start | bytes 983048 | tf_op jit(solution)/shard_map/sum_first_y_up/ppermute | solution.py:37
  67.7 9.9 %collective-permute-start.12 = (bf16[2,64,1280]{2,1,0:T(8,128)(2,1)S(1)}, bf16[2,64,1280]{2,1,0:T(8,128)(2,1)S(1)}, u32[]{:S(2)}, u32[]{:S(2)}) collective-permute-start(bf16[2,64,1280]{2,1,0:T(8,128)(2,1)S(1)} %get-tuple-element.60), channel_id=1, source_target_pairs={{0,3},{1,0},{2,1},{3,2},{8,9},{9,10},{10,11},{11,8},{4,7},{5,4},{6... | collective-permute-start | bytes 983048 | tf_op jit(solution)/shard_map/sum_first_y_down/ppermute | solution.py:42
  72.4 53.1 %copy-start.23 = (bf16[2,576,256]{2,1,0:T(8,128)(2,1)}, bf16[2,576,256]{2,1,0:T(8,128)(2,1)S(1)}, u32[]{:S(2)}) copy-start(bf16[2,576,256]{2,1,0:T(8,128)(2,1)S(1)} %get-tuple-element.82.refs_18_) | copy-start | bytes 1769476
  72.5 53.1 %copy-start.24 = (bf16[2,576,256]{2,1,0:T(8,128)(2,1)}, bf16[2,576,256]{2,1,0:T(8,128)(2,1)S(1)}, u32[]{:S(2)}) copy-start(bf16[2,576,256]{2,1,0:T(8,128)(2,1)S(1)} %get-tuple-element.83.refs_19_) | copy-start | bytes 1769476
  72.5 52.2 %copy-start = (bf16[1,256,1280]{2,1,0:T(8,128)(2,1)S(1)}, bf16[1,256,1280]{2,1,0:T(8,128)(2,1)}, u32[]{:S(2)}) copy-start(bf16[1,256,1280]{2,1,0:T(8,128)(2,1)} %tokens.3) | copy-start | bytes 1966084
  72.5 52.2 %copy-start.1 = (bf16[1,256,1280]{2,1,0:T(8,128)(2,1)S(1)}, bf16[1,256,1280]{2,1,0:T(8,128)(2,1)}, u32[]{:S(2)}) copy-start(bf16[1,256,1280]{2,1,0:T(8,128)(2,1)} %grad_out.3) | copy-start | bytes 1966084
  72.5 52.2 %copy-start.3 = (f32[128,256]{1,0:T(8,128)S(1)}, f32[128,256]{1,0:T(8,128)}, u32[]{:S(2)}) copy-start(f32[128,256]{1,0:T(8,128)} %get-tuple-element.45.p_dispatch) | copy-start | bytes 393220
  72.5 52.2 %copy-start.20 = (f32[128,256]{1,0:T(8,128)S(1)}, f32[128,256]{1,0:T(8,128)}, u32[]{:S(2)}) copy-start(f32[128,256]{1,0:T(8,128)} %get-tuple-element.76.p_combine) | copy-start | bytes 393220
  72.5 6.3 %collective-permute-start.21 = (bf16[2,64,1280]{2,1,0:T(8,128)(2,1)S(1)}, bf16[2,64,1280]{2,1,0:T(8,128)(2,1)S(1)}, u32[]{:S(2)}, u32[]{:S(2)}) collective-permute-start(bf16[2,64,1280]{2,1,0:T(8,128)(2,1)S(1)} %get-tuple-element.70), channel_id=1, source_target_pairs={{0,4},{4,0},{1,5},{5,1},{2,6},{6,2},{3,7},{7,3},{8,12},{12,8},{9,1... | collective-permute-start | bytes 983048 | tf_op jit(solution)/shard_map/sum_second_far_across/ppermute | solution.py:47
  73.0 9.7 %collective-permute-start.26 = (bf16[2,64,1280]{2,1,0:T(8,128)(2,1)S(1)}, bf16[2,64,1280]{2,1,0:T(8,128)(2,1)S(1)}, u32[]{:S(2)}, u32[]{:S(2)}) collective-permute-start(bf16[2,64,1280]{2,1,0:T(8,128)(2,1)S(1)} %get-tuple-element.75), channel_id=1, source_target_pairs={{0,3},{1,0},{2,1},{3,2},{8,9},{9,10},{10,11},{11,8},{4,7},{5,4},{6... | collective-permute-start | bytes 983048 | tf_op jit(solution)/shard_map/sum_second_y_down/ppermute | solution.py:42
  73.8 9.6 %collective-permute-start.25 = (bf16[2,64,1280]{2,1,0:T(8,128)(2,1)S(1)}, bf16[2,64,1280]{2,1,0:T(8,128)(2,1)S(1)}, u32[]{:S(2)}, u32[]{:S(2)}) collective-permute-start(bf16[2,64,1280]{2,1,0:T(8,128)(2,1)S(1)} %get-tuple-element.74), channel_id=1, source_target_pairs={{0,1},{1,2},{2,3},{3,0},{8,11},{9,8},{10,9},{11,10},{4,5},{5,6},{6... | collective-permute-start | bytes 983048 | tf_op jit(solution)/shard_map/sum_second_y_up/ppermute | solution.py:37
  75.8 13.6 %collective-permute-start.9 = (bf16[2,64,1280]{2,1,0:T(8,128)(2,1)S(1)}, bf16[2,64,1280]{2,1,0:T(8,128)(2,1)S(1)}, u32[]{:S(2)}, u32[]{:S(2)}) collective-permute-start(bf16[2,64,1280]{2,1,0:T(8,128)(2,1)S(1)} %add_convert_fusion.5), channel_id=1, source_target_pairs={{0,1},{1,2},{2,3},{3,0},{8,11},{9,8},{10,9},{11,10},{4,5},{5,6},{6... | collective-permute-start | bytes 983048 | tf_op jit(solution)/shard_map/sum_first_on_up/ppermute | solution.py:37
  77.7 16.9 %collective-permute-start.13 = (bf16[2,64,1280]{2,1,0:T(8,128)(2,1)S(1)}, bf16[2,64,1280]{2,1,0:T(8,128)(2,1)S(1)}, u32[]{:S(2)}, u32[]{:S(2)}) collective-permute-start(bf16[2,64,1280]{2,1,0:T(8,128)(2,1)S(1)} %add_convert_fusion.3), channel_id=1, source_target_pairs={{0,4},{4,0},{1,5},{5,1},{2,6},{6,2},{3,7},{7,3},{8,12},{12,8},{9,1... | collective-permute-start | bytes 983048 | tf_op jit(solution)/shard_map/sum_first_across/ppermute | solution.py:47
  78.9 14.0 %collective-permute-start.22 = (bf16[2,64,1280]{2,1,0:T(8,128)(2,1)S(1)}, bf16[2,64,1280]{2,1,0:T(8,128)(2,1)S(1)}, u32[]{:S(2)}, u32[]{:S(2)}) collective-permute-start(bf16[2,64,1280]{2,1,0:T(8,128)(2,1)S(1)} %add_convert_fusion.2), channel_id=1, source_target_pairs={{0,3},{1,0},{2,1},{3,2},{8,9},{9,10},{10,11},{11,8},{4,7},{5,4},{6... | collective-permute-start | bytes 983048 | tf_op jit(solution)/shard_map/sum_second_on_down/ppermute | solution.py:42
  83.5 11.0 %collective-permute-start.27 = (bf16[2,64,1280]{2,1,0:T(8,128)(2,1)S(1)}, bf16[2,64,1280]{2,1,0:T(8,128)(2,1)S(1)}, u32[]{:S(2)}, u32[]{:S(2)}) collective-permute-start(bf16[2,64,1280]{2,1,0:T(8,128)(2,1)S(1)} %add_convert_fusion), channel_id=1, source_target_pairs={{0,4},{4,0},{1,5},{5,1},{2,6},{6,2},{3,7},{7,3},{8,12},{12,8},{9,1... | collective-permute-start | bytes 983048 | tf_op jit(solution)/shard_map/sum_second_across/ppermute | solution.py:47
  89.5 9.0 %collective-permute-start.10 = (bf16[2,64,1280]{2,1,0:T(8,128)(2,1)S(1)}, bf16[2,64,1280]{2,1,0:T(8,128)(2,1)S(1)}, u32[]{:S(2)}, u32[]{:S(2)}) collective-permute-start(bf16[2,64,1280]{2,1,0:T(8,128)(2,1)S(1)} %add_convert_fusion.4), channel_id=1, source_target_pairs={{0,1},{1,2},{2,3},{3,0},{8,11},{9,8},{10,9},{11,10},{4,5},{5,6},{6... | collective-permute-start | bytes 983048 | tf_op jit(solution)/shard_map/sum_first_up/ppermute | solution.py:37
  92.9 9.8 %collective-permute-start.23 = (bf16[2,64,1280]{2,1,0:T(8,128)(2,1)S(1)}, bf16[2,64,1280]{2,1,0:T(8,128)(2,1)S(1)}, u32[]{:S(2)}, u32[]{:S(2)}) collective-permute-start(bf16[2,64,1280]{2,1,0:T(8,128)(2,1)S(1)} %get-tuple-element.71), channel_id=1, source_target_pairs={{0,1},{1,2},{2,3},{3,0},{8,11},{9,8},{10,9},{11,10},{4,5},{5,6},{6... | collective-permute-start | bytes 983048 | tf_op jit(solution)/shard_map/sum_second_up/ppermute | solution.py:37
  93.1 9.7 %collective-permute-start.24 = (bf16[2,64,1280]{2,1,0:T(8,128)(2,1)S(1)}, bf16[2,64,1280]{2,1,0:T(8,128)(2,1)S(1)}, u32[]{:S(2)}, u32[]{:S(2)}) collective-permute-start(bf16[2,64,1280]{2,1,0:T(8,128)(2,1)S(1)} %add_convert_fusion.1), channel_id=1, source_target_pairs={{0,3},{1,0},{2,1},{3,2},{8,9},{9,10},{10,11},{11,8},{4,7},{5,4},{6... | collective-permute-start | bytes 983048 | tf_op jit(solution)/shard_map/sum_second_down/ppermute | solution.py:42
  146.1 19.7 %all-to-all-start.3 = ((f32[128,1,1280]{2,1,0:T(1,128)}), f32[128,1,1280]{2,1,0:T(1,128)S(1)}, u32[]{:S(2)}, u32[]{:S(2)}) async-start(f32[128,1,1280]{2,1,0:T(1,128)} %reshape.28), calls=%async_computation.3 | async-start | bytes 1310720 | tf_op jit(solution)/shard_map/all_to_all | solution.py:348
  150.7 9.8 %copy-start.2 = (bf16[128,1280]{1,0:T(8,128)(2,1)S(1)}, bf16[128,1280]{1,0:T(8,128)(2,1)}, u32[]{:S(2)}) copy-start(bf16[128,1280]{1,0:T(8,128)(2,1)} %slot_params.3) | copy-start | bytes 983044
  (6 other events, 34.1 us)

commit v7 on v6

--- a/solution.py
+++ b/solution.py
@@ -304,7 +304,7 @@
     )
     dl = grad.astype(BF)
     d_logits[...] = dl
-    local[...] = dot(dl, t, 1, 0)
+    local[...] = dot(dl, t, 1, 0).reshape(local.shape)
 
 
 def logits_back(tokens, grad_out, back, p_dispatch, p_combine, n_expert):
@@ -314,7 +314,7 @@
         functools.partial(logits_kernel, n_expert),
         out_shape=(
             jax.ShapeDtypeStruct(p_dispatch.shape, BF),
-            jax.ShapeDtypeStruct((slots, feature), F32),
+            jax.ShapeDtypeStruct((slots, 1, feature), F32),
             jax.ShapeDtypeStruct((slots, feature), BF),
         ),
         compiler_params=params(),
@@ -339,13 +339,22 @@
     )(p_dispatch, d_slot_in, d_logits, slot_params)
 
 
+def sum_kernel(terms, copies):
+    total = jnp.sum(terms[...], axis=0, keepdims=True)
+    copies[...] = jnp.broadcast_to(total, copies.shape)
+
+
 def sum_over_all(value):
-    n = lax.axis_size(NAMES)
-    rows, feature = value.shape
+    slots, _, feature = value.shape
     terms = lax.all_to_all(value, NAMES, split_axis=0, concat_axis=0, tiled=True)
-    mine = jnp.sum(terms.reshape(n, rows // n, feature), axis=0)
-    copies = jnp.broadcast_to(mine[None], (n, rows // n, feature)).reshape(rows, feature)
-    return lax.all_to_all(copies, NAMES, split_axis=0, concat_axis=0, tiled=True)
+    copies = pl.pallas_call(
+        sum_kernel,
+        out_shape=jax.ShapeDtypeStruct(value.shape, F32),
+        compiler_params=params(),
+        name="sum_terms",
+    )(terms)
+    total = lax.all_to_all(copies, NAMES, split_axis=0, concat_axis=0, tiled=True)
+    return total.reshape(slots, feature)
 
 
 def split(outputs):

time: 167 us -> 166 us (level)
  local copies, waits for them, and re-layouts: 2.84 us -> 0.99 us
where the time goes in v7:
time: 166 us
  blocking collectives  61.2 us (37%)
  starting transfers between devices  36.2 us (22%)
  waiting for transfers between devices  35 us (21%)
  Pallas kernels  30.8 us (19%)
    all_to_all x2, blocking collectives, exchange(): return lax.all_to_all(rows, EXPERT, split_axis=0, concat_axis=0, tiled=True)  42.9 us
    ppermute x10, waiting for transfers between devices, up(): lax.ppermute(value, ('c', 'z'), [turn(c, z, 1) for c in range(2) for z in...  26.6 us
    ppermute x10, starting transfers between devices, up(): lax.ppermute(value, ('c', 'z'), [turn(c, z, 1) for c in range(2) for z in...  22.2 us
    all_to_all x1, blocking collectives, sum_over_all(): lax.all_to_all(value, NAMES, split_axis=0, concat_axis=0, tiled=True)  18.3 us
    pallas_call x1, Pallas kernels, weight_grads(): pl.pallas_call(functools.partial(weights_kernel, half), grid=(2 * half,),...  9.77 us
    pallas_call x2, Pallas kernels, expert_call(): pl.pallas_call(expert_kernel, grid=(count,), in_specs=[per_expert(block,...  8.67 us
    ppermute x8, starting transfers between devices, across(): return lax.ppermute(value, 'yl', SWAP)  4.86 us
    all_to_all x1, starting transfers between devices, sum_over_all(): lax.all_to_all(copies, NAMES, split_axis=0, concat_axis=0, tiled=True)  4.58 us
  transfers between devices with their start and end apart: 29, of which 12 were waited for; matrix products, arithmetic and copies ran while one was open for 0% of the time, Pallas kernels for 15%

profile of v7, /device:TPU:1, one launch (start us, length us, event | category | flops | bytes accessed | tf_op | source)
XLA Modules:
  0.0 165.8 jit_solution(8806718671809357389)
XLA Ops:
  0.6 3.3 %route.1 = (bf16[256,1280]{1,0:T(8,128)(2,1)}, f32[128,256]{1,0:T(8,128)}, f32[128,256]{1,0:T(8,128)}) custom-call(bf16[1,256,1280]{2,1,0:T(8,128)(2,1)} %tokens.3, bf16[128,1280]{1,0:T(8,128)(2,1)} %slot_params.3, bf16[1,256,1280]{2,1,0:T(8,128)(2,1)} %grad_out.3), custom_call_target="tpu_custom_call" | custom-call | tf_op jit(solution)/shard_map/route/pallas_call | solution.py:81
  3.9 21.6 %all_to_all.32 = bf16[16,16,1280]{2,1,0:T(8,128)(2,1)S(1)} all-to-all(bf16[16,16,1280]{2,1,0:T(8,128)(2,1)} %bitcast.11), channel_id=1, replica_groups=mesh['yh'=2,'x'=4,'c'=2,'yl'=2,'z'=4] {'yh','x','c'}, dimensions={0} | all-to-all | bytes 1310720 | tf_op jit(solution)/shard_map/all_to_all | solution.py:288
  25.6 0.3 sort_rows.1
  26.0 3.8 %collective-permute-start = (bf16[2,64,1280]{2,1,0:T(8,128)(2,1)S(1)}, bf16[2,64,1280]{2,1,0:T(8,128)(2,1)S(1)}, u32[]{:S(2)}, u32[]{:S(2)}) collective-permute-start(bf16[2,64,1280]{2,1,0:T(8,128)(2,1)S(1)} %get-tuple-element.47.refs_0_), channel_id=1, source_target_pairs={{0,1},{1,2},{2,3},{3,0},{8,11},{9,8},{10,9},{11,10},{4,5},{5,6},{6... | collective-permute-start | bytes 983048 | tf_op jit(solution)/shard_map/first_up/ppermute | solution.py:37
  29.8 0.4 collective-permute-start.3
  30.2 6.2 %collective-permute-done.refs_1_ = bf16[2,64,1280]{2,1,0:T(8,128)(2,1)S(1)} collective-permute-done((bf16[2,64,1280]{2,1,0:T(8,128)(2,1)S(1)}, bf16[2,64,1280]{2,1,0:T(8,128)(2,1)S(1)}, u32[]{:S(2)}, u32[]{:S(2)}) %collective-permute-start) | collective-permute-done | bytes 327712 | tf_op jit(solution)/shard_map/first_up/ppermute | solution.py:37
  36.4 3.4 %collective-permute-start.1 = (bf16[2,64,1280]{2,1,0:T(8,128)(2,1)S(1)}, bf16[2,64,1280]{2,1,0:T(8,128)(2,1)S(1)}, u32[]{:S(2)}, u32[]{:S(2)}) collective-permute-start(bf16[2,64,1280]{2,1,0:T(8,128)(2,1)S(1)} %collective-permute-done.refs_1_), channel_id=1, source_target_pairs={{0,1},{1,2},{2,3},{3,0},{8,11},{9,8},{10,9},{11,10},{4,5},{5,6},{6... | collective-permute-start | bytes 983048 | tf_op jit(solution)/shard_map/first_on_up/ppermute | solution.py:37
  39.8 2.2 %collective-permute-start.4 = (bf16[2,64,1280]{2,1,0:T(8,128)(2,1)S(1)}, bf16[2,64,1280]{2,1,0:T(8,128)(2,1)S(1)}, u32[]{:S(2)}, u32[]{:S(2)}) collective-permute-start(bf16[2,64,1280]{2,1,0:T(8,128)(2,1)S(1)} %collective-permute-done.3.refs_4_), channel_id=1, source_target_pairs={{0,1},{1,2},{2,3},{3,0},{8,11},{9,8},{10,9},{11,10},{4,5},{5,6},{6... | collective-permute-start | bytes 983048 | tf_op jit(solution)/shard_map/first_y_up/ppermute | solution.py:37
  42.0 0.4 collective-permute-start.17
  42.4 0.3 collective-permute-start.6
  42.6 1.7 %collective-permute-done.1.refs_2_ = bf16[2,64,1280]{2,1,0:T(8,128)(2,1)S(1)} collective-permute-done((bf16[2,64,1280]{2,1,0:T(8,128)(2,1)S(1)}, bf16[2,64,1280]{2,1,0:T(8,128)(2,1)S(1)}, u32[]{:S(2)}, u32[]{:S(2)}) %collective-permute-start.1) | collective-permute-done | bytes 327712 | tf_op jit(solution)/shard_map/first_on_up/ppermute | solution.py:37
  44.4 0.4 collective-permute-start.5
  44.8 4.8 %collective-permute-done.4.refs_5_ = bf16[2,64,1280]{2,1,0:T(8,128)(2,1)S(1)} collective-permute-done((bf16[2,64,1280]{2,1,0:T(8,128)(2,1)S(1)}, bf16[2,64,1280]{2,1,0:T(8,128)(2,1)S(1)}, u32[]{:S(2)}, u32[]{:S(2)}) %collective-permute-start.4) | collective-permute-done | bytes 327712 | tf_op jit(solution)/shard_map/first_y_up/ppermute | solution.py:37
  49.6 3.4 %collective-permute-start.14 = (bf16[2,64,1280]{2,1,0:T(8,128)(2,1)S(1)}, bf16[2,64,1280]{2,1,0:T(8,128)(2,1)S(1)}, u32[]{:S(2)}, u32[]{:S(2)}) collective-permute-start(bf16[2,64,1280]{2,1,0:T(8,128)(2,1)S(1)} %get-tuple-element.64.refs_0_.refs_10_), channel_id=1, source_target_pairs={{0,1},{1,2},{2,3},{3,0},{8,11},{9,8},{10,9},{11,10},{4,5},{5,6},{6... | collective-permute-start | bytes 983048 | tf_op jit(solution)/shard_map/second_up/ppermute | solution.py:37
  53.1 4.5 %stage.1 = (bf16[4,576,1280]{2,1,0:T(8,128)(2,1)S(1)}, bf16[4,576,1280]{2,1,0:T(8,128)(2,1)S(1)}) custom-call(bf16[4,576,1280]{2,1,0:T(8,128)(2,1)} %w_in, bf16[4,576,1280]{2,1,0:T(8,128)(2,1)} %w_out), custom_call_target="tpu_custom_call" | custom-call | tf_op jit(solution)/shard_map/stage/pallas_call | solution.py:124
  57.6 0.5 collective-permute-start.19
  58.0 1.3 collective-permute-start.20
  59.4 4.3 %expert.2 = (bf16[2,576,256]{2,1,0:T(8,128)(2,1)S(1)}, bf16[2,576,256]{2,1,0:T(8,128)(2,1)S(1)}, bf16[2,64,1280]{2,1,0:T(8,128)(2,1)S(1)}, bf16[2,64,1280]{2,1,0...) custom-call(bf16[2,64,1280]{2,1,0:T(8,128)(2,1)S(1)} %get-tuple-elem, ...), custom_call_target="tpu_custom_call" | custom-call | flops 3019898880 | bytes 12582912 | tf_op jit(solution)/shard_map/expert/pallas_call | solution.py:188
  63.8 1.1 collective-permute-start.8
  65.0 2.7 %collective-permute-start.11 = (bf16[2,64,1280]{2,1,0:T(8,128)(2,1)S(1)}, bf16[2,64,1280]{2,1,0:T(8,128)(2,1)S(1)}, u32[]{:S(2)}, u32[]{:S(2)}) collective-permute-start(bf16[2,64,1280]{2,1,0:T(8,128)(2,1)S(1)} %get-tuple-element.59), channel_id=1, source_target_pairs={{0,1},{1,2},{2,3},{3,0},{8,11},{9,8},{10,9},{11,10},{4,5},{5,6},{6... | collective-permute-start | bytes 983048 | tf_op jit(solution)/shard_map/sum_first_y_up/ppermute | solution.py:37
  67.7 0.3 collective-permute-done.20.refs_7_.refs_17_
  68.0 4.3 %expert.3 = (bf16[2,576,256]{2,1,0:T(8,128)(2,1)S(1)}, bf16[2,576,256]{2,1,0:T(8,128)(2,1)S(1)}, bf16[2,64,1280]{2,1,0:T(8,128)(2,1)S(1)}, bf16[2,64,1280]{2,1,0...) custom-call(bf16[2,64,1280]{2,1,0:T(8,128)(2,1)S(1)} %get-tuple-elem, ...), custom_call_target="tpu_custom_call" | custom-call | flops 3019898880 | bytes 12582912 | tf_op jit(solution)/shard_map/expert/pallas_call | solution.py:188
  72.5 0.5 collective-permute-start.21
  73.0 0.7 collective-permute-start.26
  73.8 2.0 %collective-permute-start.25 = (bf16[2,64,1280]{2,1,0:T(8,128)(2,1)S(1)}, bf16[2,64,1280]{2,1,0:T(8,128)(2,1)S(1)}, u32[]{:S(2)}, u32[]{:S(2)}) collective-permute-start(bf16[2,64,1280]{2,1,0:T(8,128)(2,1)S(1)} %get-tuple-element.74), channel_id=1, source_target_pairs={{0,1},{1,2},{2,3},{3,0},{8,11},{9,8},{10,9},{11,10},{4,5},{5,6},{6... | collective-permute-start | bytes 983048 | tf_op jit(solution)/shard_map/sum_second_y_up/ppermute | solution.py:37
  75.8 1.1 collective-permute-start.9
  77.0 0.6 collective-permute-done.12
  77.7 0.6 collective-permute-start.13
  78.2 0.6 collective-permute-done.21
  78.9 0.8 collective-permute-start.22
  79.7 3.0 %collective-permute-done.26 = bf16[2,64,1280]{2,1,0:T(8,128)(2,1)S(1)} collective-permute-done((bf16[2,64,1280]{2,1,0:T(8,128)(2,1)S(1)}, bf16[2,64,1280]{2,1,0:T(8,128)(2,1)S(1)}, u32[]{:S(2)}, u32[]{:S(2)}) %collective-permute-start.26) | collective-permute-done | bytes 327712 | tf_op jit(solution)/shard_map/sum_second_y_down/ppermute | solution.py:42
  82.7 0.8 collective-permute-done.25
  83.5 1.0 collective-permute-start.27
  84.5 4.9 %collective-permute-done.9 = bf16[2,64,1280]{2,1,0:T(8,128)(2,1)S(1)} collective-permute-done((bf16[2,64,1280]{2,1,0:T(8,128)(2,1)S(1)}, bf16[2,64,1280]{2,1,0:T(8,128)(2,1)S(1)}, u32[]{:S(2)}, u32[]{:S(2)}) %collective-permute-start.9) | collective-permute-done | bytes 327712 | tf_op jit(solution)/shard_map/sum_first_on_up/ppermute | solution.py:37
  89.5 3.4 %collective-permute-start.10 = (bf16[2,64,1280]{2,1,0:T(8,128)(2,1)S(1)}, bf16[2,64,1280]{2,1,0:T(8,128)(2,1)S(1)}, u32[]{:S(2)}, u32[]{:S(2)}) collective-permute-start(bf16[2,64,1280]{2,1,0:T(8,128)(2,1)S(1)} %add_convert_fusion.4), channel_id=1, source_target_pairs={{0,1},{1,2},{2,3},{3,0},{8,11},{9,8},{10,9},{11,10},{4,5},{5,6},{6... | collective-permute-start | bytes 983048 | tf_op jit(solution)/shard_map/sum_first_up/ppermute | solution.py:37
  93.1 1.4 collective-permute-start.24
  94.5 4.0 %collective-permute-done.10.refs_2_ = bf16[2,64,1280]{2,1,0:T(8,128)(2,1)S(1)} collective-permute-done((bf16[2,64,1280]{2,1,0:T(8,128)(2,1)S(1)}, bf16[2,64,1280]{2,1,0:T(8,128)(2,1)S(1)}, u32[]{:S(2)}, u32[]{:S(2)}) %collective-permute-start.10) | collective-permute-done | bytes 327712 | tf_op jit(solution)/shard_map/sum_first_up/ppermute | solution.py:37
  98.6 4.2 %collective-permute-done.23.refs_5_ = bf16[2,64,1280]{2,1,0:T(8,128)(2,1)S(1)} collective-permute-done((bf16[2,64,1280]{2,1,0:T(8,128)(2,1)S(1)}, bf16[2,64,1280]{2,1,0:T(8,128)(2,1)S(1)}, u32[]{:S(2)}, u32[]{:S(2)}) %collective-permute-start.23) | collective-permute-done | bytes 327712 | tf_op jit(solution)/shard_map/sum_second_up/ppermute | solution.py:37
  102.8 0.6 unsort_rows.1
  103.4 21.3 %all_to_all.33 = bf16[16,16,1280]{2,1,0:T(8,128)(2,1)S(1)} all-to-all(bf16[16,16,1280]{2,1,0:T(8,128)(2,1)S(1)} %bitcast.8), channel_id=1, replica_groups=mesh['yh'=2,'x'=4,'c'=2,'yl'=2,'z'=4] {'yh','x','c'}, dimensions={0} | all-to-all | bytes 1310720 | tf_op jit(solution)/shard_map/all_to_all | solution.py:288
  124.7 0.9 logits_back.1
  125.6 18.3 %all_to_all.34.terms = f32[128,1,1280]{2,1,0:T(1,128)S(1)} all-to-all(f32[128,1,1280]{2,1,0:T(1,128)S(1)} %get-tuple-element.79), channel_id=1, replica_groups=mesh['yh'=2,'x'=4,'c'=2,'yl'=2,'z'=4] {'yh','x','c','yl','z'}, dimensions={0} | all-to-all | bytes 1310720 | tf_op jit(solution)/shard_map/all_to_all | solution.py:349
  143.9 1.3 sum_terms.1
  145.2 4.6 %all-to-all-start.3 = ((f32[128,1,1280]{2,1,0:T(1,128)}), f32[128,1,1280]{2,1,0:T(1,128)S(1)}, u32[]{:S(2)}, u32[]{:S(2)}) async-start(f32[128,1,1280]{2,1,0:T(1,128)} %sum_terms.1), calls=%async_computation.3 | async-start | bytes 1310720 | tf_op jit(solution)/shard_map/all_to_all | solution.py:356
  149.8 9.8 %weight_grads.1 = (bf16[4,576,1280]{2,1,0:T(8,128)(2,1)}, bf16[4,576,1280]{2,1,0:T(8,128)(2,1)}) custom-call(bf16[2,64,1280]{2,1,0:T(8,128)(2,1)} %copy-done.4, bf16[2,64,1280]{2,1,0:T(8,128)(2,1)} %copy-done.6, bf16[2,64,1280]{2,1,0:T(8,128)(2,1)} %copy-done.10, bf16[2,64,1280]{2,1,0:T(8,128)(2,1)} %copy-done.7, bf16[2,64,1280]{2,1,0:T(8,128)(2,1)} %copy-done.8, ...), custom_call_target="tpu_custom_call" | custom-call | flops 3019898880 | bytes 20971520 | tf_op jit(solution)/shard_map/weight_grads/pallas_call | solution.py:235
  159.6 1.4 tokens_back.1
  161.0 3.9 %all-to-all-done.3 = f32[128,1,1280]{2,1,0:T(1,128)S(1)} async-done(((f32[128,1,1280]{2,1,0:T(1,128)}), f32[128,1,1280]{2,1,0:T(1,128)S(1)}, u32[]{:S(2)}, u32[]{:S(2)}) %all-to-all-start.3) | async-done | bytes 655392 | tf_op jit(solution)/shard_map/all_to_all | solution.py:356
  164.9 0.9 copy.11
  (80 shorter events, 0.9 us)
Async XLA Ops:
  26.0 33.4 %copy-start.4 = (bf16[2,64,1280]{2,1,0:T(8,128)(2,1)}, bf16[2,64,1280]{2,1,0:T(8,128)(2,1)S(1)}, u32[]{:S(2)}) copy-start(bf16[2,64,1280]{2,1,0:T(8,128)(2,1)S(1)} %get-tuple-element.47.refs_0_) | copy-start | bytes 983044
  26.0 42.1 %copy-start.5 = (bf16[2,64,1280]{2,1,0:T(8,128)(2,1)}, bf16[2,64,1280]{2,1,0:T(8,128)(2,1)S(1)}, u32[]{:S(2)}) copy-start(bf16[2,64,1280]{2,1,0:T(8,128)(2,1)S(1)} %get-tuple-element.64.refs_0_.refs_10_) | copy-start | bytes 983044
  26.0 10.4 %collective-permute-start = (bf16[2,64,1280]{2,1,0:T(8,128)(2,1)S(1)}, bf16[2,64,1280]{2,1,0:T(8,128)(2,1)S(1)}, u32[]{:S(2)}, u32[]{:S(2)}) collective-permute-start(bf16[2,64,1280]{2,1,0:T(8,128)(2,1)S(1)} %get-tuple-element.47.refs_0_), channel_id=1, source_target_pairs={{0,1},{1,2},{2,3},{3,0},{8,11},{9,8},{10,9},{11,10},{4,5},{5,6},{6... | collective-permute-start | bytes 983048 | tf_op jit(solution)/shard_map/first_up/ppermute | solution.py:37
  29.8 10.0 %collective-permute-start.2 = (bf16[2,64,1280]{2,1,0:T(8,128)(2,1)S(1)}, bf16[2,64,1280]{2,1,0:T(8,128)(2,1)S(1)}, u32[]{:S(2)}, u32[]{:S(2)}) collective-permute-start(bf16[2,64,1280]{2,1,0:T(8,128)(2,1)S(1)} %get-tuple-element.47.refs_0_), channel_id=1, source_target_pairs={{0,3},{1,0},{2,1},{3,2},{8,9},{9,10},{10,11},{11,8},{4,7},{5,4},{6... | collective-permute-start | bytes 983048 | tf_op jit(solution)/shard_map/first_down/ppermute | solution.py:42
  29.8 10.0 %collective-permute-start.3 = (bf16[2,64,1280]{2,1,0:T(8,128)(2,1)S(1)}, bf16[2,64,1280]{2,1,0:T(8,128)(2,1)S(1)}, u32[]{:S(2)}, u32[]{:S(2)}) collective-permute-start(bf16[2,64,1280]{2,1,0:T(8,128)(2,1)S(1)} %get-tuple-element.47.refs_0_), channel_id=1, source_target_pairs={{0,4},{4,0},{1,5},{5,1},{2,6},{6,2},{3,7},{7,3},{8,12},{12,8},{9,1... | collective-permute-start | bytes 983048 | tf_op jit(solution)/shard_map/first_across/ppermute | solution.py:47
  30.2 12.2 %collective-permute-start.15 = (bf16[2,64,1280]{2,1,0:T(8,128)(2,1)S(1)}, bf16[2,64,1280]{2,1,0:T(8,128)(2,1)S(1)}, u32[]{:S(2)}, u32[]{:S(2)}) collective-permute-start(bf16[2,64,1280]{2,1,0:T(8,128)(2,1)S(1)} %get-tuple-element.64.refs_0_.refs_10_), channel_id=1, source_target_pairs={{0,3},{1,0},{2,1},{3,2},{8,9},{9,10},{10,11},{11,8},{4,7},{5,4},{6... | collective-permute-start | bytes 983048 | tf_op jit(solution)/shard_map/second_down/ppermute | solution.py:42
  36.4 23.0 %copy-start.6 = (bf16[2,64,1280]{2,1,0:T(8,128)(2,1)}, bf16[2,64,1280]{2,1,0:T(8,128)(2,1)S(1)}, u32[]{:S(2)}) copy-start(bf16[2,64,1280]{2,1,0:T(8,128)(2,1)S(1)} %collective-permute-done.refs_1_) | copy-start | bytes 983044
  36.4 8.0 %collective-permute-start.1 = (bf16[2,64,1280]{2,1,0:T(8,128)(2,1)S(1)}, bf16[2,64,1280]{2,1,0:T(8,128)(2,1)S(1)}, u32[]{:S(2)}, u32[]{:S(2)}) collective-permute-start(bf16[2,64,1280]{2,1,0:T(8,128)(2,1)S(1)} %collective-permute-done.refs_1_), channel_id=1, source_target_pairs={{0,1},{1,2},{2,3},{3,0},{8,11},{9,8},{10,9},{11,10},{4,5},{5,6},{6... | collective-permute-start | bytes 983048 | tf_op jit(solution)/shard_map/first_on_up/ppermute | solution.py:37
  39.8 19.6 %copy-start.7 = (bf16[2,64,1280]{2,1,0:T(8,128)(2,1)}, bf16[2,64,1280]{2,1,0:T(8,128)(2,1)S(1)}, u32[]{:S(2)}) copy-start(bf16[2,64,1280]{2,1,0:T(8,128)(2,1)S(1)} %collective-permute-done.2.refs_3_) | copy-start | bytes 983044
  39.8 19.6 %copy-start.8 = (bf16[2,64,1280]{2,1,0:T(8,128)(2,1)}, bf16[2,64,1280]{2,1,0:T(8,128)(2,1)S(1)}, u32[]{:S(2)}) copy-start(bf16[2,64,1280]{2,1,0:T(8,128)(2,1)S(1)} %collective-permute-done.3.refs_4_) | copy-start | bytes 983044
  39.8 9.8 %collective-permute-start.4 = (bf16[2,64,1280]{2,1,0:T(8,128)(2,1)S(1)}, bf16[2,64,1280]{2,1,0:T(8,128)(2,1)S(1)}, u32[]{:S(2)}, u32[]{:S(2)}) collective-permute-start(bf16[2,64,1280]{2,1,0:T(8,128)(2,1)S(1)} %collective-permute-done.3.refs_4_), channel_id=1, source_target_pairs={{0,1},{1,2},{2,3},{3,0},{8,11},{9,8},{10,9},{11,10},{4,5},{5,6},{6... | collective-permute-start | bytes 983048 | tf_op jit(solution)/shard_map/first_y_up/ppermute | solution.py:37
  42.0 11.0 %collective-permute-start.17 = (bf16[2,64,1280]{2,1,0:T(8,128)(2,1)S(1)}, bf16[2,64,1280]{2,1,0:T(8,128)(2,1)S(1)}, u32[]{:S(2)}, u32[]{:S(2)}) collective-permute-start(bf16[2,64,1280]{2,1,0:T(8,128)(2,1)S(1)} %get-tuple-element.64.refs_0_.refs_10_), channel_id=1, source_target_pairs={{0,4},{4,0},{1,5},{5,1},{2,6},{6,2},{3,7},{7,3},{8,12},{12,8},{9,1... | collective-permute-start | bytes 983048 | tf_op jit(solution)/shard_map/second_across/ppermute | solution.py:47
  42.4 25.6 %copy-start.9 = (bf16[2,64,1280]{2,1,0:T(8,128)(2,1)}, bf16[2,64,1280]{2,1,0:T(8,128)(2,1)S(1)}, u32[]{:S(2)}) copy-start(bf16[2,64,1280]{2,1,0:T(8,128)(2,1)S(1)} %collective-permute-done.15.refs_3_.refs_13_) | copy-start | bytes 983044
  42.4 15.2 %collective-permute-start.16 = (bf16[2,64,1280]{2,1,0:T(8,128)(2,1)S(1)}, bf16[2,64,1280]{2,1,0:T(8,128)(2,1)S(1)}, u32[]{:S(2)}, u32[]{:S(2)}) collective-permute-start(bf16[2,64,1280]{2,1,0:T(8,128)(2,1)S(1)} %collective-permute-done.15.refs_3_.refs_13_), channel_id=1, source_target_pairs={{0,3},{1,0},{2,1},{3,2},{8,9},{9,10},{10,11},{11,8},{4,7},{5,4},{6... | collective-permute-start | bytes 983048 | tf_op jit(solution)/shard_map/second_on_down/ppermute | solution.py:42
  42.4 15.6 %collective-permute-start.6 = (bf16[2,64,1280]{2,1,0:T(8,128)(2,1)S(1)}, bf16[2,64,1280]{2,1,0:T(8,128)(2,1)S(1)}, u32[]{:S(2)}, u32[]{:S(2)}) collective-permute-start(bf16[2,64,1280]{2,1,0:T(8,128)(2,1)S(1)} %collective-permute-done.3.refs_4_), channel_id=1, source_target_pairs={{0,3},{1,0},{2,1},{3,2},{8,9},{9,10},{10,11},{11,8},{4,7},{5,4},{6... | collective-permute-start | bytes 983048 | tf_op jit(solution)/shard_map/first_y_down/ppermute | solution.py:42
  44.4 15.1 %copy-start.10 = (bf16[2,64,1280]{2,1,0:T(8,128)(2,1)}, bf16[2,64,1280]{2,1,0:T(8,128)(2,1)S(1)}, u32[]{:S(2)}) copy-start(bf16[2,64,1280]{2,1,0:T(8,128)(2,1)S(1)} %collective-permute-done.1.refs_2_) | copy-start | bytes 983044
  44.4 15.0 %collective-permute-start.5 = (bf16[2,64,1280]{2,1,0:T(8,128)(2,1)S(1)}, bf16[2,64,1280]{2,1,0:T(8,128)(2,1)S(1)}, u32[]{:S(2)}, u32[]{:S(2)}) collective-permute-start(bf16[2,64,1280]{2,1,0:T(8,128)(2,1)S(1)} %collective-permute-done.1.refs_2_), channel_id=1, source_target_pairs={{0,4},{4,0},{1,5},{5,1},{2,6},{6,2},{3,7},{7,3},{8,12},{12,8},{9,1... | collective-permute-start | bytes 983048 | tf_op jit(solution)/shard_map/first_far_across/ppermute | solution.py:47
  49.6 9.9 %copy-start.11 = (bf16[2,64,1280]{2,1,0:T(8,128)(2,1)}, bf16[2,64,1280]{2,1,0:T(8,128)(2,1)S(1)}, u32[]{:S(2)}) copy-start(bf16[2,64,1280]{2,1,0:T(8,128)(2,1)S(1)} %collective-permute-done.4.refs_5_) | copy-start | bytes 983044
  49.6 15.4 %collective-permute-start.14 = (bf16[2,64,1280]{2,1,0:T(8,128)(2,1)S(1)}, bf16[2,64,1280]{2,1,0:T(8,128)(2,1)S(1)}, u32[]{:S(2)}, u32[]{:S(2)}) collective-permute-start(bf16[2,64,1280]{2,1,0:T(8,128)(2,1)S(1)} %get-tuple-element.64.refs_0_.refs_10_), channel_id=1, source_target_pairs={{0,1},{1,2},{2,3},{3,0},{8,11},{9,8},{10,9},{11,10},{4,5},{5,6},{6... | collective-permute-start | bytes 983048 | tf_op jit(solution)/shard_map/second_up/ppermute | solution.py:37
  53.0 15.0 %copy-start.12 = (bf16[2,64,1280]{2,1,0:T(8,128)(2,1)}, bf16[2,64,1280]{2,1,0:T(8,128)(2,1)S(1)}, u32[]{:S(2)}) copy-start(bf16[2,64,1280]{2,1,0:T(8,128)(2,1)S(1)} %collective-permute-done.17.refs_4_.refs_14_) | copy-start | bytes 983044
  53.0 12.0 %collective-permute-start.18 = (bf16[2,64,1280]{2,1,0:T(8,128)(2,1)S(1)}, bf16[2,64,1280]{2,1,0:T(8,128)(2,1)S(1)}, u32[]{:S(2)}, u32[]{:S(2)}) collective-permute-start(bf16[2,64,1280]{2,1,0:T(8,128)(2,1)S(1)} %collective-permute-done.17.refs_4_.refs_14_), channel_id=1, source_target_pairs={{0,1},{1,2},{2,3},{3,0},{8,11},{9,8},{10,9},{11,10},{4,5},{5,6},{6... | collective-permute-start | bytes 983048 | tf_op jit(solution)/shard_map/second_y_up/ppermute | solution.py:37
  57.5 10.5 %copy-start.13 = (bf16[2,64,1280]{2,1,0:T(8,128)(2,1)}, bf16[2,64,1280]{2,1,0:T(8,128)(2,1)S(1)}, u32[]{:S(2)}) copy-start(bf16[2,64,1280]{2,1,0:T(8,128)(2,1)S(1)} %collective-permute-done.16.refs_2_.refs_12_) | copy-start | bytes 983044
  57.6 10.1 %collective-permute-start.19 = (bf16[2,64,1280]{2,1,0:T(8,128)(2,1)S(1)}, bf16[2,64,1280]{2,1,0:T(8,128)(2,1)S(1)}, u32[]{:S(2)}, u32[]{:S(2)}) collective-permute-start(bf16[2,64,1280]{2,1,0:T(8,128)(2,1)S(1)} %collective-permute-done.16.refs_2_.refs_12_), channel_id=1, source_target_pairs={{0,4},{4,0},{1,5},{5,1},{2,6},{6,2},{3,7},{7,3},{8,12},{12,8},{9,1... | collective-permute-start | bytes 983048 | tf_op jit(solution)/shard_map/second_far_across/ppermute | solution.py:47
  58.0 10.0 %collective-permute-start.20 = (bf16[2,64,1280]{2,1,0:T(8,128)(2,1)S(1)}, bf16[2,64,1280]{2,1,0:T(8,128)(2,1)S(1)}, u32[]{:S(2)}, u32[]{:S(2)}) collective-permute-start(bf16[2,64,1280]{2,1,0:T(8,128)(2,1)S(1)} %collective-permute-done.17.refs_4_.refs_14_), channel_id=1, source_target_pairs={{0,3},{1,0},{2,1},{3,2},{8,9},{9,10},{10,11},{11,8},{4,7},{5,4},{6... | collective-permute-start | bytes 983048 | tf_op jit(solution)/shard_map/second_y_down/ppermute | solution.py:42
  63.8 8.6 %copy-start.21 = (bf16[2,576,256]{2,1,0:T(8,128)(2,1)}, bf16[2,576,256]{2,1,0:T(8,128)(2,1)S(1)}, u32[]{:S(2)}) copy-start(bf16[2,576,256]{2,1,0:T(8,128)(2,1)S(1)} %get-tuple-element.80.refs_8_) | copy-start | bytes 1769476
  63.8 8.6 %copy-start.22 = (bf16[2,576,256]{2,1,0:T(8,128)(2,1)}, bf16[2,576,256]{2,1,0:T(8,128)(2,1)S(1)}, u32[]{:S(2)}) copy-start(bf16[2,576,256]{2,1,0:T(8,128)(2,1)S(1)} %get-tuple-element.81.refs_9_) | copy-start | bytes 1769476
  63.8 9.2 %collective-permute-start.8 = (bf16[2,64,1280]{2,1,0:T(8,128)(2,1)S(1)}, bf16[2,64,1280]{2,1,0:T(8,128)(2,1)S(1)}, u32[]{:S(2)}, u32[]{:S(2)}) collective-permute-start(bf16[2,64,1280]{2,1,0:T(8,128)(2,1)S(1)} %get-tuple-element.57), channel_id=1, source_target_pairs={{0,4},{4,0},{1,5},{5,1},{2,6},{6,2},{3,7},{7,3},{8,12},{12,8},{9,1... | collective-permute-start | bytes 983048 | tf_op jit(solution)/shard_map/sum_first_far_across/ppermute | solution.py:47
  65.0 8.8 %collective-permute-start.7 = (bf16[2,64,1280]{2,1,0:T(8,128)(2,1)S(1)}, bf16[2,64,1280]{2,1,0:T(8,128)(2,1)S(1)}, u32[]{:S(2)}, u32[]{:S(2)}) collective-permute-start(bf16[2,64,1280]{2,1,0:T(8,128)(2,1)S(1)} %get-tuple-element.54), channel_id=1, source_target_pairs={{0,3},{1,0},{2,1},{3,2},{8,9},{9,10},{10,11},{11,8},{4,7},{5,4},{6... | collective-permute-start | bytes 983048 | tf_op jit(solution)/shard_map/sum_first_down/ppermute | solution.py:42
  65.0 10.8 %collective-permute-start.11 = (bf16[2,64,1280]{2,1,0:T(8,128)(2,1)S(1)}, bf16[2,64,1280]{2,1,0:T(8,128)(2,1)S(1)}, u32[]{:S(2)}, u32[]{:S(2)}) collective-permute-start(bf16[2,64,1280]{2,1,0:T(8,128)(2,1)S(1)} %get-tuple-element.59), channel_id=1, source_target_pairs={{0,1},{1,2},{2,3},{3,0},{8,11},{9,8},{10,9},{11,10},{4,5},{5,6},{6... | collective-permute-start | bytes 983048 | tf_op jit(solution)/shard_map/sum_first_y_up/ppermute | solution.py:37
  67.7 9.9 %collective-permute-start.12 = (bf16[2,64,1280]{2,1,0:T(8,128)(2,1)S(1)}, bf16[2,64,1280]{2,1,0:T(8,128)(2,1)S(1)}, u32[]{:S(2)}, u32[]{:S(2)}) collective-permute-start(bf16[2,64,1280]{2,1,0:T(8,128)(2,1)S(1)} %get-tuple-element.60), channel_id=1, source_target_pairs={{0,3},{1,0},{2,1},{3,2},{8,9},{9,10},{10,11},{11,8},{4,7},{5,4},{6... | collective-permute-start | bytes 983048 | tf_op jit(solution)/shard_map/sum_first_y_down/ppermute | solution.py:42
  72.4 53.2 %copy-start.23 = (bf16[2,576,256]{2,1,0:T(8,128)(2,1)}, bf16[2,576,256]{2,1,0:T(8,128)(2,1)S(1)}, u32[]{:S(2)}) copy-start(bf16[2,576,256]{2,1,0:T(8,128)(2,1)S(1)} %get-tuple-element.82.refs_18_) | copy-start | bytes 1769476
  72.5 53.2 %copy-start.24 = (bf16[2,576,256]{2,1,0:T(8,128)(2,1)}, bf16[2,576,256]{2,1,0:T(8,128)(2,1)S(1)}, u32[]{:S(2)}) copy-start(bf16[2,576,256]{2,1,0:T(8,128)(2,1)S(1)} %get-tuple-element.83.refs_19_) | copy-start | bytes 1769476
  72.5 52.2 %copy-start = (bf16[1,256,1280]{2,1,0:T(8,128)(2,1)S(1)}, bf16[1,256,1280]{2,1,0:T(8,128)(2,1)}, u32[]{:S(2)}) copy-start(bf16[1,256,1280]{2,1,0:T(8,128)(2,1)} %tokens.3) | copy-start | bytes 1966084
  72.5 52.2 %copy-start.1 = (bf16[1,256,1280]{2,1,0:T(8,128)(2,1)S(1)}, bf16[1,256,1280]{2,1,0:T(8,128)(2,1)}, u32[]{:S(2)}) copy-start(bf16[1,256,1280]{2,1,0:T(8,128)(2,1)} %grad_out.3) | copy-start | bytes 1966084
  72.5 52.2 %copy-start.3 = (f32[128,256]{1,0:T(8,128)S(1)}, f32[128,256]{1,0:T(8,128)}, u32[]{:S(2)}) copy-start(f32[128,256]{1,0:T(8,128)} %get-tuple-element.45.p_dispatch) | copy-start | bytes 393220
  72.5 52.2 %copy-start.20 = (f32[128,256]{1,0:T(8,128)S(1)}, f32[128,256]{1,0:T(8,128)}, u32[]{:S(2)}) copy-start(f32[128,256]{1,0:T(8,128)} %get-tuple-element.76.p_combine) | copy-start | bytes 393220
  72.5 6.3 %collective-permute-start.21 = (bf16[2,64,1280]{2,1,0:T(8,128)(2,1)S(1)}, bf16[2,64,1280]{2,1,0:T(8,128)(2,1)S(1)}, u32[]{:S(2)}, u32[]{:S(2)}) collective-permute-start(bf16[2,64,1280]{2,1,0:T(8,128)(2,1)S(1)} %get-tuple-element.70), channel_id=1, source_target_pairs={{0,4},{4,0},{1,5},{5,1},{2,6},{6,2},{3,7},{7,3},{8,12},{12,8},{9,1... | collective-permute-start | bytes 983048 | tf_op jit(solution)/shard_map/sum_second_far_across/ppermute | solution.py:47
  73.0 9.7 %collective-permute-start.26 = (bf16[2,64,1280]{2,1,0:T(8,128)(2,1)S(1)}, bf16[2,64,1280]{2,1,0:T(8,128)(2,1)S(1)}, u32[]{:S(2)}, u32[]{:S(2)}) collective-permute-start(bf16[2,64,1280]{2,1,0:T(8,128)(2,1)S(1)} %get-tuple-element.75), channel_id=1, source_target_pairs={{0,3},{1,0},{2,1},{3,2},{8,9},{9,10},{10,11},{11,8},{4,7},{5,4},{6... | collective-permute-start | bytes 983048 | tf_op jit(solution)/shard_map/sum_second_y_down/ppermute | solution.py:42
  73.8 9.6 %collective-permute-start.25 = (bf16[2,64,1280]{2,1,0:T(8,128)(2,1)S(1)}, bf16[2,64,1280]{2,1,0:T(8,128)(2,1)S(1)}, u32[]{:S(2)}, u32[]{:S(2)}) collective-permute-start(bf16[2,64,1280]{2,1,0:T(8,128)(2,1)S(1)} %get-tuple-element.74), channel_id=1, source_target_pairs={{0,1},{1,2},{2,3},{3,0},{8,11},{9,8},{10,9},{11,10},{4,5},{5,6},{6... | collective-permute-start | bytes 983048 | tf_op jit(solution)/shard_map/sum_second_y_up/ppermute | solution.py:37
  75.8 13.6 %collective-permute-start.9 = (bf16[2,64,1280]{2,1,0:T(8,128)(2,1)S(1)}, bf16[2,64,1280]{2,1,0:T(8,128)(2,1)S(1)}, u32[]{:S(2)}, u32[]{:S(2)}) collective-permute-start(bf16[2,64,1280]{2,1,0:T(8,128)(2,1)S(1)} %add_convert_fusion.5), channel_id=1, source_target_pairs={{0,1},{1,2},{2,3},{3,0},{8,11},{9,8},{10,9},{11,10},{4,5},{5,6},{6... | collective-permute-start | bytes 983048 | tf_op jit(solution)/shard_map/sum_first_on_up/ppermute | solution.py:37
  77.7 16.9 %collective-permute-start.13 = (bf16[2,64,1280]{2,1,0:T(8,128)(2,1)S(1)}, bf16[2,64,1280]{2,1,0:T(8,128)(2,1)S(1)}, u32[]{:S(2)}, u32[]{:S(2)}) collective-permute-start(bf16[2,64,1280]{2,1,0:T(8,128)(2,1)S(1)} %add_convert_fusion.3), channel_id=1, source_target_pairs={{0,4},{4,0},{1,5},{5,1},{2,6},{6,2},{3,7},{7,3},{8,12},{12,8},{9,1... | collective-permute-start | bytes 983048 | tf_op jit(solution)/shard_map/sum_first_across/ppermute | solution.py:47
  78.9 14.0 %collective-permute-start.22 = (bf16[2,64,1280]{2,1,0:T(8,128)(2,1)S(1)}, bf16[2,64,1280]{2,1,0:T(8,128)(2,1)S(1)}, u32[]{:S(2)}, u32[]{:S(2)}) collective-permute-start(bf16[2,64,1280]{2,1,0:T(8,128)(2,1)S(1)} %add_convert_fusion.2), channel_id=1, source_target_pairs={{0,3},{1,0},{2,1},{3,2},{8,9},{9,10},{10,11},{11,8},{4,7},{5,4},{6... | collective-permute-start | bytes 983048 | tf_op jit(solution)/shard_map/sum_second_on_down/ppermute | solution.py:42
  83.5 11.0 %collective-permute-start.27 = (bf16[2,64,1280]{2,1,0:T(8,128)(2,1)S(1)}, bf16[2,64,1280]{2,1,0:T(8,128)(2,1)S(1)}, u32[]{:S(2)}, u32[]{:S(2)}) collective-permute-start(bf16[2,64,1280]{2,1,0:T(8,128)(2,1)S(1)} %add_convert_fusion), channel_id=1, source_target_pairs={{0,4},{4,0},{1,5},{5,1},{2,6},{6,2},{3,7},{7,3},{8,12},{12,8},{9,1... | collective-permute-start | bytes 983048 | tf_op jit(solution)/shard_map/sum_second_across/ppermute | solution.py:47
  89.5 9.0 %collective-permute-start.10 = (bf16[2,64,1280]{2,1,0:T(8,128)(2,1)S(1)}, bf16[2,64,1280]{2,1,0:T(8,128)(2,1)S(1)}, u32[]{:S(2)}, u32[]{:S(2)}) collective-permute-start(bf16[2,64,1280]{2,1,0:T(8,128)(2,1)S(1)} %add_convert_fusion.4), channel_id=1, source_target_pairs={{0,1},{1,2},{2,3},{3,0},{8,11},{9,8},{10,9},{11,10},{4,5},{5,6},{6... | collective-permute-start | bytes 983048 | tf_op jit(solution)/shard_map/sum_first_up/ppermute | solution.py:37
  92.9 9.8 %collective-permute-start.23 = (bf16[2,64,1280]{2,1,0:T(8,128)(2,1)S(1)}, bf16[2,64,1280]{2,1,0:T(8,128)(2,1)S(1)}, u32[]{:S(2)}, u32[]{:S(2)}) collective-permute-start(bf16[2,64,1280]{2,1,0:T(8,128)(2,1)S(1)} %get-tuple-element.71), channel_id=1, source_target_pairs={{0,1},{1,2},{2,3},{3,0},{8,11},{9,8},{10,9},{11,10},{4,5},{5,6},{6... | collective-permute-start | bytes 983048 | tf_op jit(solution)/shard_map/sum_second_up/ppermute | solution.py:37
  93.1 9.7 %collective-permute-start.24 = (bf16[2,64,1280]{2,1,0:T(8,128)(2,1)S(1)}, bf16[2,64,1280]{2,1,0:T(8,128)(2,1)S(1)}, u32[]{:S(2)}, u32[]{:S(2)}) collective-permute-start(bf16[2,64,1280]{2,1,0:T(8,128)(2,1)S(1)} %add_convert_fusion.1), channel_id=1, source_target_pairs={{0,3},{1,0},{2,1},{3,2},{8,9},{9,10},{10,11},{11,8},{4,7},{5,4},{6... | collective-permute-start | bytes 983048 | tf_op jit(solution)/shard_map/sum_second_down/ppermute | solution.py:42
  145.2 19.7 %all-to-all-start.3 = ((f32[128,1,1280]{2,1,0:T(1,128)}), f32[128,1,1280]{2,1,0:T(1,128)S(1)}, u32[]{:S(2)}, u32[]{:S(2)}) async-start(f32[128,1,1280]{2,1,0:T(1,128)} %sum_terms.1), calls=%async_computation.3 | async-start | bytes 1310720 | tf_op jit(solution)/shard_map/all_to_all | solution.py:356
  149.8 9.8 %copy-start.2 = (bf16[128,1280]{1,0:T(8,128)(2,1)S(1)}, bf16[128,1280]{1,0:T(8,128)(2,1)}, u32[]{:S(2)}) copy-start(bf16[128,1280]{1,0:T(8,128)(2,1)} %slot_params.3) | copy-start | bytes 983044
  (6 other events, 34.1 us)

commit v8 on v7

--- a/solution.py
+++ b/solution.py
@@ -56,7 +56,11 @@
     return (k == wanted).astype(F32).astype(BF)
 
 
-def route_kernel(n_expert, tokens, slot_params, grad_out, rows, p_dispatch, p_combine):
+def route_kernel(
+    n_expert, tokens, slot_params, grad_out, rows, p_dispatch, p_combine, grad, sem
+):
+    copy = pltpu.make_async_copy(grad_out.at[0], grad, sem)
+    copy.start()
     t = tokens[0]
     slots, feature = slot_params.shape
     logits = dot(slot_params[...], t, 1, 1)
@@ -68,7 +72,8 @@
     p_combine[...] = pc
     shape = (n_expert, slots // n_expert, feature)
     slot_in = dot(pd.astype(BF), t, 1, 0).reshape(shape)
-    d_slot_out = dot(pc.astype(BF), grad_out[0], 1, 0).reshape(shape)
+    copy.wait()
+    d_slot_out = dot(pc.astype(BF), grad[...], 1, 0).reshape(shape)
     both = jnp.concatenate([slot_in, d_slot_out], axis=1).astype(BF)
     rows[...] = both.reshape(rows.shape)
 
@@ -80,7 +85,13 @@
     probs = jax.ShapeDtypeStruct((slots, length), F32)
     return pl.pallas_call(
         functools.partial(route_kernel, n_expert),
+        in_specs=[
+            pl.BlockSpec(memory_space=pltpu.VMEM),
+            pl.BlockSpec(memory_space=pltpu.VMEM),
+            pl.BlockSpec(memory_space=pl.ANY),
+        ],
         out_shape=(rows, probs, probs),
+        scratch_shapes=[pltpu.VMEM((length, feature), BF), pltpu.SemaphoreType.DMA],
         compiler_params=params(60),
         name="route",
     )(tokens, slot_params, grad_out)

time: 166 us -> 166 us (level)
  no operation moved by 1% of the time
where the time goes in v8:
time: 166 us
  blocking collectives  61.3 us (37%)
  starting transfers between devices  36.2 us (22%)
  waiting for transfers between devices  35 us (21%)
  Pallas kernels  30.9 us (19%)
    all_to_all x2, blocking collectives, exchange(): return lax.all_to_all(rows, EXPERT, split_axis=0, concat_axis=0, tiled=True)  43 us
    ppermute x10, waiting for transfers between devices, up(): lax.ppermute(value, ('c', 'z'), [turn(c, z, 1) for c in range(2) for z in...  26.6 us
    ppermute x10, starting transfers between devices, up(): lax.ppermute(value, ('c', 'z'), [turn(c, z, 1) for c in range(2) for z in...  22.2 us
    all_to_all x1, blocking collectives, sum_over_all(): lax.all_to_all(value, NAMES, split_axis=0, concat_axis=0, tiled=True)  18.3 us
    pallas_call x1, Pallas kernels, weight_grads(): pl.pallas_call(functools.partial(weights_kernel, half), grid=(2 * half,),...  9.77 us
    pallas_call x2, Pallas kernels, expert_call(): pl.pallas_call(expert_kernel, grid=(count,), in_specs=[per_expert(block,...  8.68 us
    ppermute x8, starting transfers between devices, across(): return lax.ppermute(value, 'yl', SWAP)  4.87 us
    all_to_all x1, starting transfers between devices, sum_over_all(): lax.all_to_all(copies, NAMES, split_axis=0, concat_axis=0, tiled=True)  4.58 us
  transfers between devices with their start and end apart: 29, of which 12 were waited for; matrix products, arithmetic and copies ran while one was open for 0% of the time, Pallas kernels for 15%

profile of v8, /device:TPU:1, one launch (start us, length us, event | category | flops | bytes accessed | tf_op | source)
XLA Modules:
  0.0 166.0 jit_solution(13280273654757094462)
XLA Ops:
  0.6 3.4 %route.1 = (bf16[256,1280]{1,0:T(8,128)(2,1)}, f32[128,256]{1,0:T(8,128)}, f32[128,256]{1,0:T(8,128)}) custom-call(bf16[1,256,1280]{2,1,0:T(8,128)(2,1)} %tokens.3, bf16[128,1280]{1,0:T(8,128)(2,1)} %slot_params.3, bf16[1,256,1280]{2,1,0:T(8,128)(2,1)} %grad_out.3), custom_call_target="tpu_custom_call" | custom-call | tf_op jit(solution)/shard_map/route/pallas_call | solution.py:86
  4.1 21.7 %all_to_all.32 = bf16[16,16,1280]{2,1,0:T(8,128)(2,1)S(1)} all-to-all(bf16[16,16,1280]{2,1,0:T(8,128)(2,1)} %bitcast.11), channel_id=1, replica_groups=mesh['yh'=2,'x'=4,'c'=2,'yl'=2,'z'=4] {'yh','x','c'}, dimensions={0} | all-to-all | bytes 1310720 | tf_op jit(solution)/shard_map/all_to_all | solution.py:299
  25.7 0.3 sort_rows.1
  26.1 3.8 %collective-permute-start = (bf16[2,64,1280]{2,1,0:T(8,128)(2,1)S(1)}, bf16[2,64,1280]{2,1,0:T(8,128)(2,1)S(1)}, u32[]{:S(2)}, u32[]{:S(2)}) collective-permute-start(bf16[2,64,1280]{2,1,0:T(8,128)(2,1)S(1)} %get-tuple-element.47.refs_0_), channel_id=1, source_target_pairs={{0,1},{1,2},{2,3},{3,0},{8,11},{9,8},{10,9},{11,10},{4,5},{5,6},{6... | collective-permute-start | bytes 983048 | tf_op jit(solution)/shard_map/first_up/ppermute | solution.py:37
  29.9 0.4 collective-permute-start.3
  30.3 6.2 %collective-permute-done.refs_1_ = bf16[2,64,1280]{2,1,0:T(8,128)(2,1)S(1)} collective-permute-done((bf16[2,64,1280]{2,1,0:T(8,128)(2,1)S(1)}, bf16[2,64,1280]{2,1,0:T(8,128)(2,1)S(1)}, u32[]{:S(2)}, u32[]{:S(2)}) %collective-permute-start) | collective-permute-done | bytes 327712 | tf_op jit(solution)/shard_map/first_up/ppermute | solution.py:37
  36.5 3.4 %collective-permute-start.1 = (bf16[2,64,1280]{2,1,0:T(8,128)(2,1)S(1)}, bf16[2,64,1280]{2,1,0:T(8,128)(2,1)S(1)}, u32[]{:S(2)}, u32[]{:S(2)}) collective-permute-start(bf16[2,64,1280]{2,1,0:T(8,128)(2,1)S(1)} %collective-permute-done.refs_1_), channel_id=1, source_target_pairs={{0,1},{1,2},{2,3},{3,0},{8,11},{9,8},{10,9},{11,10},{4,5},{5,6},{6... | collective-permute-start | bytes 983048 | tf_op jit(solution)/shard_map/first_on_up/ppermute | solution.py:37
  39.9 2.2 %collective-permute-start.4 = (bf16[2,64,1280]{2,1,0:T(8,128)(2,1)S(1)}, bf16[2,64,1280]{2,1,0:T(8,128)(2,1)S(1)}, u32[]{:S(2)}, u32[]{:S(2)}) collective-permute-start(bf16[2,64,1280]{2,1,0:T(8,128)(2,1)S(1)} %collective-permute-done.3.refs_4_), channel_id=1, source_target_pairs={{0,1},{1,2},{2,3},{3,0},{8,11},{9,8},{10,9},{11,10},{4,5},{5,6},{6... | collective-permute-start | bytes 983048 | tf_op jit(solution)/shard_map/first_y_up/ppermute | solution.py:37
  42.1 0.4 collective-permute-start.17
  42.5 0.3 collective-permute-start.6
  42.8 1.7 %collective-permute-done.1.refs_2_ = bf16[2,64,1280]{2,1,0:T(8,128)(2,1)S(1)} collective-permute-done((bf16[2,64,1280]{2,1,0:T(8,128)(2,1)S(1)}, bf16[2,64,1280]{2,1,0:T(8,128)(2,1)S(1)}, u32[]{:S(2)}, u32[]{:S(2)}) %collective-permute-start.1) | collective-permute-done | bytes 327712 | tf_op jit(solution)/shard_map/first_on_up/ppermute | solution.py:37
  44.5 0.4 collective-permute-start.5
  44.9 4.8 %collective-permute-done.4.refs_5_ = bf16[2,64,1280]{2,1,0:T(8,128)(2,1)S(1)} collective-permute-done((bf16[2,64,1280]{2,1,0:T(8,128)(2,1)S(1)}, bf16[2,64,1280]{2,1,0:T(8,128)(2,1)S(1)}, u32[]{:S(2)}, u32[]{:S(2)}) %collective-permute-start.4) | collective-permute-done | bytes 327712 | tf_op jit(solution)/shard_map/first_y_up/ppermute | solution.py:37
  49.7 3.4 %collective-permute-start.14 = (bf16[2,64,1280]{2,1,0:T(8,128)(2,1)S(1)}, bf16[2,64,1280]{2,1,0:T(8,128)(2,1)S(1)}, u32[]{:S(2)}, u32[]{:S(2)}) collective-permute-start(bf16[2,64,1280]{2,1,0:T(8,128)(2,1)S(1)} %get-tuple-element.64.refs_0_.refs_10_), channel_id=1, source_target_pairs={{0,1},{1,2},{2,3},{3,0},{8,11},{9,8},{10,9},{11,10},{4,5},{5,6},{6... | collective-permute-start | bytes 983048 | tf_op jit(solution)/shard_map/second_up/ppermute | solution.py:37
  53.2 4.5 %stage.1 = (bf16[4,576,1280]{2,1,0:T(8,128)(2,1)S(1)}, bf16[4,576,1280]{2,1,0:T(8,128)(2,1)S(1)}) custom-call(bf16[4,576,1280]{2,1,0:T(8,128)(2,1)} %w_in, bf16[4,576,1280]{2,1,0:T(8,128)(2,1)} %w_out), custom_call_target="tpu_custom_call" | custom-call | tf_op jit(solution)/shard_map/stage/pallas_call | solution.py:135
  57.7 0.5 collective-permute-start.19
  58.2 1.3 collective-permute-start.20
  59.6 4.3 %expert.2 = (bf16[2,576,256]{2,1,0:T(8,128)(2,1)S(1)}, bf16[2,576,256]{2,1,0:T(8,128)(2,1)S(1)}, bf16[2,64,1280]{2,1,0:T(8,128)(2,1)S(1)}, bf16[2,64,1280]{2,1,0...) custom-call(bf16[2,64,1280]{2,1,0:T(8,128)(2,1)S(1)} %get-tuple-elem, ...), custom_call_target="tpu_custom_call" | custom-call | flops 3019898880 | bytes 12582912 | tf_op jit(solution)/shard_map/expert/pallas_call | solution.py:199
  64.0 1.1 collective-permute-start.8
  65.1 2.7 %collective-permute-start.11 = (bf16[2,64,1280]{2,1,0:T(8,128)(2,1)S(1)}, bf16[2,64,1280]{2,1,0:T(8,128)(2,1)S(1)}, u32[]{:S(2)}, u32[]{:S(2)}) collective-permute-start(bf16[2,64,1280]{2,1,0:T(8,128)(2,1)S(1)} %get-tuple-element.59), channel_id=1, source_target_pairs={{0,1},{1,2},{2,3},{3,0},{8,11},{9,8},{10,9},{11,10},{4,5},{5,6},{6... | collective-permute-start | bytes 983048 | tf_op jit(solution)/shard_map/sum_first_y_up/ppermute | solution.py:37
  67.8 0.3 collective-permute-done.20.refs_7_.refs_17_
  68.2 4.3 %expert.3 = (bf16[2,576,256]{2,1,0:T(8,128)(2,1)S(1)}, bf16[2,576,256]{2,1,0:T(8,128)(2,1)S(1)}, bf16[2,64,1280]{2,1,0:T(8,128)(2,1)S(1)}, bf16[2,64,1280]{2,1,0...) custom-call(bf16[2,64,1280]{2,1,0:T(8,128)(2,1)S(1)} %get-tuple-elem, ...), custom_call_target="tpu_custom_call" | custom-call | flops 3019898880 | bytes 12582912 | tf_op jit(solution)/shard_map/expert/pallas_call | solution.py:199
  72.7 0.5 collective-permute-start.21
  73.1 0.7 collective-permute-start.26
  73.9 2.1 %collective-permute-start.25 = (bf16[2,64,1280]{2,1,0:T(8,128)(2,1)S(1)}, bf16[2,64,1280]{2,1,0:T(8,128)(2,1)S(1)}, u32[]{:S(2)}, u32[]{:S(2)}) collective-permute-start(bf16[2,64,1280]{2,1,0:T(8,128)(2,1)S(1)} %get-tuple-element.74), channel_id=1, source_target_pairs={{0,1},{1,2},{2,3},{3,0},{8,11},{9,8},{10,9},{11,10},{4,5},{5,6},{6... | collective-permute-start | bytes 983048 | tf_op jit(solution)/shard_map/sum_second_y_up/ppermute | solution.py:37
  76.0 1.1 collective-permute-start.9
  77.1 0.5 collective-permute-done.12
  77.8 0.6 collective-permute-start.13
  78.4 0.6 collective-permute-done.21
  79.0 0.8 collective-permute-start.22
  79.8 3.0 %collective-permute-done.26 = bf16[2,64,1280]{2,1,0:T(8,128)(2,1)S(1)} collective-permute-done((bf16[2,64,1280]{2,1,0:T(8,128)(2,1)S(1)}, bf16[2,64,1280]{2,1,0:T(8,128)(2,1)S(1)}, u32[]{:S(2)}, u32[]{:S(2)}) %collective-permute-start.26) | collective-permute-done | bytes 327712 | tf_op jit(solution)/shard_map/sum_second_y_down/ppermute | solution.py:42
  82.8 0.8 collective-permute-done.25
  83.7 1.0 collective-permute-start.27
  84.7 4.9 %collective-permute-done.9 = bf16[2,64,1280]{2,1,0:T(8,128)(2,1)S(1)} collective-permute-done((bf16[2,64,1280]{2,1,0:T(8,128)(2,1)S(1)}, bf16[2,64,1280]{2,1,0:T(8,128)(2,1)S(1)}, u32[]{:S(2)}, u32[]{:S(2)}) %collective-permute-start.9) | collective-permute-done | bytes 327712 | tf_op jit(solution)/shard_map/sum_first_on_up/ppermute | solution.py:37
  89.7 3.4 %collective-permute-start.10 = (bf16[2,64,1280]{2,1,0:T(8,128)(2,1)S(1)}, bf16[2,64,1280]{2,1,0:T(8,128)(2,1)S(1)}, u32[]{:S(2)}, u32[]{:S(2)}) collective-permute-start(bf16[2,64,1280]{2,1,0:T(8,128)(2,1)S(1)} %add_convert_fusion.4), channel_id=1, source_target_pairs={{0,1},{1,2},{2,3},{3,0},{8,11},{9,8},{10,9},{11,10},{4,5},{5,6},{6... | collective-permute-start | bytes 983048 | tf_op jit(solution)/shard_map/sum_first_up/ppermute | solution.py:37
  93.2 1.4 collective-permute-start.24
  94.7 4.0 %collective-permute-done.10.refs_2_ = bf16[2,64,1280]{2,1,0:T(8,128)(2,1)S(1)} collective-permute-done((bf16[2,64,1280]{2,1,0:T(8,128)(2,1)S(1)}, bf16[2,64,1280]{2,1,0:T(8,128)(2,1)S(1)}, u32[]{:S(2)}, u32[]{:S(2)}) %collective-permute-start.10) | collective-permute-done | bytes 327712 | tf_op jit(solution)/shard_map/sum_first_up/ppermute | solution.py:37
  98.7 4.1 %collective-permute-done.23.refs_5_ = bf16[2,64,1280]{2,1,0:T(8,128)(2,1)S(1)} collective-permute-done((bf16[2,64,1280]{2,1,0:T(8,128)(2,1)S(1)}, bf16[2,64,1280]{2,1,0:T(8,128)(2,1)S(1)}, u32[]{:S(2)}, u32[]{:S(2)}) %collective-permute-start.23) | collective-permute-done | bytes 327712 | tf_op jit(solution)/shard_map/sum_second_up/ppermute | solution.py:37
  102.8 0.6 unsort_rows.1
  103.5 21.4 %all_to_all.33 = bf16[16,16,1280]{2,1,0:T(8,128)(2,1)S(1)} all-to-all(bf16[16,16,1280]{2,1,0:T(8,128)(2,1)S(1)} %bitcast.8), channel_id=1, replica_groups=mesh['yh'=2,'x'=4,'c'=2,'yl'=2,'z'=4] {'yh','x','c'}, dimensions={0} | all-to-all | bytes 1310720 | tf_op jit(solution)/shard_map/all_to_all | solution.py:299
  124.9 0.9 logits_back.1
  125.8 18.3 %all_to_all.34.terms = f32[128,1,1280]{2,1,0:T(1,128)S(1)} all-to-all(f32[128,1,1280]{2,1,0:T(1,128)S(1)} %get-tuple-element.79), channel_id=1, replica_groups=mesh['yh'=2,'x'=4,'c'=2,'yl'=2,'z'=4] {'yh','x','c','yl','z'}, dimensions={0} | all-to-all | bytes 1310720 | tf_op jit(solution)/shard_map/all_to_all | solution.py:360
  144.1 1.3 sum_terms.1
  145.4 4.6 %all-to-all-start.3 = ((f32[128,1,1280]{2,1,0:T(1,128)}), f32[128,1,1280]{2,1,0:T(1,128)S(1)}, u32[]{:S(2)}, u32[]{:S(2)}) async-start(f32[128,1,1280]{2,1,0:T(1,128)} %sum_terms.1), calls=%async_computation.3 | async-start | bytes 1310720 | tf_op jit(solution)/shard_map/all_to_all | solution.py:367
  150.0 9.8 %weight_grads.1 = (bf16[4,576,1280]{2,1,0:T(8,128)(2,1)}, bf16[4,576,1280]{2,1,0:T(8,128)(2,1)}) custom-call(bf16[2,64,1280]{2,1,0:T(8,128)(2,1)} %copy-done.4, bf16[2,64,1280]{2,1,0:T(8,128)(2,1)} %copy-done.6, bf16[2,64,1280]{2,1,0:T(8,128)(2,1)} %copy-done.10, bf16[2,64,1280]{2,1,0:T(8,128)(2,1)} %copy-done.7, bf16[2,64,1280]{2,1,0:T(8,128)(2,1)} %copy-done.8, ...), custom_call_target="tpu_custom_call" | custom-call | flops 3019898880 | bytes 20971520 | tf_op jit(solution)/shard_map/weight_grads/pallas_call | solution.py:246
  159.8 1.4 tokens_back.1
  161.1 3.9 %all-to-all-done.3 = f32[128,1,1280]{2,1,0:T(1,128)S(1)} async-done(((f32[128,1,1280]{2,1,0:T(1,128)}), f32[128,1,1280]{2,1,0:T(1,128)S(1)}, u32[]{:S(2)}, u32[]{:S(2)}) %all-to-all-start.3) | async-done | bytes 655392 | tf_op jit(solution)/shard_map/all_to_all | solution.py:367
  165.1 0.9 copy.11
  (80 shorter events, 0.9 us)
Async XLA Ops:
  26.1 33.4 %copy-start.4 = (bf16[2,64,1280]{2,1,0:T(8,128)(2,1)}, bf16[2,64,1280]{2,1,0:T(8,128)(2,1)S(1)}, u32[]{:S(2)}) copy-start(bf16[2,64,1280]{2,1,0:T(8,128)(2,1)S(1)} %get-tuple-element.47.refs_0_) | copy-start | bytes 983044
  26.1 42.1 %copy-start.5 = (bf16[2,64,1280]{2,1,0:T(8,128)(2,1)}, bf16[2,64,1280]{2,1,0:T(8,128)(2,1)S(1)}, u32[]{:S(2)}) copy-start(bf16[2,64,1280]{2,1,0:T(8,128)(2,1)S(1)} %get-tuple-element.64.refs_0_.refs_10_) | copy-start | bytes 983044
  26.1 10.4 %collective-permute-start = (bf16[2,64,1280]{2,1,0:T(8,128)(2,1)S(1)}, bf16[2,64,1280]{2,1,0:T(8,128)(2,1)S(1)}, u32[]{:S(2)}, u32[]{:S(2)}) collective-permute-start(bf16[2,64,1280]{2,1,0:T(8,128)(2,1)S(1)} %get-tuple-element.47.refs_0_), channel_id=1, source_target_pairs={{0,1},{1,2},{2,3},{3,0},{8,11},{9,8},{10,9},{11,10},{4,5},{5,6},{6... | collective-permute-start | bytes 983048 | tf_op jit(solution)/shard_map/first_up/ppermute | solution.py:37
  29.9 10.0 %collective-permute-start.2 = (bf16[2,64,1280]{2,1,0:T(8,128)(2,1)S(1)}, bf16[2,64,1280]{2,1,0:T(8,128)(2,1)S(1)}, u32[]{:S(2)}, u32[]{:S(2)}) collective-permute-start(bf16[2,64,1280]{2,1,0:T(8,128)(2,1)S(1)} %get-tuple-element.47.refs_0_), channel_id=1, source_target_pairs={{0,3},{1,0},{2,1},{3,2},{8,9},{9,10},{10,11},{11,8},{4,7},{5,4},{6... | collective-permute-start | bytes 983048 | tf_op jit(solution)/shard_map/first_down/ppermute | solution.py:42
  29.9 10.0 %collective-permute-start.3 = (bf16[2,64,1280]{2,1,0:T(8,128)(2,1)S(1)}, bf16[2,64,1280]{2,1,0:T(8,128)(2,1)S(1)}, u32[]{:S(2)}, u32[]{:S(2)}) collective-permute-start(bf16[2,64,1280]{2,1,0:T(8,128)(2,1)S(1)} %get-tuple-element.47.refs_0_), channel_id=1, source_target_pairs={{0,4},{4,0},{1,5},{5,1},{2,6},{6,2},{3,7},{7,3},{8,12},{12,8},{9,1... | collective-permute-start | bytes 983048 | tf_op jit(solution)/shard_map/first_across/ppermute | solution.py:47
  30.3 12.2 %collective-permute-start.15 = (bf16[2,64,1280]{2,1,0:T(8,128)(2,1)S(1)}, bf16[2,64,1280]{2,1,0:T(8,128)(2,1)S(1)}, u32[]{:S(2)}, u32[]{:S(2)}) collective-permute-start(bf16[2,64,1280]{2,1,0:T(8,128)(2,1)S(1)} %get-tuple-element.64.refs_0_.refs_10_), channel_id=1, source_target_pairs={{0,3},{1,0},{2,1},{3,2},{8,9},{9,10},{10,11},{11,8},{4,7},{5,4},{6... | collective-permute-start | bytes 983048 | tf_op jit(solution)/shard_map/second_down/ppermute | solution.py:42
  36.5 23.0 %copy-start.6 = (bf16[2,64,1280]{2,1,0:T(8,128)(2,1)}, bf16[2,64,1280]{2,1,0:T(8,128)(2,1)S(1)}, u32[]{:S(2)}) copy-start(bf16[2,64,1280]{2,1,0:T(8,128)(2,1)S(1)} %collective-permute-done.refs_1_) | copy-start | bytes 983044
  36.5 8.0 %collective-permute-start.1 = (bf16[2,64,1280]{2,1,0:T(8,128)(2,1)S(1)}, bf16[2,64,1280]{2,1,0:T(8,128)(2,1)S(1)}, u32[]{:S(2)}, u32[]{:S(2)}) collective-permute-start(bf16[2,64,1280]{2,1,0:T(8,128)(2,1)S(1)} %collective-permute-done.refs_1_), channel_id=1, source_target_pairs={{0,1},{1,2},{2,3},{3,0},{8,11},{9,8},{10,9},{11,10},{4,5},{5,6},{6... | collective-permute-start | bytes 983048 | tf_op jit(solution)/shard_map/first_on_up/ppermute | solution.py:37
  39.9 19.6 %copy-start.7 = (bf16[2,64,1280]{2,1,0:T(8,128)(2,1)}, bf16[2,64,1280]{2,1,0:T(8,128)(2,1)S(1)}, u32[]{:S(2)}) copy-start(bf16[2,64,1280]{2,1,0:T(8,128)(2,1)S(1)} %collective-permute-done.2.refs_3_) | copy-start | bytes 983044
  39.9 19.6 %copy-start.8 = (bf16[2,64,1280]{2,1,0:T(8,128)(2,1)}, bf16[2,64,1280]{2,1,0:T(8,128)(2,1)S(1)}, u32[]{:S(2)}) copy-start(bf16[2,64,1280]{2,1,0:T(8,128)(2,1)S(1)} %collective-permute-done.3.refs_4_) | copy-start | bytes 983044
  39.9 9.8 %collective-permute-start.4 = (bf16[2,64,1280]{2,1,0:T(8,128)(2,1)S(1)}, bf16[2,64,1280]{2,1,0:T(8,128)(2,1)S(1)}, u32[]{:S(2)}, u32[]{:S(2)}) collective-permute-start(bf16[2,64,1280]{2,1,0:T(8,128)(2,1)S(1)} %collective-permute-done.3.refs_4_), channel_id=1, source_target_pairs={{0,1},{1,2},{2,3},{3,0},{8,11},{9,8},{10,9},{11,10},{4,5},{5,6},{6... | collective-permute-start | bytes 983048 | tf_op jit(solution)/shard_map/first_y_up/ppermute | solution.py:37
  42.1 11.0 %collective-permute-start.17 = (bf16[2,64,1280]{2,1,0:T(8,128)(2,1)S(1)}, bf16[2,64,1280]{2,1,0:T(8,128)(2,1)S(1)}, u32[]{:S(2)}, u32[]{:S(2)}) collective-permute-start(bf16[2,64,1280]{2,1,0:T(8,128)(2,1)S(1)} %get-tuple-element.64.refs_0_.refs_10_), channel_id=1, source_target_pairs={{0,4},{4,0},{1,5},{5,1},{2,6},{6,2},{3,7},{7,3},{8,12},{12,8},{9,1... | collective-permute-start | bytes 983048 | tf_op jit(solution)/shard_map/second_across/ppermute | solution.py:47
  42.5 25.6 %copy-start.9 = (bf16[2,64,1280]{2,1,0:T(8,128)(2,1)}, bf16[2,64,1280]{2,1,0:T(8,128)(2,1)S(1)}, u32[]{:S(2)}) copy-start(bf16[2,64,1280]{2,1,0:T(8,128)(2,1)S(1)} %collective-permute-done.15.refs_3_.refs_13_) | copy-start | bytes 983044
  42.5 15.2 %collective-permute-start.16 = (bf16[2,64,1280]{2,1,0:T(8,128)(2,1)S(1)}, bf16[2,64,1280]{2,1,0:T(8,128)(2,1)S(1)}, u32[]{:S(2)}, u32[]{:S(2)}) collective-permute-start(bf16[2,64,1280]{2,1,0:T(8,128)(2,1)S(1)} %collective-permute-done.15.refs_3_.refs_13_), channel_id=1, source_target_pairs={{0,3},{1,0},{2,1},{3,2},{8,9},{9,10},{10,11},{11,8},{4,7},{5,4},{6... | collective-permute-start | bytes 983048 | tf_op jit(solution)/shard_map/second_on_down/ppermute | solution.py:42
  42.5 15.6 %collective-permute-start.6 = (bf16[2,64,1280]{2,1,0:T(8,128)(2,1)S(1)}, bf16[2,64,1280]{2,1,0:T(8,128)(2,1)S(1)}, u32[]{:S(2)}, u32[]{:S(2)}) collective-permute-start(bf16[2,64,1280]{2,1,0:T(8,128)(2,1)S(1)} %collective-permute-done.3.refs_4_), channel_id=1, source_target_pairs={{0,3},{1,0},{2,1},{3,2},{8,9},{9,10},{10,11},{11,8},{4,7},{5,4},{6... | collective-permute-start | bytes 983048 | tf_op jit(solution)/shard_map/first_y_down/ppermute | solution.py:42
  44.5 15.1 %copy-start.10 = (bf16[2,64,1280]{2,1,0:T(8,128)(2,1)}, bf16[2,64,1280]{2,1,0:T(8,128)(2,1)S(1)}, u32[]{:S(2)}) copy-start(bf16[2,64,1280]{2,1,0:T(8,128)(2,1)S(1)} %collective-permute-done.1.refs_2_) | copy-start | bytes 983044
  44.5 15.0 %collective-permute-start.5 = (bf16[2,64,1280]{2,1,0:T(8,128)(2,1)S(1)}, bf16[2,64,1280]{2,1,0:T(8,128)(2,1)S(1)}, u32[]{:S(2)}, u32[]{:S(2)}) collective-permute-start(bf16[2,64,1280]{2,1,0:T(8,128)(2,1)S(1)} %collective-permute-done.1.refs_2_), channel_id=1, source_target_pairs={{0,4},{4,0},{1,5},{5,1},{2,6},{6,2},{3,7},{7,3},{8,12},{12,8},{9,1... | collective-permute-start | bytes 983048 | tf_op jit(solution)/shard_map/first_far_across/ppermute | solution.py:47
  49.7 9.9 %copy-start.11 = (bf16[2,64,1280]{2,1,0:T(8,128)(2,1)}, bf16[2,64,1280]{2,1,0:T(8,128)(2,1)S(1)}, u32[]{:S(2)}) copy-start(bf16[2,64,1280]{2,1,0:T(8,128)(2,1)S(1)} %collective-permute-done.4.refs_5_) | copy-start | bytes 983044
  49.7 15.4 %collective-permute-start.14 = (bf16[2,64,1280]{2,1,0:T(8,128)(2,1)S(1)}, bf16[2,64,1280]{2,1,0:T(8,128)(2,1)S(1)}, u32[]{:S(2)}, u32[]{:S(2)}) collective-permute-start(bf16[2,64,1280]{2,1,0:T(8,128)(2,1)S(1)} %get-tuple-element.64.refs_0_.refs_10_), channel_id=1, source_target_pairs={{0,1},{1,2},{2,3},{3,0},{8,11},{9,8},{10,9},{11,10},{4,5},{5,6},{6... | collective-permute-start | bytes 983048 | tf_op jit(solution)/shard_map/second_up/ppermute | solution.py:37
  53.1 15.0 %copy-start.12 = (bf16[2,64,1280]{2,1,0:T(8,128)(2,1)}, bf16[2,64,1280]{2,1,0:T(8,128)(2,1)S(1)}, u32[]{:S(2)}) copy-start(bf16[2,64,1280]{2,1,0:T(8,128)(2,1)S(1)} %collective-permute-done.17.refs_4_.refs_14_) | copy-start | bytes 983044
  53.1 12.0 %collective-permute-start.18 = (bf16[2,64,1280]{2,1,0:T(8,128)(2,1)S(1)}, bf16[2,64,1280]{2,1,0:T(8,128)(2,1)S(1)}, u32[]{:S(2)}, u32[]{:S(2)}) collective-permute-start(bf16[2,64,1280]{2,1,0:T(8,128)(2,1)S(1)} %collective-permute-done.17.refs_4_.refs_14_), channel_id=1, source_target_pairs={{0,1},{1,2},{2,3},{3,0},{8,11},{9,8},{10,9},{11,10},{4,5},{5,6},{6... | collective-permute-start | bytes 983048 | tf_op jit(solution)/shard_map/second_y_up/ppermute | solution.py:37
  57.7 10.5 %copy-start.13 = (bf16[2,64,1280]{2,1,0:T(8,128)(2,1)}, bf16[2,64,1280]{2,1,0:T(8,128)(2,1)S(1)}, u32[]{:S(2)}) copy-start(bf16[2,64,1280]{2,1,0:T(8,128)(2,1)S(1)} %collective-permute-done.16.refs_2_.refs_12_) | copy-start | bytes 983044
  57.7 10.1 %collective-permute-start.19 = (bf16[2,64,1280]{2,1,0:T(8,128)(2,1)S(1)}, bf16[2,64,1280]{2,1,0:T(8,128)(2,1)S(1)}, u32[]{:S(2)}, u32[]{:S(2)}) collective-permute-start(bf16[2,64,1280]{2,1,0:T(8,128)(2,1)S(1)} %collective-permute-done.16.refs_2_.refs_12_), channel_id=1, source_target_pairs={{0,4},{4,0},{1,5},{5,1},{2,6},{6,2},{3,7},{7,3},{8,12},{12,8},{9,1... | collective-permute-start | bytes 983048 | tf_op jit(solution)/shard_map/second_far_across/ppermute | solution.py:47
  58.2 10.0 %collective-permute-start.20 = (bf16[2,64,1280]{2,1,0:T(8,128)(2,1)S(1)}, bf16[2,64,1280]{2,1,0:T(8,128)(2,1)S(1)}, u32[]{:S(2)}, u32[]{:S(2)}) collective-permute-start(bf16[2,64,1280]{2,1,0:T(8,128)(2,1)S(1)} %collective-permute-done.17.refs_4_.refs_14_), channel_id=1, source_target_pairs={{0,3},{1,0},{2,1},{3,2},{8,9},{9,10},{10,11},{11,8},{4,7},{5,4},{6... | collective-permute-start | bytes 983048 | tf_op jit(solution)/shard_map/second_y_down/ppermute | solution.py:42
  63.9 8.6 %copy-start.21 = (bf16[2,576,256]{2,1,0:T(8,128)(2,1)}, bf16[2,576,256]{2,1,0:T(8,128)(2,1)S(1)}, u32[]{:S(2)}) copy-start(bf16[2,576,256]{2,1,0:T(8,128)(2,1)S(1)} %get-tuple-element.80.refs_8_) | copy-start | bytes 1769476
  64.0 8.6 %copy-start.22 = (bf16[2,576,256]{2,1,0:T(8,128)(2,1)}, bf16[2,576,256]{2,1,0:T(8,128)(2,1)S(1)}, u32[]{:S(2)}) copy-start(bf16[2,576,256]{2,1,0:T(8,128)(2,1)S(1)} %get-tuple-element.81.refs_9_) | copy-start | bytes 1769476
  64.0 9.2 %collective-permute-start.8 = (bf16[2,64,1280]{2,1,0:T(8,128)(2,1)S(1)}, bf16[2,64,1280]{2,1,0:T(8,128)(2,1)S(1)}, u32[]{:S(2)}, u32[]{:S(2)}) collective-permute-start(bf16[2,64,1280]{2,1,0:T(8,128)(2,1)S(1)} %get-tuple-element.57), channel_id=1, source_target_pairs={{0,4},{4,0},{1,5},{5,1},{2,6},{6,2},{3,7},{7,3},{8,12},{12,8},{9,1... | collective-permute-start | bytes 983048 | tf_op jit(solution)/shard_map/sum_first_far_across/ppermute | solution.py:47
  65.1 8.8 %collective-permute-start.7 = (bf16[2,64,1280]{2,1,0:T(8,128)(2,1)S(1)}, bf16[2,64,1280]{2,1,0:T(8,128)(2,1)S(1)}, u32[]{:S(2)}, u32[]{:S(2)}) collective-permute-start(bf16[2,64,1280]{2,1,0:T(8,128)(2,1)S(1)} %get-tuple-element.54), channel_id=1, source_target_pairs={{0,3},{1,0},{2,1},{3,2},{8,9},{9,10},{10,11},{11,8},{4,7},{5,4},{6... | collective-permute-start | bytes 983048 | tf_op jit(solution)/shard_map/sum_first_down/ppermute | solution.py:42
  65.1 10.8 %collective-permute-start.11 = (bf16[2,64,1280]{2,1,0:T(8,128)(2,1)S(1)}, bf16[2,64,1280]{2,1,0:T(8,128)(2,1)S(1)}, u32[]{:S(2)}, u32[]{:S(2)}) collective-permute-start(bf16[2,64,1280]{2,1,0:T(8,128)(2,1)S(1)} %get-tuple-element.59), channel_id=1, source_target_pairs={{0,1},{1,2},{2,3},{3,0},{8,11},{9,8},{10,9},{11,10},{4,5},{5,6},{6... | collective-permute-start | bytes 983048 | tf_op jit(solution)/shard_map/sum_first_y_up/ppermute | solution.py:37
  67.8 9.8 %collective-permute-start.12 = (bf16[2,64,1280]{2,1,0:T(8,128)(2,1)S(1)}, bf16[2,64,1280]{2,1,0:T(8,128)(2,1)S(1)}, u32[]{:S(2)}, u32[]{:S(2)}) collective-permute-start(bf16[2,64,1280]{2,1,0:T(8,128)(2,1)S(1)} %get-tuple-element.60), channel_id=1, source_target_pairs={{0,3},{1,0},{2,1},{3,2},{8,9},{9,10},{10,11},{11,8},{4,7},{5,4},{6... | collective-permute-start | bytes 983048 | tf_op jit(solution)/shard_map/sum_first_y_down/ppermute | solution.py:42
  72.6 53.2 %copy-start.23 = (bf16[2,576,256]{2,1,0:T(8,128)(2,1)}, bf16[2,576,256]{2,1,0:T(8,128)(2,1)S(1)}, u32[]{:S(2)}) copy-start(bf16[2,576,256]{2,1,0:T(8,128)(2,1)S(1)} %get-tuple-element.82.refs_18_) | copy-start | bytes 1769476
  72.6 53.2 %copy-start.24 = (bf16[2,576,256]{2,1,0:T(8,128)(2,1)}, bf16[2,576,256]{2,1,0:T(8,128)(2,1)S(1)}, u32[]{:S(2)}) copy-start(bf16[2,576,256]{2,1,0:T(8,128)(2,1)S(1)} %get-tuple-element.83.refs_19_) | copy-start | bytes 1769476
  72.6 52.3 %copy-start = (bf16[1,256,1280]{2,1,0:T(8,128)(2,1)S(1)}, bf16[1,256,1280]{2,1,0:T(8,128)(2,1)}, u32[]{:S(2)}) copy-start(bf16[1,256,1280]{2,1,0:T(8,128)(2,1)} %tokens.3) | copy-start | bytes 1966084
  72.6 52.3 %copy-start.1 = (bf16[1,256,1280]{2,1,0:T(8,128)(2,1)S(1)}, bf16[1,256,1280]{2,1,0:T(8,128)(2,1)}, u32[]{:S(2)}) copy-start(bf16[1,256,1280]{2,1,0:T(8,128)(2,1)} %grad_out.3) | copy-start | bytes 1966084
  72.6 52.2 %copy-start.3 = (f32[128,256]{1,0:T(8,128)S(1)}, f32[128,256]{1,0:T(8,128)}, u32[]{:S(2)}) copy-start(f32[128,256]{1,0:T(8,128)} %get-tuple-element.45.p_dispatch) | copy-start | bytes 393220
  72.6 52.2 %copy-start.20 = (f32[128,256]{1,0:T(8,128)S(1)}, f32[128,256]{1,0:T(8,128)}, u32[]{:S(2)}) copy-start(f32[128,256]{1,0:T(8,128)} %get-tuple-element.76.p_combine) | copy-start | bytes 393220
  72.7 6.3 %collective-permute-start.21 = (bf16[2,64,1280]{2,1,0:T(8,128)(2,1)S(1)}, bf16[2,64,1280]{2,1,0:T(8,128)(2,1)S(1)}, u32[]{:S(2)}, u32[]{:S(2)}) collective-permute-start(bf16[2,64,1280]{2,1,0:T(8,128)(2,1)S(1)} %get-tuple-element.70), channel_id=1, source_target_pairs={{0,4},{4,0},{1,5},{5,1},{2,6},{6,2},{3,7},{7,3},{8,12},{12,8},{9,1... | collective-permute-start | bytes 983048 | tf_op jit(solution)/shard_map/sum_second_far_across/ppermute | solution.py:47
  73.1 9.7 %collective-permute-start.26 = (bf16[2,64,1280]{2,1,0:T(8,128)(2,1)S(1)}, bf16[2,64,1280]{2,1,0:T(8,128)(2,1)S(1)}, u32[]{:S(2)}, u32[]{:S(2)}) collective-permute-start(bf16[2,64,1280]{2,1,0:T(8,128)(2,1)S(1)} %get-tuple-element.75), channel_id=1, source_target_pairs={{0,3},{1,0},{2,1},{3,2},{8,9},{9,10},{10,11},{11,8},{4,7},{5,4},{6... | collective-permute-start | bytes 983048 | tf_op jit(solution)/shard_map/sum_second_y_down/ppermute | solution.py:42
  73.9 9.7 %collective-permute-start.25 = (bf16[2,64,1280]{2,1,0:T(8,128)(2,1)S(1)}, bf16[2,64,1280]{2,1,0:T(8,128)(2,1)S(1)}, u32[]{:S(2)}, u32[]{:S(2)}) collective-permute-start(bf16[2,64,1280]{2,1,0:T(8,128)(2,1)S(1)} %get-tuple-element.74), channel_id=1, source_target_pairs={{0,1},{1,2},{2,3},{3,0},{8,11},{9,8},{10,9},{11,10},{4,5},{5,6},{6... | collective-permute-start | bytes 983048 | tf_op jit(solution)/shard_map/sum_second_y_up/ppermute | solution.py:37
  76.0 13.6 %collective-permute-start.9 = (bf16[2,64,1280]{2,1,0:T(8,128)(2,1)S(1)}, bf16[2,64,1280]{2,1,0:T(8,128)(2,1)S(1)}, u32[]{:S(2)}, u32[]{:S(2)}) collective-permute-start(bf16[2,64,1280]{2,1,0:T(8,128)(2,1)S(1)} %add_convert_fusion.5), channel_id=1, source_target_pairs={{0,1},{1,2},{2,3},{3,0},{8,11},{9,8},{10,9},{11,10},{4,5},{5,6},{6... | collective-permute-start | bytes 983048 | tf_op jit(solution)/shard_map/sum_first_on_up/ppermute | solution.py:37
  77.8 16.9 %collective-permute-start.13 = (bf16[2,64,1280]{2,1,0:T(8,128)(2,1)S(1)}, bf16[2,64,1280]{2,1,0:T(8,128)(2,1)S(1)}, u32[]{:S(2)}, u32[]{:S(2)}) collective-permute-start(bf16[2,64,1280]{2,1,0:T(8,128)(2,1)S(1)} %add_convert_fusion.3), channel_id=1, source_target_pairs={{0,4},{4,0},{1,5},{5,1},{2,6},{6,2},{3,7},{7,3},{8,12},{12,8},{9,1... | collective-permute-start | bytes 983048 | tf_op jit(solution)/shard_map/sum_first_across/ppermute | solution.py:47
  79.0 14.0 %collective-permute-start.22 = (bf16[2,64,1280]{2,1,0:T(8,128)(2,1)S(1)}, bf16[2,64,1280]{2,1,0:T(8,128)(2,1)S(1)}, u32[]{:S(2)}, u32[]{:S(2)}) collective-permute-start(bf16[2,64,1280]{2,1,0:T(8,128)(2,1)S(1)} %add_convert_fusion.2), channel_id=1, source_target_pairs={{0,3},{1,0},{2,1},{3,2},{8,9},{9,10},{10,11},{11,8},{4,7},{5,4},{6... | collective-permute-start | bytes 983048 | tf_op jit(solution)/shard_map/sum_second_on_down/ppermute | solution.py:42
  83.7 11.0 %collective-permute-start.27 = (bf16[2,64,1280]{2,1,0:T(8,128)(2,1)S(1)}, bf16[2,64,1280]{2,1,0:T(8,128)(2,1)S(1)}, u32[]{:S(2)}, u32[]{:S(2)}) collective-permute-start(bf16[2,64,1280]{2,1,0:T(8,128)(2,1)S(1)} %add_convert_fusion), channel_id=1, source_target_pairs={{0,4},{4,0},{1,5},{5,1},{2,6},{6,2},{3,7},{7,3},{8,12},{12,8},{9,1... | collective-permute-start | bytes 983048 | tf_op jit(solution)/shard_map/sum_second_across/ppermute | solution.py:47
  89.7 9.0 %collective-permute-start.10 = (bf16[2,64,1280]{2,1,0:T(8,128)(2,1)S(1)}, bf16[2,64,1280]{2,1,0:T(8,128)(2,1)S(1)}, u32[]{:S(2)}, u32[]{:S(2)}) collective-permute-start(bf16[2,64,1280]{2,1,0:T(8,128)(2,1)S(1)} %add_convert_fusion.4), channel_id=1, source_target_pairs={{0,1},{1,2},{2,3},{3,0},{8,11},{9,8},{10,9},{11,10},{4,5},{5,6},{6... | collective-permute-start | bytes 983048 | tf_op jit(solution)/shard_map/sum_first_up/ppermute | solution.py:37
  93.0 9.8 %collective-permute-start.23 = (bf16[2,64,1280]{2,1,0:T(8,128)(2,1)S(1)}, bf16[2,64,1280]{2,1,0:T(8,128)(2,1)S(1)}, u32[]{:S(2)}, u32[]{:S(2)}) collective-permute-start(bf16[2,64,1280]{2,1,0:T(8,128)(2,1)S(1)} %get-tuple-element.71), channel_id=1, source_target_pairs={{0,1},{1,2},{2,3},{3,0},{8,11},{9,8},{10,9},{11,10},{4,5},{5,6},{6... | collective-permute-start | bytes 983048 | tf_op jit(solution)/shard_map/sum_second_up/ppermute | solution.py:37
  93.2 9.6 %collective-permute-start.24 = (bf16[2,64,1280]{2,1,0:T(8,128)(2,1)S(1)}, bf16[2,64,1280]{2,1,0:T(8,128)(2,1)S(1)}, u32[]{:S(2)}, u32[]{:S(2)}) collective-permute-start(bf16[2,64,1280]{2,1,0:T(8,128)(2,1)S(1)} %add_convert_fusion.1), channel_id=1, source_target_pairs={{0,3},{1,0},{2,1},{3,2},{8,9},{9,10},{10,11},{11,8},{4,7},{5,4},{6... | collective-permute-start | bytes 983048 | tf_op jit(solution)/shard_map/sum_second_down/ppermute | solution.py:42
  145.4 19.7 %all-to-all-start.3 = ((f32[128,1,1280]{2,1,0:T(1,128)}), f32[128,1,1280]{2,1,0:T(1,128)S(1)}, u32[]{:S(2)}, u32[]{:S(2)}) async-start(f32[128,1,1280]{2,1,0:T(1,128)} %sum_terms.1), calls=%async_computation.3 | async-start | bytes 1310720 | tf_op jit(solution)/shard_map/all_to_all | solution.py:367
  150.0 9.8 %copy-start.2 = (bf16[128,1280]{1,0:T(8,128)(2,1)S(1)}, bf16[128,1280]{1,0:T(8,128)(2,1)}, u32[]{:S(2)}) copy-start(bf16[128,1280]{1,0:T(8,128)(2,1)} %slot_params.3) | copy-start | bytes 983044
  (6 other events, 34.2 us)
